TPU v7x, 32 devices: a whole 2x2x4 slice. The times are simulated.
32 devices in a mesh: ctx: 4 (over y, core), fsdp: 4 (over z), tp: 2 (over x).
Axes of the slice: x: 2, y: 2, z: 4, core: 2. Of those that a mesh axis runs over, the one named last changes fastest.
Arguments:
- hidden_in: bfloat16 [4, 1024, 2048], P('fsdp', 'ctx'), may hold values from -6 to 6
- teacher: bfloat16 [4, 1024, 2048], P('fsdp', ('ctx', 'tp')), may hold values from -6 to 6
- lengths: int32 [4], replicated, may hold values from 256 to 1024, as said below
- routes: int32 [4, 1024, 8], P('fsdp', ('ctx', 'tp')), may hold values from 0 to 31, all different within a row; in each aligned block of 128 rows (0 to 127, 128 to 255, ..., all dimensions but the last counted through in order) at most 48 rows name the same one
- attn_gain: float32 [2048], replicated, may hold values from 0.25 to 1.75
- w_query: bfloat16 [2048, 4096], P('fsdp', 'tp'), may hold values from -0.125 to 0.125
- w_key: bfloat16 [2048, 512], P('fsdp', 'tp'), may hold values from -0.125 to 0.125
- w_value: bfloat16 [2048, 512], P('fsdp', 'tp'), may hold values from -0.125 to 0.125
- w_output: bfloat16 [4096, 2048], P('tp', 'fsdp'), may hold values from -1.5 to 1.5
- query_gain: float32 [128], replicated, may hold values from 0.25 to 1.75
- key_gain: float32 [128], replicated, may hold values from 0.25 to 1.75
- ffn_gain: float32 [2048], replicated, may hold values from 0.25 to 1.75
- w_router: bfloat16 [2048, 32], P('fsdp'), may hold values from -0.0625 to 0.0625
- w_expert_in: bfloat16 [32, 2048, 1536], P(('ctx', 'fsdp', 'tp')), may hold values from -0.125 to 0.125
- w_expert_out: bfloat16 [32, 768, 2048], P(('ctx', 'fsdp', 'tp')), may hold values from -1.25 to 1.25
Outputs:
- output: bfloat16 [4, 1024, 2048], P('fsdp', ('ctx', 'tp'))
- loss_value: float32 [], replicated
- grad_input: float32 [4, 1024, 2048], P('fsdp', ('ctx', 'tp'))
- grad_attn_gain: float32 [2048], replicated
- grad_query: float32 [2048, 4096], P('fsdp', 'tp')
- grad_key: float32 [2048, 512], P('fsdp', 'tp')
- grad_value: float32 [2048, 512], P('fsdp', 'tp')
- grad_w_output: float32 [4096, 2048], P('tp', 'fsdp')
- grad_query_gain: float32 [128], replicated
- grad_key_gain: float32 [128], replicated
- grad_ffn_gain: float32 [2048], replicated
- grad_router: float32 [2048, 32], P('fsdp')
- grad_expert_in: float32 [32, 2048, 1536], P(('ctx', 'fsdp', 'tp'))
- grad_expert_out: float32 [32, 768, 2048], P(('ctx', 'fsdp', 'tp'))
Inputs may be any that keep to these rules, and one draw needn't show every extreme that they name: `lengths`: one sequence, which one drawn from the seed, has all 1024 slots valid; valid slots are the first ones of a sequence. `routes`: A row names 8 different experts. In every aligned block of 128 rows (flattened in order), no expert is named by more than 48 rows; in some blocks one expert is named by exactly 48.
All inputs are finite; a program needn't handle non-finite values.
Results may differ from a plain program's by a relative error of at most 0.012.
The roundings to bfloat16 on the way count: a program that leaves them out, or rounds other values in their place, can miss the bound.
Values may be sent and summed in bfloat16 or wider, within the bound.
A program may use at most 256 MiB of HBM per device.

v0:
```python
import jax
import jax.numpy as jnp
from jax import lax
from jax.sharding import PartitionSpec as P

EPS = 1e-06
ROPE_BASE = 1000000.0
MASKED = -1e30


def norm_rows(values, gain_vec):
    factor = lax.rsqrt(jnp.mean(values * values, axis=-1, keepdims=True) + EPS)
    return (values * factor * gain_vec, factor)


def norm_back(values, factor, gain_vec, upstream):
    weighted = upstream * gain_vec
    inner_mean = jnp.mean(values * weighted, axis=-1, keepdims=True)
    return (
        factor * weighted - values * (factor * factor * factor) * inner_mean,
        upstream * values * factor,
    )


def rope_tables(positions, head_size):
    half_size = head_size // 2
    frequency = jnp.power(ROPE_BASE, -jnp.arange(half_size, dtype=jnp.float32) * (2.0 / head_size))
    angles = positions.astype(jnp.float32)[:, None] * frequency[None, :]
    return (jnp.cos(angles), jnp.sin(angles))


def rotate(values, cosine, sine_tab):
    half_size = values.shape[-1] // 2
    front_half = values[..., :half_size]
    back_half = values[..., half_size:]
    cos_rows = cosine[:, None, :]
    sin_rows = sine_tab[:, None, :]
    return jnp.concatenate(
        [
            front_half * cos_rows - back_half * sin_rows,
            back_half * cos_rows + front_half * sin_rows,
        ],
        axis=-1,
    )


def inner_rows(left, right):
    return lax.dot_general(
        left, right, (((0,), (0,)), ((), ())), preferred_element_type=jnp.float32
    )


def outer_cols(left, right):
    return lax.dot_general(
        left, right, (((1,), (1,)), ((), ())), preferred_element_type=jnp.float32
    )


def block_scores(queries, key_rows, offset, positions, length, inv_root):
    block_len = key_rows.shape[1]
    raw_scores = (
        jnp.einsum("kgqd,kjd->kgqj", queries, key_rows, preferred_element_type=jnp.float32)
        * inv_root
    )
    key_pos = offset + jnp.arange(block_len, dtype=jnp.int32)
    allowed = (key_pos[None, :] <= positions[:, None]) & (key_pos[None, :] < length)
    return (jnp.where(allowed, raw_scores, MASKED), allowed)


def local(
    hidden_in,
    teacher,
    lengths,
    routes,
    attn_gain,
    w_query,
    w_key,
    w_value,
    w_output,
    query_gain,
    key_gain,
    ffn_gain,
    w_router,
    w_expert_in,
    w_expert_out,
):
    ctx_index = lax.axis_index("ctx")
    seq_index = lax.axis_index("fsdp")
    head_index = lax.axis_index("tp")
    ctx_count = lax.axis_size("ctx")
    tp_count = lax.axis_size("tp")
    row_count = hidden_in.shape[1]
    width = hidden_in.shape[2]
    half_rows = row_count // tp_count
    head_size = query_gain.shape[0]
    inv_root = head_size ** (-0.5)
    bf_type = jnp.bfloat16
    fl_type = jnp.float32
    full_q, full_k, full_v, full_o, full_router = (
        lax.all_gather(w_query, "fsdp", axis=0, tiled=True),
        lax.all_gather(w_key, "fsdp", axis=0, tiled=True),
        lax.all_gather(w_value, "fsdp", axis=0, tiled=True),
        lax.all_gather(w_output, "fsdp", axis=1, tiled=True),
        lax.all_gather(w_router, "fsdp", axis=0, tiled=True),
    )
    q_heads = full_q.shape[1] // head_size
    kv_heads = full_k.shape[1] // head_size
    group_size = q_heads // kv_heads
    inputs = hidden_in[0].astype(fl_type)
    normed, norm_factor = norm_rows(inputs, attn_gain)
    normed_low = normed.astype(bf_type)
    q_raw = jnp.dot(normed_low, full_q, preferred_element_type=fl_type).reshape(
        row_count, q_heads, head_size
    )
    k_raw = jnp.dot(normed_low, full_k, preferred_element_type=fl_type).reshape(
        row_count, kv_heads, head_size
    )
    values_low = (
        jnp.dot(normed_low, full_v, preferred_element_type=fl_type)
        .astype(bf_type)
        .reshape(row_count, kv_heads, head_size)
    )
    q_normed, q_factor = norm_rows(q_raw, query_gain)
    k_normed, k_factor = norm_rows(k_raw, key_gain)
    positions = ctx_index * row_count + jnp.arange(row_count, dtype=jnp.int32)
    cosine, sine_tab = rope_tables(positions, head_size)
    q_rot = rotate(q_normed, cosine, sine_tab).astype(bf_type)
    k_rot = rotate(k_normed, cosine, sine_tab).astype(bf_type)
    queries = jnp.transpose(q_rot.reshape(row_count, kv_heads, group_size, head_size), (1, 2, 0, 3))
    all_keys, all_values = (
        lax.all_gather(jnp.transpose(k_rot, (1, 0, 2)), "ctx", axis=1, tiled=True),
        lax.all_gather(jnp.transpose(values_low, (1, 0, 2)), "ctx", axis=1, tiled=True),
    )
    total_len = all_keys.shape[1]
    block_len = min(1024, total_len)
    offsets = jnp.arange(total_len // block_len, dtype=jnp.int32) * block_len
    length = jnp.take(lengths, seq_index)
    stat_shape = (kv_heads, group_size, row_count)

    def lse_step(carry, offset):
        running_max, running_sum = carry
        key_rows = lax.dynamic_slice_in_dim(all_keys, offset, block_len, 1)
        scores, allowed = block_scores(queries, key_rows, offset, positions, length, inv_root)
        new_max = jnp.maximum(running_max, jnp.max(scores, axis=-1))
        exponent = jnp.where(allowed, jnp.exp(scores - new_max[..., None]), 0.0)
        return (
            (new_max, running_sum * jnp.exp(running_max - new_max) + jnp.sum(exponent, axis=-1)),
            None,
        )

    (row_max, row_sum), _ = lax.scan(
        lse_step, (jnp.full(stat_shape, MASKED, fl_type), jnp.zeros(stat_shape, fl_type)), offsets
    )
    log_total = row_max + jnp.log(row_sum)

    def probs_of(offset):
        key_rows = lax.dynamic_slice_in_dim(all_keys, offset, block_len, 1)
        value_rows = lax.dynamic_slice_in_dim(all_values, offset, block_len, 1)
        scores, allowed = block_scores(queries, key_rows, offset, positions, length, inv_root)
        return (
            jnp.where(allowed, jnp.exp(scores - log_total[..., None]), 0.0),
            key_rows,
            value_rows,
        )

    def out_step(running, offset):
        probabilities, key_rows, value_rows = probs_of(offset)
        return (
            running
            + jnp.einsum(
                "kgqj,kjd->kgqd",
                probabilities.astype(bf_type),
                value_rows,
                preferred_element_type=fl_type,
            ),
            None,
        )

    attn_acc, _ = lax.scan(
        out_step, jnp.zeros((kv_heads, group_size, row_count, head_size), fl_type), offsets
    )
    heads_low = (
        jnp.transpose(attn_acc, (2, 0, 1, 3))
        .reshape(row_count, q_heads * head_size)
        .astype(bf_type)
    )
    attn_rows = lax.psum_scatter(
        jnp.dot(heads_low, full_o, preferred_element_type=fl_type),
        "tp",
        scatter_dimension=0,
        tiled=True,
    )
    row_start = head_index * half_rows
    own_inputs = lax.dynamic_slice_in_dim(inputs, row_start, half_rows, 0)
    own_factor = lax.dynamic_slice_in_dim(norm_factor, row_start, half_rows, 0)
    own_positions = lax.dynamic_slice_in_dim(positions, row_start, half_rows, 0)
    residual = own_inputs + attn_rows
    ffn_in, ffn_factor = norm_rows(residual, ffn_gain)
    ffn_low = ffn_in.astype(bf_type)
    logits = jnp.dot(ffn_low, full_router, preferred_element_type=fl_type)
    route_ids = routes[0]
    top_count = route_ids.shape[1]
    chosen = jnp.take_along_axis(logits, route_ids, axis=1)
    shifted = jnp.exp(chosen - jnp.max(chosen, axis=-1, keepdims=True))
    gates = shifted / jnp.sum(shifted, axis=-1, keepdims=True)
    expert_count = full_router.shape[1]
    capacity = max(2, half_rows * top_count * 3 // (2 * expert_count))
    flat_routes = route_ids.reshape(-1)
    assign_count = flat_routes.shape[0]
    expert_ids = jnp.arange(expert_count, dtype=jnp.int32)
    onehot = (flat_routes[:, None] == expert_ids[None, :]).astype(jnp.int32)
    earlier = jnp.cumsum(onehot, axis=0) - onehot
    slot_rank = jnp.sum(earlier * onehot, axis=1)
    slot_place = flat_routes * capacity + slot_rank
    slot_owner = (
        jnp.full((expert_count * capacity,), assign_count, jnp.int32)
        .at[slot_place]
        .set(jnp.arange(assign_count, dtype=jnp.int32))
    )
    zero_row = jnp.zeros((1, width), bf_type)
    padded_rows = jnp.concatenate([ffn_low, zero_row], axis=0)
    send_rows = padded_rows[slot_owner // top_count].reshape(expert_count, capacity, width)
    received = lax.all_to_all(
        send_rows, ("ctx", "fsdp", "tp"), split_axis=0, concat_axis=0, tiled=True
    )
    expert_rows = received.reshape(-1, width)
    both_pre = jnp.dot(expert_rows, w_expert_in[0], preferred_element_type=fl_type)
    ff_width = w_expert_out.shape[1]
    gate_pre = both_pre[:, :ff_width]
    up_pre = both_pre[:, ff_width:]
    sigmoid_gate = jax.nn.sigmoid(gate_pre)
    silu_gate = gate_pre * sigmoid_gate
    mixed_low = (silu_gate * up_pre).astype(bf_type)
    expert_out = (
        jnp.dot(mixed_low, w_expert_out[0], preferred_element_type=fl_type)
        .astype(bf_type)
        .reshape(expert_count, capacity, width)
    )
    returned = lax.all_to_all(
        expert_out, ("ctx", "fsdp", "tp"), split_axis=0, concat_axis=0, tiled=True
    )
    picked = (
        returned.reshape(expert_count * capacity, width)[slot_place]
        .reshape(half_rows, top_count, width)
        .astype(fl_type)
    )
    output_f = residual + jnp.sum(gates[..., None] * picked, axis=1)
    count = jnp.sum(lengths).astype(fl_type)
    tokens_total = lengths.shape[0] * row_count * ctx_count
    valid = own_positions < length
    error = jnp.where(valid[:, None], output_f - teacher[0].astype(fl_type), 0.0)
    loss_part = jnp.sum(error * error)
    grad_out = error * (tokens_total / count)
    grad_gate = jnp.einsum("rd,rkd->rk", grad_out, picked)
    grad_chosen = gates * (grad_gate - jnp.sum(gates * grad_gate, axis=-1, keepdims=True))
    route_hot = (route_ids[..., None] == expert_ids[None, None, :]).astype(fl_type)
    grad_logits = jnp.einsum("rk,rke->re", grad_chosen, route_hot).astype(bf_type)
    grad_y = (gates[..., None] * grad_out[:, None, :]).reshape(assign_count, width).astype(bf_type)
    send_grads = jnp.concatenate([grad_y, zero_row], axis=0)[slot_owner].reshape(
        expert_count, capacity, width
    )
    grad_recv = lax.all_to_all(
        send_grads, ("ctx", "fsdp", "tp"), split_axis=0, concat_axis=0, tiled=True
    ).reshape(-1, width)
    grad_mixed = outer_cols(grad_recv, w_expert_out[0])
    grad_expert_out = inner_rows(mixed_low, grad_recv)
    grad_gate_pre = grad_mixed * up_pre * (sigmoid_gate * (1.0 + gate_pre * (1.0 - sigmoid_gate)))
    grad_up_pre = grad_mixed * silu_gate
    grad_pre = jnp.concatenate([grad_gate_pre, grad_up_pre], axis=1).astype(bf_type)
    grad_expert_in = inner_rows(expert_rows, grad_pre)
    grad_rows = (
        outer_cols(grad_pre, w_expert_in[0]).astype(bf_type).reshape(expert_count, capacity, width)
    )
    grad_home = lax.all_to_all(
        grad_rows, ("ctx", "fsdp", "tp"), split_axis=0, concat_axis=0, tiled=True
    )
    grad_picked = (
        grad_home.reshape(expert_count * capacity, width)[slot_place]
        .reshape(half_rows, top_count, width)
        .astype(fl_type)
    )
    grad_ffn = jnp.sum(grad_picked, axis=1) + outer_cols(grad_logits, full_router)
    router_part = inner_rows(ffn_low, grad_logits)
    grad_resid_norm, ffn_gain_terms = norm_back(residual, ffn_factor, ffn_gain, grad_ffn)
    grad_residual = grad_out + grad_resid_norm
    grad_attn = lax.all_gather(grad_residual.astype(bf_type), "tp", axis=0, tiled=True)
    grad_w_output = inner_rows(heads_low, grad_attn)
    grad_heads = jnp.transpose(
        outer_cols(grad_attn, full_o)
        .astype(bf_type)
        .reshape(row_count, kv_heads, group_size, head_size),
        (1, 2, 0, 3),
    )

    def delta_step(running, offset):
        probabilities, key_rows, value_rows = probs_of(offset)
        grad_weights = jnp.einsum(
            "kgqd,kjd->kgqj", grad_heads, value_rows, preferred_element_type=fl_type
        )
        return (running + jnp.sum(probabilities * grad_weights, axis=-1), None)

    delta, _ = lax.scan(delta_step, jnp.zeros(stat_shape, fl_type), offsets)

    def grad_step(running, offset):
        probabilities, key_rows, value_rows = probs_of(offset)
        grad_weights = jnp.einsum(
            "kgqd,kjd->kgqj", grad_heads, value_rows, preferred_element_type=fl_type
        )
        grad_scores = (probabilities * (grad_weights - delta[..., None])).astype(bf_type)
        running = (
            running
            + jnp.einsum("kgqj,kjd->kgqd", grad_scores, key_rows, preferred_element_type=fl_type)
            * inv_root
        )
        key_part = (
            jnp.einsum("kgqj,kgqd->kjd", grad_scores, queries, preferred_element_type=fl_type)
            * inv_root
        )
        value_part = jnp.einsum(
            "kgqj,kgqd->kjd",
            probabilities.astype(bf_type),
            grad_heads,
            preferred_element_type=fl_type,
        )
        return (running, (key_part, value_part))

    grad_qrot, (key_blocks, value_blocks) = lax.scan(
        grad_step, jnp.zeros((kv_heads, group_size, row_count, head_size), fl_type), offsets
    )
    key_grads_all = jnp.transpose(key_blocks, (1, 0, 2, 3)).reshape(kv_heads, total_len, head_size)
    value_grads_all = jnp.transpose(value_blocks, (1, 0, 2, 3)).reshape(
        kv_heads, total_len, head_size
    )
    grad_krot, grad_values = (
        lax.psum_scatter(key_grads_all, "ctx", scatter_dimension=1, tiled=True),
        lax.psum_scatter(value_grads_all, "ctx", scatter_dimension=1, tiled=True),
    )
    grad_krot = jnp.transpose(grad_krot, (1, 0, 2))
    grad_values_low = jnp.transpose(grad_values, (1, 0, 2)).astype(bf_type).reshape(row_count, -1)
    grad_qrot = jnp.transpose(grad_qrot, (2, 0, 1, 3)).reshape(row_count, q_heads, head_size)
    grad_qraw, query_gain_terms = norm_back(
        q_raw, q_factor, query_gain, rotate(grad_qrot, cosine, -sine_tab)
    )
    grad_kraw, key_gain_terms = norm_back(
        k_raw, k_factor, key_gain, rotate(grad_krot, cosine, -sine_tab)
    )
    grad_qraw_low = grad_qraw.astype(bf_type).reshape(row_count, -1)
    grad_kraw_low = grad_kraw.astype(bf_type).reshape(row_count, -1)
    grad_query_full = inner_rows(normed_low, grad_qraw_low)
    grad_key_full = inner_rows(normed_low, grad_kraw_low)
    grad_value_full = inner_rows(normed_low, grad_values_low)
    grad_normed = lax.psum_scatter(
        (
            outer_cols(grad_qraw_low, full_q)
            + outer_cols(grad_kraw_low, full_k)
            + outer_cols(grad_values_low, full_v)
        ).astype(jnp.bfloat16),
        "tp",
        scatter_dimension=0,
        tiled=True,
    ).astype(jnp.float32)
    grad_input_norm, attn_gain_terms = norm_back(own_inputs, own_factor, attn_gain, grad_normed)
    grad_input = grad_residual + grad_input_norm
    sum_attn_gain, sum_ffn_gain, sum_query_gain, sum_key_gain, router_total, loss_total = lax.psum(
        (
            jnp.sum(attn_gain_terms, axis=0),
            jnp.sum(ffn_gain_terms, axis=0),
            jnp.sum(query_gain_terms, axis=(0, 1)),
            jnp.sum(key_gain_terms, axis=(0, 1)),
            router_part,
            loss_part,
        ),
        ("ctx", "fsdp", "tp"),
    )
    shard_rows = w_query.shape[0]
    grad_router = lax.dynamic_slice_in_dim(router_total, seq_index * shard_rows, shard_rows, 0)
    total_query, total_key, total_value, total_output = lax.psum(
        (grad_query_full, grad_key_full, grad_value_full, grad_w_output), ("ctx", "fsdp")
    )
    grad_query = lax.dynamic_slice_in_dim(total_query, seq_index * shard_rows, shard_rows, 0)
    grad_key = lax.dynamic_slice_in_dim(total_key, seq_index * shard_rows, shard_rows, 0)
    grad_value = lax.dynamic_slice_in_dim(total_value, seq_index * shard_rows, shard_rows, 0)
    grad_output_w = lax.dynamic_slice_in_dim(total_output, seq_index * shard_rows, shard_rows, 1)
    loss_value = loss_total / (count * width)
    return (
        output_f.astype(bf_type)[None],
        loss_value,
        grad_input[None],
        sum_attn_gain,
        grad_query,
        grad_key,
        grad_value,
        grad_output_w,
        sum_query_gain,
        sum_key_gain,
        sum_ffn_gain,
        grad_router,
        grad_expert_in[None],
        grad_expert_out[None],
    )


def solution(mesh):
    return jax.shard_map(
        local,
        mesh=mesh,
        in_specs=(
            P("fsdp", "ctx", None),
            P("fsdp", ("ctx", "tp"), None),
            P(),
            P("fsdp", ("ctx", "tp"), None),
            P(),
            P("fsdp", "tp"),
            P("fsdp", "tp"),
            P("fsdp", "tp"),
            P("tp", "fsdp"),
            P(),
            P(),
            P(),
            P("fsdp", None),
            P(("ctx", "fsdp", "tp"), None, None),
            P(("ctx", "fsdp", "tp"), None, None),
        ),
        out_specs=(
            P("fsdp", ("ctx", "tp"), None),
            P(),
            P("fsdp", ("ctx", "tp"), None),
            P(),
            P("fsdp", "tp"),
            P("fsdp", "tp"),
            P("fsdp", "tp"),
            P("tp", "fsdp"),
            P(),
            P(),
            P(),
            P("fsdp", None),
            P(("ctx", "fsdp", "tp"), None, None),
            P(("ctx", "fsdp", "tp"), None, None),
        ),
        check_vma=False,
    )
```

profile of v0, /device:TPU:25, one launch (start us, length us, event | category | flops | bytes accessed | tf_op | source)
XLA Modules:
  0.0 2053.3 jit_solution(8380437582337504100)
XLA Ops:
  14.1 22.9 %all-gather.8.cloned.1.call-done = bf16[2048,256]{1,0:T(8,128)(2,1)} async-done(((bf16[512,256]{1,0:T(8,128)(2,1)}), bf16[2048,256]{1,0:T(8,128)(2,1)}) %all-gather.8.cloned.1.call-update) | async-done | bytes 1048592 | tf_op jit(solution)/shard_map/all_gather | solution.py:101
  43.4 22.7 %all-gather.10.cloned.1.call-done = bf16[2048,256]{1,0:T(8,128)(2,1)} async-done(((bf16[512,256]{1,0:T(8,128)(2,1)}), bf16[2048,256]{1,0:T(8,128)(2,1)}) %all-gather.10.cloned.1.call-update) | async-done | bytes 1048592 | tf_op jit(solution)/shard_map/all_gather | solution.py:102
  85.5 130.0 %all-gather.6.cloned.1.call-done = bf16[2048,2048]{1,0:T(8,128)(2,1)} async-done(((bf16[512,2048]{1,0:T(8,128)(2,1)}), bf16[2048,2048]{1,0:T(8,128)(2,1)}) %all-gather.6.cloned.1.call-update) | async-done | bytes 8388624 | tf_op jit(solution)/shard_map/all_gather | solution.py:100
  215.5 12.5 copy.41
  260.3 104.5 %all-gather.12.cloned.1.call-done = bf16[2048,2048]{1,0:T(8,128)(2,1)} async-done(((bf16[2048,512]{1,0:T(8,128)(2,1)}), bf16[2048,2048]{1,0:T(8,128)(2,1)}) %all-gather.12.cloned.1.call-update) | async-done | bytes 8388624 | tf_op jit(solution)/shard_map/all_gather | solution.py:103
  389.9 15.5 reduce-scatter.5.cloned.1.call-done
  409.9 13.8 gather_fusion
  423.8 142.4 %all_to_all.20 = bf16[32,48,2048]{2,1,0:T(8,128)(2,1)S(1)} all-to-all(bf16[32,48,2048]{2,1,0:T(8,128)(2,1)} %bitcast.227), channel_id=1, replica_groups=mesh['ctx'=4,'fsdp'=4,'tp'=2] {'ctx','fsdp','tp'}, dimensions={0} | all-to-all | bytes 12582912 | tf_op jit(solution)/shard_map/all_to_all | solution.py:223
  566.1 15.0 fusion.4
  599.9 141.6 %all_gather.30 = bf16[2048,32]{0,1:T(8,128)(2,1)S(1)} all-gather(bf16[512,32]{0,1:T(8,128)(2,1)S(1)} %copy-done.53), channel_id=1, replica_groups=mesh['ctx'=4,'fsdp'=4,'tp'=2] {'fsdp'}, dimensions={0}, use_global_device_ids=true | all-gather | bytes 163840 | tf_op jit(solution)/shard_map/all_gather | solution.py:104
  750.8 12.4 gather_fusion.1
  775.4 15.4 gather_fusion.2
  790.8 145.0 %all_to_all.21 = bf16[32,48,2048]{2,1,0:T(8,128)(2,1)S(1)} all-to-all(bf16[32,48,2048]{2,1,0:T(8,128)(2,1)} %bitcast.228), channel_id=1, replica_groups=mesh['ctx'=4,'fsdp'=4,'tp'=2] {'ctx','fsdp','tp'}, dimensions={0} | all-to-all | bytes 12582912 | tf_op jit(solution)/shard_map/all_to_all | solution.py:262
  947.2 11.8 convolution_convert_fusion.1
  971.4 132.6 %all-to-all-done.3 = bf16[32,48,2048]{2,1,0:T(8,128)(2,1)} async-done(((bf16[32,48,2048]{2,1,0:T(8,128)(2,1)}), bf16[32,48,2048]{2,1,0:T(8,128)(2,1)}, u32[]{:S(2)}, u32[]{:S(2)}) %all-to-all-start.3) | async-done | bytes 6291488 | tf_op jit(solution)/shard_map/all_to_all | solution.py:274
  1103.9 12.4 gather_fusion.3
  1125.7 21.0 %all-gather.14.cloned.1.call-done = bf16[256,2048]{1,0:T(8,128)(2,1)} async-done(((bf16[128,2048]{1,0:T(8,128)(2,1)}), bf16[256,2048]{1,0:T(8,128)(2,1)}) %all-gather.14.cloned.1.call-update) | async-done | bytes 1048592 | tf_op jit(solution)/shard_map/all_gather | solution.py:286
  1153.1 12.8 multiply_reduce_fusion
  1165.9 12.8 multiply_convert_fusion
  1212.4 25.6 %reduce-scatter.9.cloned.1.call-done = f32[2,256,128]{2,1,0:T(8,128)} async-done(((f32[2,1024,128]{2,1,0:T(8,128)}), f32[2,256,128]{2,1,0:T(8,128)}) %reduce-scatter.9.cloned.1.call-update) | async-done | bytes 262160 | tf_op jit(solution)/shard_map/reduce_scatter | solution.py:336
  1266.3 101.0 %all-reduce.7.cloned.1.call-done = f32[2048,32]{0,1:T(8,128)} async-done(((f32[2048,32]{0,1:T(8,128)}), f32[2048,32]{0,1:T(8,128)}) %all-reduce.7.cloned.1.call-update) | async-done | bytes 262160 | tf_op jit(solution)/shard_map/psum | solution.py:364
  1378.9 14.9 convolution_bitcast_fusion
  1395.2 43.5 %all-reduce.2 = (f32[]{:T(128)}, f32[2048]{0:T(1024)}, f32[128]{0:T(128)}, f32[128]{0:T(128)}, f32[2048]{0:T(1024)}) all-reduce(f32[]{:T(128)} %get-tuple-element.127, f32[2048]{0:T(1024)S(1)} %get-tuple-element.123, f32[128]{0:T(128)S(1)} %get-tuple-element.121, ...), channel_id=1, replica_groups=mesh['ctx'=4,'fsdp'=4,'tp'=2] {'ctx','fsdp','tp'}, use_global_device_ids=true, to_apply=%region_15.16 | all-reduce | flops 4353 | bytes 34824 | tf_op jit(solution)/shard_map/psum | solution.py:364
  1441.7 590.2 %all-reduce.9.cloned.1.call-done = (f32[2048,2048]{1,0:T(8,128)}, f32[2048,256]{1,0:T(8,128)}, f32[2048,256]{1,0:T(8,128)}, f32[2048,2048]{1,0:T(8,128)}) async-done(((f32[2048,2048]{1,0:T(8,128)}, f32[2048,256]{1,0:T(8,128)}, f32[2048,256]{1,0:T(8,128)}, f32[2048,2048]{1,0:T(8,128)}), (f32[2048,2048]{1,0:T(8,128)}, f32[2048,256]{1,0:T(8,128)}, f32[2048,256]{1,0:T(8,128)}, ...) | async-done | bytes 37748752 | tf_op jit(solution)/shard_map/psum | solution.py:377
  (302 shorter events, 262.6 us)
Async XLA Ops:
  7.2 577.7 %copy-start = (bf16[1,768,2048]{2,1,0:T(8,128)(2,1)S(1)}, bf16[1,768,2048]{2,1,0:T(8,128)(2,1)}, u32[]{:S(2)}) copy-start(bf16[1,768,2048]{2,1,0:T(8,128)(2,1)} %param.29) | copy-start | bytes 9437188
  7.2 32.1 %copy-start.41 = (f32[2048]{0:T(1024)S(1)}, f32[2048]{0:T(1024)}, u32[]{:S(2)}) copy-start(f32[2048]{0:T(1024)} %param.19) | copy-start | bytes 24580
  7.2 29.8 %all-gather.8.cloned.1.call-start = ((), (), s32[]{:S(2)}) async-start(), calls=%async_computation.9 | async-start | bytes 1310720 | tf_op jit(solution)/shard_map/all_gather | solution.py:101
  8.0 58.1 %all-gather.10.cloned.1.call-start = ((), (), s32[]{:S(2)}) async-start(), calls=%async_computation.10 | async-start | bytes 1310720 | tf_op jit(solution)/shard_map/all_gather | solution.py:102
  8.7 206.8 %all-gather.6.cloned.1.call-start = ((), (), s32[]{:S(2)}) async-start(), calls=%async_computation.8 | async-start | bytes 10485760 | tf_op jit(solution)/shard_map/all_gather | solution.py:100
  9.4 32.7 %copy-start.57 = (f32[128]{0:T(128)S(1)}, f32[128]{0:T(128)}, u32[]{:S(2)}) copy-start(f32[128]{0:T(128)} %param.25) | copy-start | bytes 1540
  9.4 355.4 %all-gather.12.cloned.1.call-start = ((), (), s32[]{:S(2)}) async-start(), calls=%async_computation.11 | async-start | bytes 10485760 | tf_op jit(solution)/shard_map/all_gather | solution.py:103
  10.0 395.3 %reduce-scatter.5.cloned.1.call-start = ((), (), s32[]{:S(2)}) async-start(), calls=%async_computation.12 | async-start | bytes 3145728 | tf_op jit(solution)/shard_map/reduce_scatter | solution.py:187
  12.9 215.1 %copy-start.54 = (f32[256]{0:T(256)}, f32[256]{0:T(256)S(1)}, u32[]{:S(2)}) copy-start(f32[256]{0:T(256)S(1)} %add_rsqrt_fusion.2) | copy-start | bytes 3076
  13.9 222.8 %copy-start.35 = (f32[256,64]{0,1:T(8,128)}, f32[256,64]{0,1:T(8,128)S(1)}, u32[]{:S(2)}) copy-start(f32[256,64]{0,1:T(8,128)S(1)} %get-tuple-element.176) | copy-start | bytes 196612
  14.1 239.2 %copy-start.20 = (pred[256,1024]{1,0:T(8,128)(4,1)}, pred[256,1024]{1,0:T(8,128)(4,1)S(1)}, u32[]{:S(2)}) copy-start(pred[256,1024]{1,0:T(8,128)(4,1)S(1)} %fusion.45) | copy-start | bytes 786436
  372.2 35.9 %copy-start.45 = (f32[2048]{0:T(1024)S(1)}, f32[2048]{0:T(1024)}, u32[]{:S(2)}) copy-start(f32[2048]{0:T(1024)} %param.26) | copy-start | bytes 24580
  591.9 149.6 %copy-start.64 = (s32[256]{0:T(256)S(1)}, s32[256]{0:T(256)}, u32[]{:S(2)}) copy-start(s32[256]{0:T(256)} %copy-done.63) | copy-start | bytes 3076
  591.9 158.9 %all-to-all-start.1 = ((bf16[32,48,2048]{2,1,0:T(8,128)(2,1)}), bf16[32,48,2048]{2,1,0:T(8,128)(2,1)}, u32[]{:S(2)}, u32[]{:S(2)}) async-start(bf16[32,48,2048]{2,1,0:T(8,128)(2,1)} %bitcast.241), calls=%async_computation.2 | async-start | bytes 12582912 | tf_op jit(solution)/shard_map/all_to_all | solution.py:239
  790.8 156.3 %slice-start.2 = ((s8[6291456]{0:T(1024)(128)(4,1)}), s8[4194304]{0:T(1024)(128)(4,1)S(1)}, s32[]{:S(2)}) async-start(s8[6291456]{0:T(1024)(128)(4,1)} %bitcast.268), calls=%async_computation.21 | async-start | bytes 8388608
  959.0 144.9 %all-to-all-start.3 = ((bf16[32,48,2048]{2,1,0:T(8,128)(2,1)}), bf16[32,48,2048]{2,1,0:T(8,128)(2,1)}, u32[]{:S(2)}, u32[]{:S(2)}) async-start(bf16[32,48,2048]{2,1,0:T(8,128)(2,1)} %bitcast.242), calls=%async_computation.4 | async-start | bytes 12582912 | tf_op jit(solution)/shard_map/all_to_all | solution.py:274
  965.4 181.3 %all-gather.14.cloned.1.call-start = ((), (), s32[]{:S(2)}) async-start(), calls=%async_computation.13 | async-start | bytes 1572864 | tf_op jit(solution)/shard_map/all_gather | solution.py:286
  1125.5 85.7 %reduce-scatter.7.cloned.1.call-start = ((), (), s32[]{:S(2)}) async-start(), calls=%async_computation.14 | async-start | bytes 1310720 | tf_op jit(solution)/shard_map/reduce_scatter | solution.py:335
  1184.9 53.1 %reduce-scatter.9.cloned.1.call-start = ((), (), s32[]{:S(2)}) async-start(), calls=%async_computation.15 | async-start | bytes 1310720 | tf_op jit(solution)/shard_map/reduce_scatter | solution.py:336
  1195.6 171.7 %all-reduce.7.cloned.1.call-start = ((), (), s32[]{:S(2)}) async-start(), calls=%async_computation.17 | async-start | bytes 524288 | tf_op jit(solution)/shard_map/psum | solution.py:364
  1196.7 197.2 %reduce-scatter.11.cloned.1.call-start = ((), (), s32[]{:S(2)}) async-start(), calls=%async_computation.16 | async-start | bytes 1572864 | tf_op jit(solution)/shard_map/reduce_scatter | solution.py:352
  1244.5 787.5 %all-reduce.9.cloned.1.call-start = ((), (), s32[]{:S(2)}) async-start(), calls=%async_computation.18 | async-start | bytes 75497472 | tf_op jit(solution)/shard_map/psum | solution.py:377
  1266.2 102.6 %copy-start.32 = (bf16[1536,768]{0,1:T(8,128)(2,1)S(1)}, bf16[1536,768]{0,1:T(8,128)(2,1)}, u32[]{:S(2)}) copy-start(bf16[1536,768]{0,1:T(8,128)(2,1)} %copy-done.31) | copy-start | bytes 7077892
  1378.9 60.5 %copy-start.26 = (f32[128,2048]{1,0:T(8,128)S(1)}, f32[128,2048]{1,0:T(8,128)}, u32[]{:S(2)}) copy-start(f32[128,2048]{1,0:T(8,128)} %get-tuple-element.154) | copy-start | bytes 3145732
  (65 other events, 531.2 us)
Sparse Core Ops, SparseCore 0:
  9.6 27.3 all-gather.7
  38.6 27.4 all-gather.9
  67.7 147.8 all-gather.5
  216.9 147.8 all-gather.11
  372.3 32.9 reduce-scatter.4
  1125.6 21.0 all-gather.13
  1185.0 24.8 reduce-scatter.6
  1213.1 24.9 reduce-scatter.8
  1245.0 122.2 all-reduce.6
  1370.1 21.9 reduce-scatter.10
  1397.5 634.4 all-reduce.8
where the time goes:
time: 2060 us; the launch traced here: 2050 us
  waiting for transfers between devices  1170 us (57%)
  blocking collectives  490 us (24%)
  matrix products  177 us (9%)
  local copies, waits for them, and re-layouts  119 us (6%)
  other arithmetic  66.1 us (3%)
    psum x1, waiting for transfers between devices, local(): lax.psum((grad_query_full, grad_key_full, grad_value_full, grad_w_output)...  590 us
    all_to_all x1, blocking collectives, local(): lax.all_to_all(send_grads, ('ctx', 'fsdp', 'tp'), split_axis=0, concat_ax...  145 us
    all_to_all x1, blocking collectives, local(): lax.all_to_all(send_rows, ('ctx', 'fsdp', 'tp'), split_axis=0, concat_axi...  142 us
    all_gather x1, blocking collectives, local(): lax.all_gather(w_router, 'fsdp', axis=0, tiled=True)  142 us
    all_to_all x1, waiting for transfers between devices, local(): lax.all_to_all(grad_rows, ('ctx', 'fsdp', 'tp'), split_axis=0, concat_axi...  133 us
    all_gather x1, waiting for transfers between devices, local(): lax.all_gather(w_query, 'fsdp', axis=0, tiled=True)  130 us
    all_gather x1, waiting for transfers between devices, local(): lax.all_gather(w_output, 'fsdp', axis=1, tiled=True)  105 us
    psum x1, waiting for transfers between devices, local(): lax.psum((jnp.sum(attn_gain_terms, axis=0), jnp.sum(ffn_gain_terms, axis=...  101 us
  transfers between devices with their start and end apart: 13, of which 10 were waited for; matrix products, arithmetic and copies ran while one was open for 8% of the time, Pallas kernels for 0%

commit v1 on v0

v1 whole, which is shorter than its diff:
```python
import functools

import jax
import jax.numpy as jnp
from jax import lax
from jax.experimental import pallas as pl
from jax.experimental.pallas import tpu as pltpu
from jax.sharding import PartitionSpec as P

EPS = 1e-06
ROPE_BASE = 1000000.0
MASKED = -1e30
AXES = ("ctx", "fsdp", "tp")
MESH = pl.DeviceIdType.MESH
ANY = pl.BlockSpec(memory_space=pl.ANY)
VMEM = pl.BlockSpec(memory_space=pltpu.VMEM)
BF = jnp.bfloat16
FL = jnp.float32
MIB = 1024 * 1024


def norm_rows(values, gain_vec):
    factor = lax.rsqrt(jnp.mean(values * values, axis=-1, keepdims=True) + EPS)
    return (values * factor * gain_vec, factor)


def norm_back(values, factor, gain_vec, upstream):
    weighted = upstream * gain_vec
    inner_mean = jnp.mean(values * weighted, axis=-1, keepdims=True)
    return (
        factor * weighted - values * (factor * factor * factor) * inner_mean,
        upstream * values * factor,
    )


def rope_tables(positions, head_size):
    half_size = head_size // 2
    frequency = jnp.power(ROPE_BASE, -jnp.arange(half_size, dtype=jnp.float32) * (2.0 / head_size))
    angles = positions.astype(jnp.float32)[:, None] * frequency[None, :]
    return (jnp.cos(angles), jnp.sin(angles))


def rotate(values, cosine, sine_tab):
    half_size = values.shape[-1] // 2
    front_half = values[..., :half_size]
    back_half = values[..., half_size:]
    cos_rows = cosine[:, None, :]
    sin_rows = sine_tab[:, None, :]
    return jnp.concatenate(
        [
            front_half * cos_rows - back_half * sin_rows,
            back_half * cos_rows + front_half * sin_rows,
        ],
        axis=-1,
    )


def inner_rows(left, right):
    return lax.dot_general(
        left, right, (((0,), (0,)), ((), ())), preferred_element_type=jnp.float32
    )


def outer_cols(left, right):
    return lax.dot_general(
        left, right, (((1,), (1,)), ((), ())), preferred_element_type=jnp.float32
    )


def block_scores(queries, key_rows, offset, positions, length, inv_root):
    block_len = key_rows.shape[1]
    raw_scores = (
        jnp.einsum("kgqd,kjd->kgqj", queries, key_rows, preferred_element_type=jnp.float32)
        * inv_root
    )
    key_pos = offset + jnp.arange(block_len, dtype=jnp.int32)
    allowed = (key_pos[None, :] <= positions[:, None]) & (key_pos[None, :] < length)
    return (jnp.where(allowed, raw_scores, MASKED), allowed)


def place():
    return tuple(lax.axis_index(axis) for axis in AXES)


def remote(source, target, sent, got, device):
    return pltpu.make_async_remote_copy(
        src_ref=source, dst_ref=target, send_sem=sent, recv_sem=got,
        device_id=device, device_id_type=MESH,
    )


def greet(devices):
    barrier = pltpu.get_barrier_semaphore()
    for device in devices:
        pl.semaphore_signal(barrier, inc=1, device_id=device, device_id_type=MESH)
    pl.semaphore_wait(barrier, len(devices))


def params(identity, mebibytes):
    return pltpu.CompilerParams(
        collective_id=identity, has_side_effects=True, vmem_limit_bytes=int(mebibytes * MIB)
    )


def gather_body(C, F, wa, wo, tab, fa, fo, ftab, loc, zs, zr, ys, yr, ks, kr, ts, tr):
    c, f, t = place()
    core, chip = lax.rem(c, 2), lax.div(c, 2)
    chips = C // 2
    sib = c + 1 - 2 * core
    ra, (ro, co) = wa.shape[0], wo.shape
    pa, po = ra // C, ro // C

    def spot(arr, b, p):
        if arr == 0:
            return fa.at[pl.ds(pl.multiple_of(b * ra + p * pa, pa), pa)]
        return fo.at[pl.ds(pl.multiple_of(p * po, po), po), pl.ds(pl.multiple_of(b * co, co), co)]

    def own(arr):
        if arr == 0:
            return wa.at[pl.ds(pl.multiple_of(c * pa, pa), pa)]
        return wo.at[pl.ds(pl.multiple_of(c * po, po), po)]

    peers = [(c, lax.rem(f + k, F), t) for k in range(1, F)]
    peers += [(lax.rem(chip + k, chips) * 2 + core, f, t) for k in range(1, chips)]
    peers += [(sib, f, t)]
    greet(peers)

    def z_copy(arr, s, d):
        b = f - (s - 1) if d == 0 else f + (s - 1)
        source = own(arr) if s == 1 else spot(arr, b, c)
        return remote(
            source, spot(arr, b, c), zs.at[d, s, arr], zr.at[d, s, arr],
            (c, f + 1 if d == 0 else f - 1, t),
        )

    def z_sends(s, d):
        b = f - (s - 1) if d == 0 else f + (s - 1)
        return (f + 1 < F) & (b >= 0) if d == 0 else (f > 0) & (b < F)

    def z_gets(s, d):
        return f - s >= 0 if d == 0 else f + s < F

    def came(s, d):
        return f - s if d == 0 else f + s

    def z_arrival(arr, s, d):
        b = came(s, d)
        here = spot(arr, b, c)
        return remote(here, here, zs.at[d, s, arr], zr.at[d, s, arr], (c, f, t))

    def y_copy(arr, s, d, k):
        here = spot(arr, came(s, d), c)
        there = (lax.rem(chip + k, chips) * 2 + core, f, t)
        return remote(here, here, ys.at[d, s, k, arr], yr.at[d, s, k, arr], there)

    def k_copy(arr, s, d, k, side):
        p = lax.rem(chip + chips - k, chips) * 2 + side
        here = spot(arr, came(s, d), p)
        return remote(here, here, ks.at[d, s, k, arr], kr.at[d, s, k, arr], (sib, f, t))

    def y_arrival(arr, s, d, k):
        p = lax.rem(chip + chips - k, chips) * 2 + core
        here = spot(arr, came(s, d), p)
        return remote(here, here, ys.at[d, s, k, arr], yr.at[d, s, k, arr], (sib, f, t))

    tabs = [
        remote(tab, ftab.at[f], ts.at[k], tr.at[k], (c, lax.rem(f + k, F), t)) for k in range(1, F)
    ]
    for copy in tabs:
        copy.start()
    for d in range(2):

        @pl.when(z_sends(1, d))
        def _():
            for arr in range(2):
                z_copy(arr, 1, d).start()

    locals_ = [
        pltpu.make_async_copy(tab, ftab.at[f], loc.at[0]),
        pltpu.make_async_copy(wa, fa.at[pl.ds(pl.multiple_of(f * ra, ra), ra)], loc.at[1]),
        pltpu.make_async_copy(wo, fo.at[:, pl.ds(pl.multiple_of(f * co, co), co)], loc.at[2]),
    ]
    for copy in locals_:
        copy.start()

    def pass_on(s, d):
        for arr in range(2):
            for k in range(1, chips):
                y_arrival(arr, s, d, k).wait_recv()
                k_copy(arr, s, d, k, core).start()

    for s in range(1, F):
        for d in range(2):

            @pl.when(z_gets(s, d))
            def _():
                for arr in range(2):
                    z_arrival(arr, s, d).wait_recv()
                    if s + 1 < F:

                        @pl.when(z_sends(s + 1, d))
                        def _():
                            z_copy(arr, s + 1, d).start()

                    for k in range(1, chips):
                        y_copy(arr, s, d, k).start()
                    k_copy(arr, s, d, 0, core).start()

        if s > 1:
            for d in range(2):
                pl.when(z_gets(s - 1, d))(functools.partial(pass_on, s - 1, d))
    for d in range(2):
        pl.when(z_gets(F - 1, d))(functools.partial(pass_on, F - 1, d))
    for copy in tabs:
        copy.wait()
    for copy in locals_:
        copy.wait()
    for s in range(1, F):
        for d in range(2):

            @pl.when(z_sends(s, d))
            def _():
                for arr in range(2):
                    z_copy(arr, s, d).wait_send()

            @pl.when(z_gets(s, d))
            def _():
                for arr in range(2):
                    for k in range(1, chips):
                        y_copy(arr, s, d, k).wait_send()
                    for k in range(chips):
                        k_copy(arr, s, d, k, core).wait_send()
                        k_copy(arr, s, d, k, 1 - core).wait_recv()


def gather_weights(C, F, wa, wo, tab):
    ra, ca = wa.shape
    ro, co = wo.shape
    chips = C // 2
    dma = pltpu.SemaphoreType.DMA
    return pl.pallas_call(
        functools.partial(gather_body, C, F),
        out_shape=(
            jax.ShapeDtypeStruct((F * ra, ca), wa.dtype),
            jax.ShapeDtypeStruct((ro, F * co), wo.dtype),
            jax.ShapeDtypeStruct((F,) + tab.shape, tab.dtype),
        ),
        in_specs=[ANY] * 3,
        out_specs=[ANY] * 3,
        scratch_shapes=[
            dma((3,)), dma((2, F, 2)), dma((2, F, 2)),
            dma((2, F, chips, 2)), dma((2, F, chips, 2)),
            dma((2, F, chips, 2)), dma((2, F, chips, 2)),
            dma((F,)), dma((F,)),
        ],
        compiler_params=params(1, 16),
    )(wa, wo, tab)


def slab_place(C, T):
    c, f, t = place()
    return c, f, t, c * T + t


def slab_device(index, f, T):
    return (lax.div(index, T), f, lax.rem(index, T))


def dispatch_body(C, F, T, tabbed, rows, select, *refs):
    if tabbed:
        tab, out, zbuf, ftab, stage, loc, zs, zr, ss, sr, ts, tr = refs
    else:
        out, zbuf, stage, loc, zs, zr, ss, sr = refs
    c, f, t, me = slab_place(C, T)
    S = C * T
    K = select.shape[2]
    copies = select.shape[3] // rows.shape[0]
    columns = [(c, lax.rem(f + k, F), t) for k in range(1, F)]
    greet(columns + [slab_device(lax.rem(me + j, S), f, T) for j in range(1, S)])
    sends = [
        remote(rows, zbuf.at[f], zs.at[k], zr.at[k], columns[k - 1]) for k in range(1, F)
    ]
    if tabbed:
        tabs = [remote(tab, ftab.at[f], ts.at[k], tr.at[k], columns[k - 1]) for k in range(1, F)]
        for copy in tabs:
            copy.start()
        ftab[f] = tab[...]
    for copy in sends:
        copy.start()
    zbuf[f] = rows[...]

    def slab_copy(k, j):
        b = lax.rem(f + F - k, F)
        e = lax.rem(me + j, S)
        return remote(
            stage.at[e, b], out.at[me, b], ss.at[k, j], sr.at[k, j], slab_device(e, f, T)
        )

    def slab_arrival(k, j):
        b = lax.rem(f + F - k, F)
        e = lax.rem(me + S - j, S)
        return remote(
            stage.at[e, b], out.at[e, b], ss.at[k, j], sr.at[k, j], slab_device(e, f, T)
        )

    def own_copy(k):
        b = lax.rem(f + F - k, F)
        return pltpu.make_async_copy(stage.at[me, b], out.at[me, b], loc.at[k])

    for k in range(F):
        b = lax.rem(f + F - k, F)
        if k > 0:
            remote(rows, zbuf.at[b], zs.at[k], zr.at[k], columns[k - 1]).wait_recv()

        def pick(j):
            e = lax.rem(me + j, S)
            block = zbuf[b]
            if copies > 1:
                block = jnp.concatenate([block] * copies, axis=0)
            stage[e, b] = jnp.dot(
                select[b, e], block, preferred_element_type=FL
            ).astype(BF)

        if S <= 8:
            for j in range(1, S):
                pick(j)
                slab_copy(k, j).start()
        else:

            def step(j, carry):
                pick(j)
                slab_copy(k, j).start()
                return carry

            lax.fori_loop(1, S, step, 0)
        pick(0)
        own_copy(k).start()
    if tabbed:
        for copy in tabs:
            copy.wait()
    for copy in sends:
        copy.wait_send()
    for k in range(F):
        own_copy(k).wait()

        def settle(j, carry):
            slab_copy(k, j).wait_send()
            slab_arrival(k, j).wait_recv()
            return carry

        lax.fori_loop(1, S, settle, 0)


def dispatch(identity, C, F, T, rows, select, tab=None):
    S = C * T
    K = select.shape[2]
    R, W = rows.shape
    dma = pltpu.SemaphoreType.DMA
    tabbed = tab is not None
    outs = [jax.ShapeDtypeStruct((S, F, K, W), BF), jax.ShapeDtypeStruct((F, R, W), BF)]
    out_specs = [ANY, VMEM]
    ins = [rows, select]
    scratch = [
        pltpu.VMEM((S, F, K, W), BF), dma((F,)), dma((F,)), dma((F,)), dma((F, S)), dma((F, S)),
    ]
    if tabbed:
        outs.append(jax.ShapeDtypeStruct((F,) + tab.shape, tab.dtype))
        out_specs.append(VMEM)
        ins.append(tab)
        scratch += [dma((F,)), dma((F,))]
    return pl.pallas_call(
        functools.partial(dispatch_body, C, F, T, tabbed),
        out_shape=tuple(outs),
        in_specs=[VMEM] * len(ins),
        out_specs=out_specs,
        scratch_shapes=scratch,
        compiler_params=params(identity, 32),
    )(*ins)


def combine_body(C, F, T, tabbed, rows, weigh, *refs):
    if tabbed:
        tab, got, part, ftab, stage, loc, zs, zr, ss, sr, ts, tr = refs
    else:
        got, part, stage, loc, zs, zr, ss, sr = refs
    c, f, t, me = slab_place(C, T)
    S = C * T
    K, W = got.shape[2], got.shape[3]
    n = weigh.shape[1]
    columns = [(c, lax.rem(f + k, F), t) for k in range(1, F)]
    greet(columns + [slab_device(lax.rem(me + j, S), f, T) for j in range(1, S)])

    def slab_copy(k, j):
        b = lax.rem(f + k, F)
        e = lax.rem(me + j, S)
        return remote(
            rows.at[e, b], got.at[b, me], ss.at[k, j], sr.at[k, j], slab_device(e, f, T)
        )

    def slab_arrival(k, j):
        b = lax.rem(f + k, F)
        e = lax.rem(me + S - j, S)
        return remote(
            rows.at[e, b], got.at[b, e], ss.at[k, j], sr.at[k, j], slab_device(e, f, T)
        )

    def own_copy(k):
        b = lax.rem(f + k, F)
        return pltpu.make_async_copy(rows.at[me, b], got.at[b, me], loc.at[k])

    order = list(range(1, F)) + [0]
    for k in order:

        def begin(j, carry):
            slab_copy(k, j).start()
            return carry

        lax.fori_loop(1, S, begin, 0)
        own_copy(k).start()
    if tabbed:
        tabs = [
            remote(tab.at[lax.rem(f + k, F)], ftab.at[f], ts.at[k], tr.at[k], columns[k - 1])
            for k in range(1, F)
        ]
        for copy in tabs:
            copy.start()
        ftab[f] = tab[f]

    def z_copy(k):
        b = lax.rem(f + k, F)
        return remote(stage.at[b], part.at[f], zs.at[k], zr.at[k], columns[k - 1])

    def z_arrival(k):
        b = lax.rem(f + F - k, F)
        return remote(stage.at[b], part.at[b], zs.at[k], zr.at[k], columns[k - 1])

    step = min(W, 512)
    for k in order:
        b = lax.rem(f + k, F)
        own_copy(k).wait()

        def settle(j, carry):
            slab_arrival(k, j).wait_recv()
            return carry

        lax.fori_loop(1, S, settle, 0)
        target = part if k == 0 else stage

        def add(i, carry):
            columns_ = pl.ds(pl.multiple_of(i * step, step), step)
            block = got[b, :, :, columns_].reshape(S * K, step)
            total = jnp.dot(weigh[b, 0], block, preferred_element_type=FL)
            for m in range(1, n):
                total += jnp.dot(weigh[b, m], block, preferred_element_type=FL)
            target[b, :, columns_] = total.astype(BF)
            return carry

        lax.fori_loop(0, W // step, add, 0)
        if k > 0:
            z_copy(k).start()
    for k in range(1, F):
        z_copy(k).wait_send()
        z_arrival(k).wait_recv()
    for k in range(F):

        def leave(j, carry):
            slab_copy(k, j).wait_send()
            return carry

        lax.fori_loop(1, S, leave, 0)
    if tabbed:
        for copy in tabs:
            copy.wait()


def combine(identity, C, F, T, rows, weigh, tab=None):
    S, _, K, W = rows.shape
    R = weigh.shape[2]
    dma = pltpu.SemaphoreType.DMA
    tabbed = tab is not None
    outs = [jax.ShapeDtypeStruct((F, S, K, W), BF), jax.ShapeDtypeStruct((F, R, W), BF)]
    ins = [rows, weigh]
    scratch = [
        pltpu.VMEM((F, R, W), BF), dma((F,)), dma((F,)), dma((F,)), dma((F, S)), dma((F, S)),
    ]
    if tabbed:
        outs.append(jax.ShapeDtypeStruct(tab.shape, tab.dtype))
        ins.append(tab)
        scratch += [dma((F,)), dma((F,))]
    return pl.pallas_call(
        functools.partial(combine_body, C, F, T, tabbed),
        out_shape=tuple(outs),
        in_specs=[ANY] + [VMEM] * (len(ins) - 1),
        out_specs=[VMEM] * len(outs),
        scratch_shapes=scratch,
        compiler_params=params(identity, 32),
    )(*ins)


def ctx_sum_body(C, x, out, got, ss, sr):
    c, f, t = place()
    peers = [(lax.rem(c + k, C), f, t) for k in range(1, C)]
    greet(peers)

    def copy(k):
        p = lax.rem(c + k, C)
        return remote(x.at[p], got.at[c], ss.at[k], sr.at[k], (p, f, t))

    def arrival(k):
        p = lax.rem(c + C - k, C)
        return remote(x.at[p], got.at[p], ss.at[k], sr.at[k], (p, f, t))

    for k in range(1, C):
        copy(k).start()
    got[c] = x[c]
    for k in range(1, C):
        arrival(k).wait_recv()
    total = got[0].astype(FL)
    for p in range(1, C):
        total += got[p].astype(FL)
    out[...] = total
    for k in range(1, C):
        copy(k).wait_send()


def ctx_sum(identity, C, x):
    dma = pltpu.SemaphoreType.DMA
    return pl.pallas_call(
        functools.partial(ctx_sum_body, C),
        out_shape=jax.ShapeDtypeStruct(x.shape[1:], FL),
        in_specs=[VMEM],
        out_specs=VMEM,
        scratch_shapes=[pltpu.VMEM(x.shape, x.dtype), dma((C,)), dma((C,))],
        compiler_params=params(identity, 24),
    )(x)


def small_body(C, F, T, x, out, zgot, mid, sgot, zs, zr, ss, sr):
    c, f, t, me = slab_place(C, T)
    S = C * T
    columns = [(c, lax.rem(f + k, F), t) for k in range(1, F)]
    greet(columns + [slab_device(lax.rem(me + j, S), f, T) for j in range(1, S)])

    def z_copy(k):
        return remote(x.at[lax.rem(f + k, F)], zgot.at[f], zs.at[k], zr.at[k], columns[k - 1])

    def z_arrival(k):
        b = lax.rem(f + F - k, F)
        return remote(x.at[b], zgot.at[b], zs.at[k], zr.at[k], columns[k - 1])

    for k in range(1, F):
        z_copy(k).start()
    zgot[f] = x[f]
    for k in range(1, F):
        z_arrival(k).wait_recv()
    total = zgot[0]
    for b in range(1, F):
        total += zgot[b]
    mid[...] = total
    sgot[me] = total

    def s_copy(j):
        return remote(
            mid, sgot.at[me], ss.at[j], sr.at[j], slab_device(lax.rem(me + j, S), f, T)
        )

    def s_arrival(j):
        e = lax.rem(me + S - j, S)
        return remote(mid, sgot.at[e], ss.at[j], sr.at[j], slab_device(e, f, T))

    for j in range(1, S):
        s_copy(j).start()
    for j in range(1, S):
        s_arrival(j).wait_recv()
    total = sgot[0]
    for e in range(1, S):
        total += sgot[e]
    out[...] = total
    for k in range(1, F):
        z_copy(k).wait_send()
    for j in range(1, S):
        s_copy(j).wait_send()


def small_sum(identity, C, F, T, x):
    dma = pltpu.SemaphoreType.DMA
    S = C * T
    one = x.shape[1:]
    return pl.pallas_call(
        functools.partial(small_body, C, F, T),
        out_shape=jax.ShapeDtypeStruct(one, FL),
        in_specs=[VMEM],
        out_specs=VMEM,
        scratch_shapes=[
            pltpu.VMEM((F,) + one, FL), pltpu.VMEM(one, FL), pltpu.VMEM((S,) + one, FL),
            dma((F,)), dma((F,)), dma((S,)), dma((S,)),
        ],
        compiler_params=params(identity, 24),
    )(x)


def far_first(F):
    table = []
    for f in range(F):
        order = []
        for i in range(F):
            ends = [F - 1 - i, i] if f * 2 < F else [i, F - 1 - i]
            for b in ends:
                if ((b > f and b == F - 1 - i) or (b < f and b == i)) and b not in order:
                    order.append(b)
        table.append(order + [f])
    return table


def grads_body(
    C, F, xt, da, ht, dt, outa, outo,
    ska, sko, rka, rko, sya, syo, rya, ryo, rza, rzo, sza, szo,
    k_s, k_r, y_s, y_r, z_s, z_r, g_s, g_r, h_s, h_r,
):
    c, f, t = place()
    core, chip = lax.rem(c, 2), lax.div(c, 2)
    chips = C // 2
    sib = c + 1 - 2 * core
    pa, po, co = outa.shape[1], outo.shape[1], outo.shape[2]
    ra = pa * C
    table = far_first(F)

    def block(q):
        value = jnp.int32(table[0][q])
        for g in range(1, F):
            value = jnp.where(f == g, table[g][q], value)
        return value

    blocks = [block(q) for q in range(F)]
    ends = [(c, lax.rem(f + 1, F), t), (c, lax.rem(f + F - 1, F), t)]
    mates = [(lax.rem(chip + k, chips) * 2 + core, f, t) for k in range(1, chips)]
    greet(ends + mates + [(sib, f, t)])

    def piece_a(b, p):
        rows = pl.ds(pl.multiple_of(b * ra + p * pa, pa), pa)
        return jnp.dot(xt[rows, :], da[...], preferred_element_type=FL)

    def piece_o(b, p):
        rows = pl.ds(pl.multiple_of(p * po, po), po)
        cols = pl.ds(pl.multiple_of(b * co, co), co)
        return jnp.dot(ht[rows, :], dt[:, cols], preferred_element_type=FL)

    def core_copies(q, k):
        b = blocks[q]
        return [
            remote(ska.at[b, k], rka.at[b, k], k_s.at[q, k, 0], k_r.at[q, k, 0], (sib, f, t)),
            remote(sko.at[b, k], rko.at[b, k], k_s.at[q, k, 1], k_r.at[q, k, 1], (sib, f, t)),
        ]

    for q in range(F):
        b = blocks[q]
        for k in [*range(1, chips), 0]:
            p = lax.rem(chip + k, chips) * 2 + 1 - core
            ska[b, k] = piece_a(b, p).astype(BF)
            sko[b, k] = piece_o(b, p).astype(BF)
            for copy in core_copies(q, k):
                copy.start()

    def chip_copies(q, k):
        b = blocks[q]
        there = mates[k - 1]
        return [
            remote(sya.at[b, k - 1], rya.at[b, k - 1], y_s.at[q, k, 0], y_r.at[q, k, 0], there),
            remote(syo.at[b, k - 1], ryo.at[b, k - 1], y_s.at[q, k, 1], y_r.at[q, k, 1], there),
        ]

    for q in range(F):
        b = blocks[q]
        for k in range(1, chips):
            p = lax.rem(chip + k, chips) * 2 + core
            for copy in core_copies(q, k):
                copy.wait_recv()
            sya[b, k - 1] = (piece_a(b, p) + rka[b, k].astype(FL)).astype(BF)
            syo[b, k - 1] = (piece_o(b, p) + rko[b, k].astype(FL)).astype(BF)
            for copy in chip_copies(q, k):
                copy.start()

    def z_copies(q, b, slot, there):
        return [
            remote(sza.at[b], rza.at[slot], z_s.at[q, 0], z_r.at[slot, 0], there),
            remote(szo.at[b], rzo.at[slot], z_s.at[q, 1], z_r.at[slot, 1], there),
        ]

    def z_wait(slot):
        for copy in z_copies(0, 0, slot, ends[0]):
            copy.wait_recv()

    for q in range(F):
        b = blocks[q]
        for copy in core_copies(q, 0):
            copy.wait_recv()
        for k in range(1, chips):
            for copy in chip_copies(q, k):
                copy.wait_recv()
        total_a = piece_a(b, c) + rka[b, 0].astype(FL)
        total_o = piece_o(b, c) + rko[b, 0].astype(FL)
        for k in range(1, chips):
            total_a += rya[b, k - 1].astype(FL)
            total_o += ryo[b, k - 1].astype(FL)
        if q < F - 1:
            up = b > f
            first = jnp.where(up, f == 0, f == F - 1)

            @pl.when(first)
            def _():
                sza[b] = total_a.astype(BF)
                szo[b] = total_o.astype(BF)

            @pl.when(jnp.logical_not(first))
            def _():
                z_wait(b)
                sza[b] = (total_a + rza[b].astype(FL)).astype(BF)
                szo[b] = (total_o + rzo[b].astype(FL)).astype(BF)

            @pl.when(up)
            def _():
                for copy in z_copies(q, b, b, (c, f + 1, t)):
                    copy.start()

            @pl.when(jnp.logical_not(up))
            def _():
                slot = jnp.where(b == f - 1, F, b)
                for copy in z_copies(q, b, slot, (c, f - 1, t)):
                    copy.start()

        else:
            sza[f] = total_a.astype(BF)
            szo[f] = total_o.astype(BF)

            @pl.when(f > 0)
            def _():
                z_wait(f)
                sza[f] = (total_a + rza[f].astype(FL)).astype(BF)
                szo[f] = (total_o + rzo[f].astype(FL)).astype(BF)

            @pl.when(f < F - 1)
            def _():
                z_wait(F)
                outa[c] = (sza[f].astype(FL) + rza[F].astype(FL)).astype(BF)
                outo[c] = (szo[f].astype(FL) + rzo[F].astype(FL)).astype(BF)

            @pl.when(f == F - 1)
            def _():
                outa[c] = sza[f]
                outo[c] = szo[f]

    def spread(k):
        there = mates[k - 1]
        return [
            remote(outa.at[c], outa.at[c], g_s.at[k, 0], g_r.at[k, 0], there),
            remote(outo.at[c], outo.at[c], g_s.at[k, 1], g_r.at[k, 1], there),
        ]

    def hand(k, side):
        p = lax.rem(chip + chips - k, chips) * 2 + side
        return [
            remote(outa.at[p], outa.at[p], h_s.at[k, 0], h_r.at[k, 0], (sib, f, t)),
            remote(outo.at[p], outo.at[p], h_s.at[k, 1], h_r.at[k, 1], (sib, f, t)),
        ]

    def spread_arrival(k):
        p = lax.rem(chip + chips - k, chips) * 2 + core
        return [
            remote(outa.at[p], outa.at[p], g_s.at[k, 0], g_r.at[k, 0], mates[k - 1]),
            remote(outo.at[p], outo.at[p], g_s.at[k, 1], g_r.at[k, 1], mates[k - 1]),
        ]

    for k in range(1, chips):
        for copy in spread(k):
            copy.start()
    for copy in hand(0, core):
        copy.start()
    for k in range(1, chips):
        for copy in spread_arrival(k):
            copy.wait_recv()
        for copy in hand(k, core):
            copy.start()
    for k in range(chips):
        for copy in hand(k, 1 - core):
            copy.wait_recv()
        for copy in hand(k, core):
            copy.wait_send()
    for k in range(1, chips):
        for copy in spread(k):
            copy.wait_send()
    for q in range(F):
        for k in range(chips):
            for copy in core_copies(q, k):
                copy.wait_send()
        for k in range(1, chips):
            for copy in chip_copies(q, k):
                copy.wait_send()
        if q < F - 1:
            for copy in z_copies(q, 0, 0, ends[0]):
                copy.wait_send()


def weight_grads(identity, C, F, xt, da, ht, dt):
    D, R = xt.shape
    pa, na = D // F // C, da.shape[1]
    po, no = ht.shape[0] // C, dt.shape[1] // F
    chips = C // 2
    dma = pltpu.SemaphoreType.DMA

    def pair(*lead):
        return [pltpu.VMEM(lead + (pa, na), BF), pltpu.VMEM(lead + (po, no), BF)]

    return pl.pallas_call(
        functools.partial(grads_body, C, F),
        out_shape=(
            jax.ShapeDtypeStruct((C, pa, na), BF),
            jax.ShapeDtypeStruct((C, po, no), BF),
        ),
        in_specs=[VMEM] * 4,
        out_specs=[VMEM] * 2,
        scratch_shapes=[
            *pair(F, chips), *pair(F, chips), *pair(F, chips - 1), *pair(F, chips - 1),
            *pair(F + 1), *pair(F),
            dma((F, chips, 2)), dma((F, chips, 2)), dma((F, chips, 2)), dma((F, chips, 2)),
            dma((F, 2)), dma((F + 1, 2)), dma((chips, 2)), dma((chips, 2)),
            dma((chips, 2)), dma((chips, 2)),
        ],
        compiler_params=params(identity, 60),
    )(xt, da, ht, dt)


def split_low(values):
    high = lax.reduce_precision(values, 8, 7)
    return high.astype(BF), (values - high).astype(BF)


def local(
    hidden_in,
    teacher,
    lengths,
    routes,
    attn_gain,
    w_query,
    w_key,
    w_value,
    w_output,
    query_gain,
    key_gain,
    ffn_gain,
    w_router,
    w_expert_in,
    w_expert_out,
):
    c, f, t = place()
    C, F, T = (lax.axis_size(axis) for axis in AXES)
    S = C * T
    row_count = hidden_in.shape[1]
    width = hidden_in.shape[2]
    half_rows = row_count // T
    head_size = query_gain.shape[0]
    inv_root = head_size ** (-0.5)
    bf_type = BF
    fl_type = FL

    expert_count = S * F
    lanes = -(-expert_count // 128) * 128
    route_ids = routes[0]
    top_count = route_ids.shape[1]
    capacity = max(2, half_rows * top_count * 3 // (2 * expert_count))
    cap = -(-capacity // 16) * 16
    expert_ids = jnp.arange(lanes, dtype=jnp.int32)
    named = jnp.any(route_ids[:, :, None] == expert_ids[None, None, :], axis=1)
    row_ids = jnp.arange(half_rows, dtype=jnp.int32)
    below = (row_ids[None, :] < row_ids[:, None]).astype(bf_type)
    earlier = jnp.dot(below, named.astype(bf_type), preferred_element_type=fl_type)
    rank_tab = jnp.where(named, earlier, -1.0)

    q_cols, kv_cols = w_query.shape[1], w_key.shape[1]
    w_all = jnp.concatenate(
        [w_query, w_key, w_value, jnp.pad(w_router, ((0, 0), (0, lanes - expert_count)))], axis=1
    )
    full_all, full_o, rank_z = gather_weights(C, F, w_all, w_output, rank_tab)
    proj_cols = q_cols + 2 * kv_cols
    full_qkv = full_all[:, :proj_cols]
    full_router = full_all[:, proj_cols : proj_cols + expert_count]

    def of_slab(table):
        picked = table[:, :, :expert_count].reshape(F, half_rows, C, F, T)
        return lax.dynamic_index_in_dim(picked, f, 3, keepdims=False).reshape(F, half_rows, S)

    rank_slab = of_slab(rank_z)
    slot_ids = jnp.arange(cap, dtype=fl_type)
    chosen_rows = rank_slab[:, :, :, None] == slot_ids
    chosen_slots = (
        jnp.transpose(rank_slab, (0, 2, 1))[:, :, None, :] == slot_ids[:, None]
    )

    q_heads = q_cols // head_size
    kv_heads = kv_cols // head_size
    group_size = q_heads // kv_heads
    inputs = hidden_in[0].astype(fl_type)
    normed, norm_factor = norm_rows(inputs, attn_gain)
    normed_low = normed.astype(bf_type)
    raw = jnp.dot(normed_low, full_qkv, preferred_element_type=fl_type)
    q_raw = raw[:, :q_cols].reshape(row_count, q_heads, head_size)
    k_raw = raw[:, q_cols : q_cols + kv_cols].reshape(row_count, kv_heads, head_size)
    values_low = raw[:, q_cols + kv_cols :].astype(bf_type).reshape(row_count, kv_heads, head_size)
    q_normed, q_factor = norm_rows(q_raw, query_gain)
    k_normed, k_factor = norm_rows(k_raw, key_gain)
    positions = c * row_count + jnp.arange(row_count, dtype=jnp.int32)
    cosine, sine_tab = rope_tables(positions, head_size)
    q_rot = rotate(q_normed, cosine, sine_tab).astype(bf_type)
    k_rot = rotate(k_normed, cosine, sine_tab).astype(bf_type)
    queries = jnp.transpose(q_rot.reshape(row_count, kv_heads, group_size, head_size), (1, 2, 0, 3))
    both = jnp.transpose(jnp.concatenate([k_rot, values_low], axis=1), (1, 0, 2))
    all_both = lax.all_gather(both, "ctx", axis=1, tiled=True)
    all_keys, all_values = all_both[:kv_heads], all_both[kv_heads:]
    total_len = all_keys.shape[1]
    block_len = min(1024, total_len)
    offsets = jnp.arange(total_len // block_len, dtype=jnp.int32) * block_len
    length = jnp.take(lengths, f)
    stat_shape = (kv_heads, group_size, row_count)

    def lse_step(carry, offset):
        running_max, running_sum = carry
        key_rows = lax.dynamic_slice_in_dim(all_keys, offset, block_len, 1)
        scores, allowed = block_scores(queries, key_rows, offset, positions, length, inv_root)
        new_max = jnp.maximum(running_max, jnp.max(scores, axis=-1))
        exponent = jnp.where(allowed, jnp.exp(scores - new_max[..., None]), 0.0)
        return (
            (new_max, running_sum * jnp.exp(running_max - new_max) + jnp.sum(exponent, axis=-1)),
            None,
        )

    (row_max, row_sum), _ = lax.scan(
        lse_step, (jnp.full(stat_shape, MASKED, fl_type), jnp.zeros(stat_shape, fl_type)), offsets
    )
    log_total = row_max + jnp.log(row_sum)

    def probs_of(offset):
        key_rows = lax.dynamic_slice_in_dim(all_keys, offset, block_len, 1)
        value_rows = lax.dynamic_slice_in_dim(all_values, offset, block_len, 1)
        scores, allowed = block_scores(queries, key_rows, offset, positions, length, inv_root)
        return (
            jnp.where(allowed, jnp.exp(scores - log_total[..., None]), 0.0),
            key_rows,
            value_rows,
        )

    def out_step(running, offset):
        probabilities, key_rows, value_rows = probs_of(offset)
        return (
            running
            + jnp.einsum(
                "kgqj,kjd->kgqd",
                probabilities.astype(bf_type),
                value_rows,
                preferred_element_type=fl_type,
            ),
            None,
        )

    attn_acc, _ = lax.scan(
        out_step, jnp.zeros((kv_heads, group_size, row_count, head_size), fl_type), offsets
    )
    heads_low = (
        jnp.transpose(attn_acc, (2, 0, 1, 3))
        .reshape(row_count, q_heads * head_size)
        .astype(bf_type)
    )
    swap = [(i, 1 - i) for i in range(T)]
    row_start = t * half_rows
    other_start = (1 - t) * half_rows
    heads_other = lax.dynamic_slice_in_dim(heads_low, other_start, half_rows, 0)
    heads_own = lax.dynamic_slice_in_dim(heads_low, row_start, half_rows, 0)
    theirs = jnp.dot(heads_other, full_o, preferred_element_type=fl_type).astype(bf_type)
    ours = lax.ppermute(theirs, "tp", swap)
    attn_rows = jnp.dot(heads_own, full_o, preferred_element_type=fl_type) + ours.astype(fl_type)
    own_inputs = lax.dynamic_slice_in_dim(inputs, row_start, half_rows, 0)
    own_factor = lax.dynamic_slice_in_dim(norm_factor, row_start, half_rows, 0)
    own_positions = lax.dynamic_slice_in_dim(positions, row_start, half_rows, 0)
    residual = own_inputs + attn_rows
    ffn_in, ffn_factor = norm_rows(residual, ffn_gain)
    ffn_low = ffn_in.astype(bf_type)
    logits = jnp.dot(ffn_low, full_router, preferred_element_type=fl_type)
    is_named = named[:, :expert_count]
    masked = jnp.where(is_named, logits, MASKED)
    shifted = jnp.where(is_named, jnp.exp(masked - jnp.max(masked, axis=-1, keepdims=True)), 0.0)
    gates = shifted / jnp.sum(shifted, axis=-1, keepdims=True)
    gate_tab = jnp.pad(gates, ((0, 0), (0, lanes - expert_count)))

    select = chosen_slots.astype(bf_type)
    received, _, gate_z = dispatch(2, C, F, T, ffn_low, select, gate_tab)
    expert_rows = received.reshape(-1, width)
    both_pre = jnp.dot(expert_rows, w_expert_in[0], preferred_element_type=fl_type)
    ff_width = w_expert_out.shape[1]
    gate_pre = both_pre[:, :ff_width]
    up_pre = both_pre[:, ff_width:]
    sigmoid_gate = jax.nn.sigmoid(gate_pre)
    silu_gate = gate_pre * sigmoid_gate
    mixed_low = (silu_gate * up_pre).astype(bf_type)
    expert_out = (
        jnp.dot(mixed_low, w_expert_out[0], preferred_element_type=fl_type)
        .astype(bf_type)
        .reshape(S, F, cap, width)
    )
    gate_slab = of_slab(gate_z)
    weigh = jnp.where(chosen_rows, gate_slab[..., None], 0.0).reshape(F, 1, half_rows, S * cap)
    weigh = jnp.concatenate(split_low(weigh), axis=1)
    returned, parts = combine(3, C, F, T, expert_out, weigh)
    output_f = residual + jnp.sum(parts.astype(fl_type), axis=0)
    count = jnp.sum(lengths).astype(fl_type)
    tokens_total = lengths.shape[0] * row_count * C
    valid = own_positions < length
    error = jnp.where(valid[:, None], output_f - teacher[0].astype(fl_type), 0.0)
    loss_part = jnp.sum(error * error)
    grad_out = error * (tokens_total / count)

    select_gates = jnp.where(
        chosen_slots, jnp.transpose(gate_slab, (0, 2, 1))[:, :, None, :], 0.0
    )
    select_gates = jnp.concatenate(split_low(select_gates), axis=-1)
    grad_recv, grad_out_z = dispatch(4, C, F, T, grad_out.astype(bf_type), select_gates)
    slot_grads = jnp.einsum("zskr,zrd->zskd", select, grad_out_z, preferred_element_type=fl_type)
    slot_gate = jnp.sum(slot_grads * returned.astype(fl_type), axis=-1)
    gate_grads = jnp.sum(jnp.where(chosen_rows, slot_gate[:, None, :, :], 0.0), axis=-1)
    gate_grads = jnp.pad(gate_grads, ((0, 0), (0, 0), (0, -S % 128)))

    grad_recv = grad_recv.reshape(-1, width)
    grad_mixed = outer_cols(grad_recv, w_expert_out[0])
    grad_expert_out = inner_rows(mixed_low, grad_recv)
    grad_gate_pre = grad_mixed * up_pre * (sigmoid_gate * (1.0 + gate_pre * (1.0 - sigmoid_gate)))
    grad_up_pre = grad_mixed * silu_gate
    grad_pre = jnp.concatenate([grad_gate_pre, grad_up_pre], axis=1).astype(bf_type)
    grad_expert_in = inner_rows(expert_rows, grad_pre)
    grad_rows = (
        outer_cols(grad_pre, w_expert_in[0]).astype(bf_type).reshape(S, F, cap, width)
    )
    weigh_one = chosen_rows.astype(bf_type).reshape(F, 1, half_rows, S * cap)
    _, grad_parts, gate_back = combine(5, C, F, T, grad_rows, weigh_one, gate_grads)
    grad_gate = jnp.transpose(
        gate_back[:, :, :S].reshape(F, half_rows, C, T), (1, 2, 0, 3)
    ).reshape(half_rows, expert_count)
    grad_logits = (
        gates * (grad_gate - jnp.sum(gates * grad_gate, axis=-1, keepdims=True))
    ).astype(bf_type)
    grad_ffn = jnp.sum(grad_parts.astype(fl_type), axis=0) + outer_cols(grad_logits, full_router)
    router_part = inner_rows(ffn_low, grad_logits)
    grad_resid_norm, ffn_gain_terms = norm_back(residual, ffn_factor, ffn_gain, grad_ffn)
    grad_residual = grad_out + grad_resid_norm
    grad_own = grad_residual.astype(bf_type)
    grad_other = lax.ppermute(grad_own, "tp", swap)
    grad_attn = jnp.where(
        t == 0,
        jnp.concatenate([grad_own, grad_other], axis=0),
        jnp.concatenate([grad_other, grad_own], axis=0),
    )
    grad_heads = jnp.transpose(
        outer_cols(grad_attn, full_o)
        .astype(bf_type)
        .reshape(row_count, kv_heads, group_size, head_size),
        (1, 2, 0, 3),
    )

    def delta_step(running, offset):
        probabilities, key_rows, value_rows = probs_of(offset)
        grad_weights = jnp.einsum(
            "kgqd,kjd->kgqj", grad_heads, value_rows, preferred_element_type=fl_type
        )
        return (running + jnp.sum(probabilities * grad_weights, axis=-1), None)

    delta, _ = lax.scan(delta_step, jnp.zeros(stat_shape, fl_type), offsets)

    def grad_step(running, offset):
        probabilities, key_rows, value_rows = probs_of(offset)
        grad_weights = jnp.einsum(
            "kgqd,kjd->kgqj", grad_heads, value_rows, preferred_element_type=fl_type
        )
        grad_scores = (probabilities * (grad_weights - delta[..., None])).astype(bf_type)
        running = (
            running
            + jnp.einsum("kgqj,kjd->kgqd", grad_scores, key_rows, preferred_element_type=fl_type)
            * inv_root
        )
        key_part = (
            jnp.einsum("kgqj,kgqd->kjd", grad_scores, queries, preferred_element_type=fl_type)
            * inv_root
        )
        value_part = jnp.einsum(
            "kgqj,kgqd->kjd",
            probabilities.astype(bf_type),
            grad_heads,
            preferred_element_type=fl_type,
        )
        return (running, (key_part, value_part))

    grad_qrot, (key_blocks, value_blocks) = lax.scan(
        grad_step, jnp.zeros((kv_heads, group_size, row_count, head_size), fl_type), offsets
    )
    both_grads = jnp.concatenate([key_blocks, value_blocks], axis=1).astype(bf_type)
    both_grads = jnp.transpose(both_grads, (0, 2, 1, 3)).reshape(C, row_count, 2 * kv_cols)
    both_sum = ctx_sum(6, C, both_grads)
    grad_krot = both_sum[:, :kv_cols].reshape(row_count, kv_heads, head_size)
    grad_values_low = both_sum[:, kv_cols:].astype(bf_type)
    grad_qrot = jnp.transpose(grad_qrot, (2, 0, 1, 3)).reshape(row_count, q_heads, head_size)
    grad_qraw, query_gain_terms = norm_back(
        q_raw, q_factor, query_gain, rotate(grad_qrot, cosine, -sine_tab)
    )
    grad_kraw, key_gain_terms = norm_back(
        k_raw, k_factor, key_gain, rotate(grad_krot, cosine, -sine_tab)
    )
    grad_raw = jnp.concatenate(
        [
            grad_qraw.astype(bf_type).reshape(row_count, -1),
            grad_kraw.astype(bf_type).reshape(row_count, -1),
            grad_values_low,
        ],
        axis=1,
    )
    raw_other = lax.dynamic_slice_in_dim(grad_raw, other_start, half_rows, 0)
    raw_own = lax.dynamic_slice_in_dim(grad_raw, row_start, half_rows, 0)
    norm_theirs = outer_cols(raw_other, full_qkv).astype(bf_type)
    norm_ours = lax.ppermute(norm_theirs, "tp", swap)
    grad_normed = outer_cols(raw_own, full_qkv) + norm_ours.astype(fl_type)
    grad_input_norm, attn_gain_terms = norm_back(own_inputs, own_factor, attn_gain, grad_normed)
    grad_input = grad_residual + grad_input_norm

    total_a, total_o = weight_grads(
        7, C, F, normed_low.T, grad_raw, heads_low.T, grad_attn
    )
    total_a = total_a.reshape(-1, proj_cols).astype(fl_type)
    grad_query = total_a[:, :q_cols]
    grad_key = total_a[:, q_cols : q_cols + kv_cols]
    grad_value = total_a[:, q_cols + kv_cols :]
    grad_output_w = total_o.reshape(w_output.shape).astype(fl_type)

    vector = jnp.concatenate(
        [
            jnp.sum(attn_gain_terms, axis=0),
            jnp.sum(ffn_gain_terms, axis=0),
            jnp.sum(query_gain_terms, axis=(0, 1)),
            jnp.sum(key_gain_terms, axis=(0, 1)),
            loss_part[None],
        ]
    )
    vector = jnp.pad(vector, (0, -vector.shape[0] % 1024)).reshape(-1, 128)
    router_rows = router_part.reshape(F, -1, 128)
    small = jnp.concatenate(
        [router_rows, jnp.broadcast_to(vector[None], (F,) + vector.shape)], axis=1
    )
    summed = small_sum(8, C, F, T, small)
    router_len = router_rows.shape[1]
    grad_router = summed[:router_len].reshape(w_router.shape)
    flat = summed[router_len:].reshape(-1)
    head_at = 2 * width
    loss_value = flat[head_at + 2 * head_size] / (count * width)
    return (
        output_f.astype(bf_type)[None],
        loss_value,
        grad_input[None],
        flat[:width],
        grad_query,
        grad_key,
        grad_value,
        grad_output_w,
        flat[head_at : head_at + head_size],
        flat[head_at + head_size : head_at + 2 * head_size],
        flat[width:head_at],
        grad_router,
        grad_expert_in[None],
        grad_expert_out[None],
    )


def solution(mesh):
    return jax.shard_map(
        local,
        mesh=mesh,
        in_specs=(
            P("fsdp", "ctx", None),
            P("fsdp", ("ctx", "tp"), None),
            P(),
            P("fsdp", ("ctx", "tp"), None),
            P(),
            P("fsdp", "tp"),
            P("fsdp", "tp"),
            P("fsdp", "tp"),
            P("tp", "fsdp"),
            P(),
            P(),
            P(),
            P("fsdp", None),
            P(("ctx", "fsdp", "tp"), None, None),
            P(("ctx", "fsdp", "tp"), None, None),
        ),
        out_specs=(
            P("fsdp", ("ctx", "tp"), None),
            P(),
            P("fsdp", ("ctx", "tp"), None),
            P(),
            P("fsdp", "tp"),
            P("fsdp", "tp"),
            P("fsdp", "tp"),
            P("tp", "fsdp"),
            P(),
            P(),
            P(),
            P("fsdp", None),
            P(("ctx", "fsdp", "tp"), None, None),
            P(("ctx", "fsdp", "tp"), None, None),
        ),
        check_vma=False,
    )
```

time: 2060 us -> 961 us (0.47)
  waiting for transfers between devices: 1170 us -> 14.5 us
  Pallas kernels: 0 us -> 623 us
  blocking collectives: 490 us -> 0 us
  local copies, waits for them, and re-layouts: 119 us -> 71 us
  matrix products: 177 us -> 150 us
    psum x2 -> x0, waiting for transfers between devices: 691 us -> none  [the longest x1 590 us: local(): lax.psum((grad_query_full, grad_key_full, grad_value_full, grad_w_output)...]
    pallas_call x0 -> x8, Pallas kernels: none -> 623 us  [the longest x2 179 us: dispatch(): pl.pallas_call(functools.partial(dispatch_body, C, F, T, tabbed), out_sha...]
    all_gather x5 -> x1, waiting for transfers between devices: 301 us -> 0.01 us  [local(): all_both = lax.all_gather(both, 'ctx', axis=1, tiled=True)]
    all_to_all x2 -> x0, blocking collectives: 287 us -> none  [the longest x1 145 us: local(): lax.all_to_all(send_grads, ('ctx', 'fsdp', 'tp'), split_axis=0, concat_ax...]
    all_gather x3 -> x0, blocking collectives: 159 us -> none  [the longest x1 142 us: local(): lax.all_gather(w_router, 'fsdp', axis=0, tiled=True)]
    all_to_all x2 -> x0, waiting for transfers between devices: 133 us -> none  [the longest x1 133 us: local(): lax.all_to_all(grad_rows, ('ctx', 'fsdp', 'tp'), split_axis=0, concat_axi...]
    gather x8 -> x0, local copies, waits for them, and re-layouts: 61.4 us -> none  [the longest x1 15.4 us: local(): jnp.concatenate([grad_y, zero_row], axis=0)[slot_owner]]
    psum x1 -> x0, blocking collectives: 43.5 us -> none  [local(): lax.psum((jnp.sum(attn_gain_terms, axis=0), jnp.sum(ffn_gain_terms, axis=...]
  transfers between devices with their start and end apart: 13 -> 4, of which waited for: 10 -> 3; matrix products, arithmetic and copies ran while one was open for 8% -> 6% of each run, Pallas kernels for 0% -> 0%
where the time goes in v1:
time: 961 us; the launch traced here: 954 us
  Pallas kernels  623 us (65%)
  matrix products  150 us (16%)
  other arithmetic  74.6 us (8%)
  local copies, waits for them, and re-layouts  71 us (7%)
  between operations  19.2 us (2%)
  waiting for transfers between devices  14.5 us (2%)
    pallas_call x2, Pallas kernels, dispatch(): pl.pallas_call(functools.partial(dispatch_body, C, F, T, tabbed), out_sha...  179 us
    pallas_call x2, Pallas kernels, combine(): pl.pallas_call(functools.partial(combine_body, C, F, T, tabbed), out_shap...  153 us
    pallas_call x1, Pallas kernels, weight_grads(): pl.pallas_call(functools.partial(grads_body, C, F), out_shape=(jax.ShapeD...  150 us
    pallas_call x1, Pallas kernels, gather_weights(): pl.pallas_call(functools.partial(gather_body, C, F), out_shape=(jax.Shape...  104 us
    dot_general x6, matrix products, outer_cols(): lax.dot_general(left, right, (((1,), (1,)), ((), ())), preferred_element_...  43.9 us
    unnamed x201, local copies, waits for them, and re-layouts  32.9 us
    dot_general x3, matrix products, inner_rows(): lax.dot_general(left, right, (((0,), (0,)), ((), ())), preferred_element_...  24 us
    pallas_call x1, Pallas kernels, small_sum(): pl.pallas_call(functools.partial(small_body, C, F, T), out_shape=jax.Shap...  21.3 us
  transfers between devices with their start and end apart: 4, of which 3 were waited for; matrix products, arithmetic and copies ran while one was open for 6% of the time, Pallas kernels for 0%

profile of v1, /device:TPU:25, one launch (start us, length us, event | category | flops | bytes accessed | tf_op | source)
XLA Modules:
  0.0 953.5 jit_solution(16917639680604907252)
XLA Ops:
  15.5 104.3 %shard_map.254 = (bf16[2048,2688]{1,0:T(8,128)(2,1)S(1)}, bf16[2048,2048]{1,0:T(8,128)(2,1)S(1)}, f32[4,128,128]{2,1,0:T(8,128)S(1)}) custom-call(bf16[512,2688]{1,0:T(8,128)(2,1)S(1)} %fusion.16.wa, bf16[2048,512]{1,0:T(8,128)(2,1)S(1)} %copy-done.6, f32[128,128]{1,0:T(8,128)S(1)} %convolution_select_fusion.tab), custom_call_target="tpu_custom_call" | custom-call | tf_op jit(solution)/shard_map/pallas_call | solution.py:241
  168.3 5.1 fusion
  173.4 5.1 select_reduce_fusion
  180.5 8.6 convolution_convert_fusion.4
  205.0 5.3 multiply_reduce_fusion.7
  213.6 93.3 %shard_map.255 = (bf16[8,4,48,2048]{3,2,1,0:T(8,128)(2,1)S(1)}, bf16[4,128,2048]{2,1,0:T(8,128)(2,1)}, f32[4,128,128]{2,1,0:T(8,128)S(1)}) custom-call(bf16[128,2048]{1,0:T(8,128)(2,1)S(1)} %multiply_convert_fusion.4.rows, bf16[4,8,48,128]{3,2,1,0:T(8,128)(2,1)S(1)} %fusion.51.select, f32[128,128]{1,0:T(8,128)S(1)} %pad.17.refs_0_), custom_call_target="tpu_custom_call" | custom-call | tf_op jit(solution)/shard_map/pallas_call | solution.py:371
  307.6 14.9 %fusion.9 = f32[1536,1536]{0,1:T(8,128)S(1)} fusion(bf16[1536,2048]{1,0:T(8,128)(2,1)S(1)} %bitcast.296, bf16[1,2048,1536]{2,1,0:T(8,128)(2,1)} %param.28), kind=kOutput, calls=%fused_computation.18 | convolution fusion | flops 9663676416 | bytes 22020096 | tf_op jit(solution)/shard_map/dot_general | solution.py:995
  330.4 7.1 convolution_convert_fusion
  337.8 73.7 %shard_map.256 = (bf16[4,8,48,2048]{3,2,1,0:T(8,128)(2,1)S(1)}, bf16[4,128,2048]{2,1,0:T(8,128)(2,1)S(1)}) custom-call(bf16[8,4,48,2048]{3,2,1,0:T(8,128)(2,1)S(1)} %bitcast.285, bf16[4,2,128,384]{3,2,1,0:T(8,128)(2,1)S(1)} %pad_maximum_fusion.5.weigh), custom_call_target="tpu_custom_call" | custom-call | tf_op jit(solution)/shard_map/pallas_call | solution.py:490
  415.0 85.4 %shard_map.257 = (bf16[8,4,48,2048]{3,2,1,0:T(8,128)(2,1)S(1)}, bf16[4,128,2048]{2,1,0:T(8,128)(2,1)S(1)}) custom-call(bf16[128,2048]{1,0:T(8,128)(2,1)S(1)} %multiply_convert_fusion.5.rows, bf16[4,8,48,256]{3,2,1,0:T(8,128)(2,1)S(1)} %pad_maximum_fusion.6.select), custom_call_target="tpu_custom_call" | custom-call | tf_op jit(solution)/shard_map/pallas_call | solution.py:371
  501.7 12.4 %multiply_convert_fusion.2 = (bf16[1536,768]{0,1:T(8,128)(2,1)S(1)}, bf16[1536,768]{0,1:T(8,128)(2,1)}) fusion(f32[1536,1536]{0,1:T(8,128)} %copy-done.23, bf16[1536,2048]{1,0:T(8,128)(2,1)S(1)} %bitcast.294, bf16[1,768,2048]{2,1,0:T(8,128)(2,1)S(1)} %copy-done), kind=kOutput, calls=%fused_computation.24 | convolution fusion | flops 4847173632 | bytes 23592960 | tf_op jit(solution)/shard_map/dot_general | solution.py:65
  514.0 14.8 %convolution_convert_fusion.1 = bf16[1536,2048]{1,0:T(8,128)(2,1)} fusion(bf16[1,2048,1536]{2,1,0:T(8,128)(2,1)} %param.28, bf16[1536,768]{0,1:T(8,128)(2,1)} %get-tuple-element.258, bf16[1536,768]{0,1:T(8,128)(2,1)S(1)} %get-tuple-element.257), kind=kOutput, calls=%fused_computation.15 | convolution fusion | flops 9676259328 | bytes 17301504 | tf_op jit(solution)/shard_map/dot_general | solution.py:65
  528.9 14.1 %convolution_bitcast_fusion = f32[1,2048,1536]{2,1,0:T(8,128)} fusion(bf16[1536,2048]{1,0:T(8,128)(2,1)S(1)} %bitcast.299, bf16[1536,768]{0,1:T(8,128)(2,1)} %get-tuple-element.258, bf16[1536,768]{0,1:T(8,128)(2,1)S(1)} %get-tuple-element.257), kind=kOutput, calls=%fused_computation.7 | convolution fusion | flops 9673113600 | bytes 23592960 | tf_op jit(solution)/shard_map/dot_general | solution.py:59
  548.2 79.2 %shard_map.258 = (bf16[4,8,48,2048]{3,2,1,0:T(8,128)(2,1)}, bf16[4,128,2048]{2,1,0:T(8,128)(2,1)S(1)}, f32[4,128,128]{2,1,0:T(8,128)S(1)}) custom-call(bf16[8,4,48,2048]{3,2,1,0:T(8,128)(2,1)S(1)} %bitcast.286, bf16[4,1,128,384]{3,2,1,0:T(8,128)(2,1)S(1)} %copy-done.7, f32[4,128,128]{2,1,0:T(8,128)S(1)} %pad.18.refs_0_), custom_call_target="tpu_custom_call" | custom-call | tf_op jit(solution)/shard_map/pallas_call | solution.py:490
  634.4 9.6 %convolution_bitcast_fusion.1 = f32[1,768,2048]{2,1,0:T(8,128)} fusion(bf16[1536,768]{0,1:T(8,128)(2,1)} %multiply_convert_fusion.3, bf16[1536,2048]{1,0:T(8,128)(2,1)} %bitcast.295), kind=kOutput, calls=%fused_computation.30 | convolution fusion | flops 4831838208 | bytes 14942208 | tf_op jit(solution)/shard_map/dot_general | solution.py:59
  647.8 6.1 fusion.29
  654.2 9.8 %fusion.33 = bf16[1,2,1024,128]{3,2,1,0:T(8,128)(2,1)S(1)} fusion(bf16[256,2,8,128]{3,2,1,0:T(8,128)(2,1)S(1)} %bitcast.316, f32[2,8,256]{2,1,0:T(8,128)S(1)} %copy-done.62, f32[2,8,256,1024]{3,2,1,0:T(8,128)} %copy-done.15, pred[256,1024]{1,0:T(8,128)(4,1)S(1)} %copy-done.30), kind=kOutput, calls=%fused_computation.74 | convolution fusion | flops 1094975488 | bytes 18628608 | tf_op jit(solution)/shard_map/while/body/eval_jaxpr/kgqj,kgqd->kjd/dot_general | solution.py:1089
  664.1 12.5 %multiply_reduce_fusion = (f32[2,8,256]{2,1,0:T(8,128)S(1)}, f32[2,8,256,1024]{3,2,1,0:T(8,128)}) fusion(f32[2,8,256]{2,1,0:T(8,128)S(1)} %copy-done.62, f32[2,8,256,1024]{3,2,1,0:T(8,128)} %copy-done.15, pred[256,1024]{1,0:T(8,128)(4,1)S(1)} %copy-done.30, bf16[4,1024,128]{2,1,0:T(8,128)(2,1)S(1)} %copy-done.50, bf16[256,2,8,128]{3,2,1,0:T(8,128)(2,1)S(1)} %bitcast.317), kind=kOutput, calls=%fused_computation.1 | convolution fusion | flops 1098903552 | bytes 35422208 | tf_op jit(solution)/shard_map/while/body/eval_jaxpr/kgqd,kjd->kgqj/dot_general | solution.py:1076
  676.5 12.8 %multiply_convert_fusion = bf16[2,8,256,1024]{3,2,1,0:T(8,128)(2,1)S(1)} fusion(f32[2,8,256,1024]{3,2,1,0:T(8,128)} %get-tuple-element.307, f32[2,8,256]{2,1,0:T(8,128)S(1)} %get-tuple-element.306, f32[2,8,256]{2,1,0:T(8,128)S(1)} %copy-done.62, f32[2,8,256,1024]{3,2,1,0:T(8,128)} %copy-done.15, pred[256,1024]{1,0:T(8,128)(4,1)S(1)} %copy-done.30), kind=kLoop, calls=%fused_computation | loop fusion | flops 29360128 | bytes 42237952 | tf_op jit(solution)/shard_map/while/body/eval_jaxpr/convert_element_type | solution.py:1079
  694.8 15.0 %shard_map.259 = f32[256,512]{1,0:T(8,128)S(1)} custom-call(bf16[4,256,512]{2,1,0:T(8,128)(2,1)S(1)} %reshape.448.x), custom_call_target="tpu_custom_call" | custom-call | tf_op jit(solution)/shard_map/pallas_call | solution.py:528
  712.1 6.3 convolution_multiply_fusion
  741.8 150.5 %shard_map.261 = (bf16[4,128,2560]{2,1,0:T(8,128)(2,1)}, bf16[4,512,512]{2,1,0:T(8,128)(2,1)}) custom-call(bf16[2048,256]{1,0:T(8,128)(2,1)} %fusion.68.xt, bf16[256,2560]{1,0:T(8,128)(2,1)} %copy-done.31, bf16[2048,256]{1,0:T(8,128)(2,1)} %bitcast.313, bf16[256,2048]{1,0:T(8,128)(2,1)} %copy-done.34), custom_call_target="tpu_custom_call" | custom-call | tf_op jit(solution)/shard_map/pallas_call | solution.py:813
  901.4 10.5 %collective-permute-done.2 = bf16[128,2048]{1,0:T(8,128)(2,1)S(1)} collective-permute-done((bf16[128,2048]{1,0:T(8,128)(2,1)S(1)}, bf16[128,2048]{1,0:T(8,128)(2,1)S(1)}, u32[]{:S(2)}, u32[]{:S(2)}) %collective-permute-start.2) | collective-permute-done | bytes 524320 | tf_op jit(solution)/shard_map/ppermute | solution.py:1123
  917.4 21.3 %shard_map.260 = f32[168,128]{1,0:T(8,128)S(1)} custom-call(f32[4,168,128]{2,1,0:T(8,128)S(1)} %pad_maximum_fusion.7.x), custom_call_target="tpu_custom_call" | custom-call | tf_op jit(solution)/shard_map/pallas_call | solution.py:589
  (342 shorter events, 156.6 us)
Async XLA Ops:
  7.2 323.2 %copy-start = (bf16[1,768,2048]{2,1,0:T(8,128)(2,1)S(1)}, bf16[1,768,2048]{2,1,0:T(8,128)(2,1)}, u32[]{:S(2)}) copy-start(bf16[1,768,2048]{2,1,0:T(8,128)(2,1)} %param.29) | copy-start | bytes 9437188
  7.2 161.1 %all-gather.2.cloned.1.call-start = ((), (), s32[]{:S(2)}) async-start(), calls=%async_computation | async-start | bytes 1310720 | tf_op jit(solution)/shard_map/all_gather | solution.py:916
  13.4 109.7 %copy-start.67 = (f32[256]{0:T(256)}, f32[256]{0:T(256)S(1)}, u32[]{:S(2)}) copy-start(f32[256]{0:T(256)S(1)} %add_rsqrt_fusion.2) | copy-start | bytes 3076
  13.4 109.7 %copy-start.21 = (bf16[1,256,2048]{1,2,0:T(8,128)(2,1)S(1)}, bf16[1,256,2048]{1,2,0:T(8,128)(2,1)}, u32[]{:S(2)}) copy-start(bf16[1,256,2048]{1,2,0:T(8,128)(2,1)} %copy.200) | copy-start | bytes 3145732
  13.5 109.7 %copy-start.63 = (f32[2048]{0:T(1024)S(1)}, f32[2048]{0:T(1024)}, u32[]{:S(2)}) copy-start(f32[2048]{0:T(1024)} %param.19) | copy-start | bytes 24580
  191.3 13.7 %collective-permute-start = (bf16[128,2048]{1,0:T(8,128)(2,1)}, bf16[128,2048]{1,0:T(8,128)(2,1)}, u32[]{:S(2)}, u32[]{:S(2)}) collective-permute-start(bf16[128,2048]{1,0:T(8,128)(2,1)} %convolution_convert_fusion.3), channel_id=1, source_target_pairs={{0,1},{1,0},{2,3},{3,2},{4,5},{5,4},{6,7},{7,6},{8,9},{9,8},{10,11... | collective-permute-start | bytes 1572872 | tf_op jit(solution)/shard_map/ppermute | solution.py:977
  337.8 74.3 %copy-start.20 = (f32[128,2048]{1,0:T(8,128)S(1)}, f32[128,2048]{1,0:T(8,128)}, u32[]{:S(2)}) copy-start(f32[128,2048]{1,0:T(8,128)} %copy-done.19) | copy-start | bytes 3145732
  337.8 74.3 %copy-start.52 = (bf16[1,128,2048]{2,1,0:T(8,128)(2,1)S(1)}, bf16[1,128,2048]{2,1,0:T(8,128)(2,1)}, u32[]{:S(2)}) copy-start(bf16[1,128,2048]{2,1,0:T(8,128)(2,1)} %param.16) | copy-start | bytes 1572868
  337.8 74.3 %copy-start.81 = (pred[128]{0:T(512)(128)(4,1)S(1)}, pred[128]{0:T(512)(128)(4,1)}, u32[]{:S(2)}) copy-start(pred[128]{0:T(512)(128)(4,1)} %dynamic-slice_compare_fusion) | copy-start | bytes 388
  414.9 114.0 %slice-start.8 = ((s8[6291456]{0:T(1024)(128)(4,1)}), s8[4194304]{0:T(1024)(128)(4,1)S(1)}, s32[]{:S(2)}) async-start(s8[6291456]{0:T(1024)(128)(4,1)} %bitcast.297), calls=%async_computation.9 | async-start | bytes 8388608
  501.7 27.2 %slice-start.9 = ((s8[6291456]{0:T(1024)(128)(4,1)}), s8[2097152]{0:T(1024)(128)(4,1)S(1)}, s32[]{:S(2)}) async-start(s8[6291456]{0:T(1024)(128)(4,1)} %bitcast.297), calls=%async_computation.10 | async-start | bytes 4194304
  548.2 80.8 %copy-start.48 = (f32[128,32]{1,0:T(8,128)S(1)}, f32[128,32]{1,0:T(8,128)}, u32[]{:S(2)}) copy-start(f32[128,32]{1,0:T(8,128)} %copy-done.47) | copy-start | bytes 49156
  548.2 81.0 %copy-start.60 = (f32[2048]{0:T(1024)S(1)}, f32[2048]{0:T(1024)}, u32[]{:S(2)}) copy-start(f32[2048]{0:T(1024)} %param.26) | copy-start | bytes 24580
  548.2 81.0 %copy-start.70 = (f32[128]{0:T(128)S(1)}, f32[128]{0:T(128)}, u32[]{:S(2)}) copy-start(f32[128]{0:T(128)} %copy-done.69) | copy-start | bytes 1540
  634.4 13.1 %collective-permute-start.1 = (bf16[128,2048]{1,0:T(8,128)(2,1)S(1)}, bf16[128,2048]{1,0:T(8,128)(2,1)S(1)}, u32[]{:S(2)}, u32[]{:S(2)}) collective-permute-start(bf16[128,2048]{1,0:T(8,128)(2,1)S(1)} %get-tuple-element.253), channel_id=1, source_target_pairs={{0,1},{1,0},{2,3},{3,2},{4,5},{5,4},{6,7},{7,6},{8,9},{9,8},{10,11... | collective-permute-start | bytes 1572872 | tf_op jit(solution)/shard_map/ppermute | solution.py:1052
  693.1 17.2 %copy-start.37 = (f32[256,64]{1,0:T(8,128)S(1)}, f32[256,64]{1,0:T(8,128)}, u32[]{:S(2)}) copy-start(f32[256,64]{1,0:T(8,128)} %copy-done.36) | copy-start | bytes 196612
  693.2 17.2 %copy-start.41 = (f32[256,64]{1,0:T(8,128)S(1)}, f32[256,64]{1,0:T(8,128)}, u32[]{:S(2)}) copy-start(f32[256,64]{1,0:T(8,128)} %get-tuple-element.294) | copy-start | bytes 196612
  693.3 17.2 %copy-start.39 = (f32[32,2,8,128]{3,2,1,0:T(8,128)S(1)}, f32[32,2,8,128]{3,2,1,0:T(8,128)}, u32[]{:S(2)}) copy-start(f32[32,2,8,128]{3,2,1,0:T(8,128)} %get-tuple-element.268) | copy-start | bytes 786436
  693.3 17.2 %copy-start.78 = (f32[128]{0:T(128)S(1)}, f32[128]{0:T(128)}, u32[]{:S(2)}) copy-start(f32[128]{0:T(128)} %param.25) | copy-start | bytes 1540
  892.3 19.6 %slice-start.5 = ((s8[11010048]{0:T(1024)(128)(4,1)}), s8[4194304]{0:T(1024)(128)(4,1)S(1)}, s32[]{:S(2)}) async-start(s8[11010048]{0:T(1024)(128)(4,1)} %bitcast.292), calls=%async_computation.6 | async-start | bytes 8388608
  894.9 17.0 %slice-start.6 = ((s8[11010048]{0:T(1024)(128)(4,1)}), s8[4194304]{0:T(1024)(128)(4,1)S(1)}, s32[]{:S(2)}) async-start(s8[11010048]{0:T(1024)(128)(4,1)} %bitcast.292), calls=%async_computation.7 | async-start | bytes 8388608
  898.5 13.4 %collective-permute-start.2 = (bf16[128,2048]{1,0:T(8,128)(2,1)S(1)}, bf16[128,2048]{1,0:T(8,128)(2,1)S(1)}, u32[]{:S(2)}, u32[]{:S(2)}) collective-permute-start(bf16[128,2048]{1,0:T(8,128)(2,1)S(1)} %fusion.17), channel_id=1, source_target_pairs={{0,1},{1,0},{2,3},{3,2},{4,5},{5,4},{6,7},{7,6},{8,9},{9,8},{10,11... | collective-permute-start | bytes 1572872 | tf_op jit(solution)/shard_map/ppermute | solution.py:1123
  911.9 30.0 %copy-start.79 = (f32[128]{0:T(128)S(1)}, f32[128]{0:T(128)}, u32[]{:S(2)}) copy-start(f32[128]{0:T(128)} %get-tuple-element.247) | copy-start | bytes 1540
  911.9 33.1 %copy-start.1 = (bf16[1,768,2048]{2,1,0:T(8,128)(2,1)S(1)}, bf16[1,768,2048]{2,1,0:T(8,128)(2,1)}, u32[]{:S(2)}) copy-start(bf16[1,768,2048]{2,1,0:T(8,128)(2,1)} %param.29) | copy-start | bytes 9437188
  (74 other events, 471.3 us)
Sparse Core Ops, SparseCore 0:
  137.7 18.0 all-gather.1

commit v2 on v1

--- a/solution.py
+++ b/solution.py
@@ -829,6 +829,418 @@
     )(xt, da, ht, dt)
 
 
+def tail_body(
+    C, F, T, KH,
+    grad_own, heads, normed, qrot, kv, keys_t, raw, lse, bias, cosf, sins, qgain, kgain, again,
+    own_in, resid_in, router, vec_in, fo, fall,
+    gin, outa, outo, small,
+    wbuf, dall, nall, hq, rq, dheads, draw, dk, dv, ksend, kgot, gains, nsend, ngot, nown,
+    sza, szo, rza, rzo, smx, zgot, mid, sgot,
+    wsem, xs, xr, as_, ar, hs, hr, ds_, dr, rs, rr, z_s, z_r, ts, tr, us, ur,
+):
+    c, f, t, me = slab_place(C, T)
+    S = C * T
+    R, QC = heads.shape
+    W = normed.shape[1]
+    PC = raw.shape[1]
+    L = kv.shape[1]
+    HS = qgain.shape[1]
+    QH = QC // HS
+    G = QH // KH
+    Rh = grad_own.shape[0]
+    KC = KH * HS
+    pa = rq.shape[2]
+    po = hq.shape[2]
+    rows_a, cols_o = outa.shape[1], outo.shape[2]
+    root = HS ** (-0.5)
+    core = lax.rem(c, 2)
+    sib = c + 1 - 2 * core
+    mate = lax.rem(c + 2, C)
+    mate_sib = lax.rem(sib + 2, C)
+    table = far_first(F)
+
+    def block(q):
+        value = jnp.int32(table[0][q])
+        for g in range(1, F):
+            value = jnp.where(f == g, table[g][q], value)
+        return value
+
+    blocks = [block(q) for q in range(F)]
+    columns = [(c, lax.rem(f + k, F), t) for k in range(1, F)]
+    greet(columns + [slab_device(lax.rem(me + j, S), f, T) for j in range(1, S)])
+    at_t = pl.ds(pl.multiple_of(t * Rh, Rh), Rh)
+    at_u = pl.ds(pl.multiple_of((1 - t) * Rh, Rh), Rh)
+    beside = (c, f, 1 - t)
+
+    load_o = pltpu.make_async_copy(fo, wbuf.at[:, pl.ds(0, W)], wsem.at[0])
+    load_o.start()
+
+    swap_d = remote(grad_own, dall.at[c, at_t], xs.at[0], xr.at[0], beside)
+    swap_d_in = remote(grad_own, dall.at[c, at_u], xs.at[0], xr.at[0], beside)
+    swap_n = remote(nsend, ngot, xs.at[1], xr.at[1], beside)
+
+    def spread(buf, n, i):
+        here = buf.at[mate] if i == 2 else buf.at[c]
+        there = (mate if i == 0 else sib, f, t)
+        return remote(here, here, as_.at[n, i], ar.at[n, i], there)
+
+    def spread_in(buf, n, i):
+        here = buf.at[(mate, sib, mate_sib)[i]]
+        return remote(here, here, as_.at[n, i], ar.at[n, i], (sib, f, t))
+
+    def spread_start(buf, n):
+        spread(buf, n, 0).start()
+        spread(buf, n, 1).start()
+
+    def spread_pass(buf, n):
+        spread_in(buf, n, 0).wait_recv()
+        spread(buf, n, 2).start()
+
+    def spread_end(buf, n):
+        spread_in(buf, n, 1).wait_recv()
+        spread_in(buf, n, 2).wait_recv()
+
+    def spread_sent(buf, n):
+        for i in range(3):
+            spread(buf, n, i).wait_send()
+
+    def chunk_copies(source, target, ss, sr):
+        out, come = [], []
+        for k in range(1, C):
+            p, o = lax.rem(c + k, C), lax.rem(c + C - k, C)
+            out.append(remote(source(p), target(c), ss.at[k], sr.at[k], (p, f, t)))
+            come.append(remote(source(o), target(o), ss.at[k], sr.at[k], (o, f, t)))
+        return out, come
+
+    def lane(p, n):
+        return pl.ds(pl.multiple_of(p * n, n), n)
+
+    heads_out, heads_come = chunk_copies(
+        lambda p: heads.at[:, lane(p, po)], lambda o: hq.at[o], hs, hr
+    )
+    kv_moves = [
+        chunk_copies(lambda p, g=g: ksend.at[g, p], lambda o, g=g: kgot.at[g, o], ds_.at[g], dr.at[g])
+        for g in range(KH)
+    ]
+    raw_out, raw_come = chunk_copies(
+        lambda p: draw.at[:, lane(p, pa)], lambda o: rq.at[o], rs, rr
+    )
+
+    swap_d.start()
+    for copy in heads_out:
+        copy.start()
+    dall[c, at_t] = grad_own[...]
+    nall[c] = normed[...]
+    spread_start(nall, 0)
+    hq[c] = heads[:, lane(c, po)]
+    swap_d_in.wait_recv()
+    spread_start(dall, 1)
+
+    load_o.wait()
+    step = min(512, QC)
+
+    def head_grads(i, carry):
+        at = lane(i, step)
+        dheads[:, at] = outer_cols(dall[c], wbuf[at, pl.ds(0, W)]).astype(BF)
+        return carry
+
+    lax.fori_loop(0, QC // step, head_grads, 0)
+    load_w = pltpu.make_async_copy(fall.at[:, pl.ds(0, PC)], wbuf, wsem.at[1])
+    load_w.start()
+
+    def unturn(values):
+        return values * cosf[...] - pltpu.roll(values, HS // 2, 1) * sins[...]
+
+    def norm_grads(values, gain_vec, upstream):
+        factor = lax.rsqrt(jnp.mean(values * values, axis=-1, keepdims=True) + EPS)
+        out, terms = norm_back(values, factor, gain_vec, upstream)
+        return out, jnp.sum(terms, axis=0, keepdims=True)
+
+    gains[...] = jnp.zeros_like(gains)
+    key_step = min(L, 512)
+    for g in range(KH):
+        dk[...] = jnp.zeros_like(dk)
+        dv[...] = jnp.zeros_like(dv)
+
+        def one_head(i, carry):
+            h = g * G + i
+            at = lane(h, HS)
+            q_head, o_grad = qrot[:, at], dheads[:, at]
+            product = o_grad.astype(FL) * heads[:, at].astype(FL)
+            delta = jnp.sum(product.T, axis=0, keepdims=True)
+            row = lse[pl.ds(h, 1), :]
+            q_grad = jnp.zeros((HS, R), FL)
+            for j in range(L // key_step):
+                ks = pl.ds(j * key_step, key_step)
+                scores = outer_cols(kv[g, ks, :], q_head) * root
+                probs = jnp.exp(scores + bias[ks, :] - row)
+                d_probs = outer_cols(kv[KH + g, ks, :], o_grad)
+                d_scores = (probs * (d_probs - delta)).astype(BF)
+                dv[ks, :] += jnp.dot(probs.astype(BF), o_grad, preferred_element_type=FL)
+                dk[ks, :] += jnp.dot(d_scores, q_head, preferred_element_type=FL)
+                q_grad += jnp.dot(keys_t[g, :, ks], d_scores, preferred_element_type=FL)
+            q_back, terms = norm_grads(raw[:, at], qgain[...], unturn(q_grad.T * root))
+            draw[:, at] = q_back.astype(BF)
+            gains[0:1, :] += terms
+            return carry
+
+        lax.fori_loop(0, G, one_head, 0)
+        for p in range(C):
+            at = pl.ds(p * R, R)
+            ksend[g, p, :, 0:HS] = (dk[at, :] * root).astype(BF)
+            ksend[g, p, :, HS : 2 * HS] = dv[at, :].astype(BF)
+        for copy in kv_moves[g][0]:
+            copy.start()
+        kgot[g, c] = ksend[g, c]
+        if g == 0:
+            spread_pass(nall, 0)
+            spread_pass(dall, 1)
+    if KH == 0:
+        spread_pass(nall, 0)
+
+    for copy in heads_come:
+        copy.wait_recv()
+    spread_end(dall, 1)
+
+    def piece_o(b):
+        return inner_rows(
+            hq[...].reshape(C * R, po), dall[:, :, lane(b, cols_o)].reshape(C * R, cols_o)
+        )
+
+    def piece_a(b):
+        return inner_rows(
+            nall[:, :, lane(b, rows_a)].reshape(C * R, rows_a), rq[...].reshape(C * R, pa)
+        )
+
+    pieces = ((piece_o, szo, rzo, outo), (piece_a, sza, rza, outa))
+    end = (f == 0) | (f == F - 1)
+
+    def z_out(n, q):
+        b = blocks[q]
+        _, send, got, _ = pieces[n]
+        return remote(send.at[b], got.at[b], z_s.at[n, q], z_r.at[n, b], (c, f + 1, t))
+
+    def z_down(n, q):
+        b = blocks[q]
+        slot = jnp.where(b == f - 1, F, b)
+        _, send, got, _ = pieces[n]
+        return remote(send.at[b], got.at[slot], z_s.at[n, q], z_r.at[n, slot], (c, f - 1, t))
+
+    def z_wait(n, slot):
+        _, send, got, _ = pieces[n]
+        remote(send.at[0], got.at[slot], z_s.at[n, 0], z_r.at[n, slot], (c, f, t)).wait_recv()
+
+    def z_send(n, q):
+        up = blocks[q] > f
+
+        @pl.when(up)
+        def _():
+            z_out(n, q).start()
+
+        @pl.when(jnp.logical_not(up))
+        def _():
+            z_down(n, q).start()
+
+    def z_first(n):
+        fn, send, _, _ = pieces[n]
+
+        @pl.when(end)
+        def _():
+            for q in range(F - 1):
+                send[blocks[q]] = fn(blocks[q]).astype(BF)
+                z_send(n, q)
+
+    def z_relay(n, q):
+        fn, send, got, _ = pieces[n]
+
+        @pl.when(jnp.logical_not(end))
+        def _():
+            b = blocks[q]
+            z_wait(n, b)
+            send[b] = (fn(b) + got[b].astype(FL)).astype(BF)
+            z_send(n, q)
+
+    def z_last(n):
+        fn, send, got, out = pieces[n]
+        send[f] = fn(f).astype(BF)
+
+        @pl.when(f > 0)
+        def _():
+            z_wait(n, f)
+            send[f] = (send[f].astype(FL) + got[f].astype(FL)).astype(BF)
+
+        @pl.when(f < F - 1)
+        def _():
+            z_wait(n, F)
+            out[c] = (send[f].astype(FL) + got[F].astype(FL)).astype(BF)
+
+        @pl.when(f == F - 1)
+        def _():
+            out[c] = send[f]
+
+    z_first(0)
+
+    for g in range(KH):
+        for copy in kv_moves[g][1]:
+            copy.wait_recv()
+        total = kgot[g, 0].astype(FL)
+        for p in range(1, C):
+            total += kgot[g, p].astype(FL)
+        k_cols = slice(QC + g * HS, QC + (g + 1) * HS)
+        k_back, terms = norm_grads(raw[:, k_cols], kgain[...], unturn(total[:, :HS]))
+        draw[:, k_cols] = k_back.astype(BF)
+        draw[:, QC + KC + g * HS : QC + KC + (g + 1) * HS] = total[:, HS:].astype(BF)
+        gains[1:2, :] += terms
+    for copy in raw_out:
+        copy.start()
+    rq[c] = draw[:, lane(c, pa)]
+    load_w.wait()
+    width_step = min(512, W)
+
+    def norm_theirs(i, carry):
+        at = lane(i, width_step)
+        nsend[:, at] = outer_cols(draw[at_u, :], wbuf[at, :]).astype(BF)
+        return carry
+
+    lax.fori_loop(0, W // width_step, norm_theirs, 0)
+    swap_n.start()
+
+    def norm_ours(i, carry):
+        at = lane(i, width_step)
+        nown[:, at] = outer_cols(draw[at_t, :], wbuf[at, :])
+        return carry
+
+    lax.fori_loop(0, W // width_step, norm_ours, 0)
+
+    spread_end(nall, 0)
+    for copy in raw_come:
+        copy.wait_recv()
+    z_first(1)
+    z_relay(0, 0)
+    z_relay(1, 0)
+
+    swap_n.wait_recv()
+    upstream = nown[...] + ngot[...].astype(FL)
+    values = own_in[...]
+    factor = lax.rsqrt(jnp.mean(values * values, axis=-1, keepdims=True) + EPS)
+    back, terms = norm_back(values, factor, again[...], upstream)
+    gin[...] = resid_in[...] + back
+    for b in range(F):
+        smx[b, 0 : router.shape[1]] = router[b]
+        at = router.shape[1]
+        smx[b, at : at + 8] = vec_in[...]
+        smx[b, at : at + 1] = jnp.sum(terms, axis=0, keepdims=True)
+        smx[b, at + 2 : at + 3, 0:HS] = gains[0:1, :]
+        smx[b, at + 2 : at + 3, HS : 2 * HS] = gains[1:2, :]
+
+    def t_copy(k):
+        return remote(smx.at[lax.rem(f + k, F)], zgot.at[f], ts.at[k], tr.at[k], columns[k - 1])
+
+    def t_arrival(k):
+        b = lax.rem(f + F - k, F)
+        return remote(smx.at[b], zgot.at[b], ts.at[k], tr.at[k], columns[k - 1])
+
+    for k in range(1, F):
+        t_copy(k).start()
+    zgot[f] = smx[f]
+    for q in range(1, F - 1):
+        z_relay(0, q)
+        z_relay(1, q)
+    for k in range(1, F):
+        t_arrival(k).wait_recv()
+    total = zgot[0]
+    for b in range(1, F):
+        total += zgot[b]
+    mid[...] = total
+    sgot[me] = total
+
+    def u_copy(j):
+        return remote(
+            mid, sgot.at[me], us.at[j], ur.at[j], slab_device(lax.rem(me + j, S), f, T)
+        )
+
+    def u_arrival(j):
+        e = lax.rem(me + S - j, S)
+        return remote(mid, sgot.at[e], us.at[j], ur.at[j], slab_device(e, f, T))
+
+    for j in range(1, S):
+        u_copy(j).start()
+    z_last(0)
+    spread_start(outo, 2)
+    z_last(1)
+    spread_start(outa, 3)
+    for j in range(1, S):
+        u_arrival(j).wait_recv()
+    total = sgot[0]
+    for e in range(1, S):
+        total += sgot[e]
+    small[...] = total
+    spread_pass(outo, 2)
+    spread_pass(outa, 3)
+    spread_end(outo, 2)
+    spread_end(outa, 3)
+
+    for buf, n in ((nall, 0), (dall, 1), (outo, 2), (outa, 3)):
+        spread_sent(buf, n)
+    swap_d.wait_send()
+    swap_n.wait_send()
+    for copy in heads_out + raw_out:
+        copy.wait_send()
+    for g in range(KH):
+        for copy in kv_moves[g][0]:
+            copy.wait_send()
+    for n in range(2):
+        for q in range(F - 1):
+            z_out(n, q).wait_send()
+    for k in range(1, F):
+        t_copy(k).wait_send()
+    for j in range(1, S):
+        u_copy(j).wait_send()
+
+
+def tail(identity, C, F, T, KH, args, D, po):
+    grad_own, heads, normed, qrot, kv, keys_t, raw, lse, bias = args[:9]
+    qgain = args[11]
+    router, fall = args[16], args[19]
+    R, QC = heads.shape
+    W = normed.shape[1]
+    PC = raw.shape[1]
+    L = kv.shape[1]
+    HS = qgain.shape[1]
+    Rh = grad_own.shape[0]
+    S = C * T
+    pa = PC // C
+    rows_a, cols_o = W // F, W // F
+    small_shape = (router.shape[1] + 8, W)
+    dma = pltpu.SemaphoreType.DMA
+    V = pltpu.VMEM
+    return pl.pallas_call(
+        functools.partial(tail_body, C, F, T, KH),
+        out_shape=(
+            jax.ShapeDtypeStruct((Rh, W), FL),
+            jax.ShapeDtypeStruct((C, rows_a, pa), BF),
+            jax.ShapeDtypeStruct((C, po, cols_o), BF),
+            jax.ShapeDtypeStruct(small_shape, FL),
+        ),
+        in_specs=[VMEM] * 18 + [ANY] * 2,
+        out_specs=[VMEM] * 4,
+        scratch_shapes=[
+            V((W, PC), BF), V((C, R, W), BF), V((C, R, W), BF), V((C, R, po), BF),
+            V((C, R, pa), BF), V((R, QC), BF), V((R, PC), BF), V((L, HS), FL), V((L, HS), FL),
+            V((KH, C, R, 2 * HS), BF), V((KH, C, R, 2 * HS), BF), V((8, HS), FL),
+            V((Rh, W), BF), V((Rh, W), BF), V((Rh, W), FL),
+            V((F, rows_a, pa), BF), V((F, po, cols_o), BF),
+            V((F + 1, rows_a, pa), BF), V((F + 1, po, cols_o), BF),
+            V((F,) + small_shape, FL), V((F,) + small_shape, FL), V(small_shape, FL),
+            V((S,) + small_shape, FL),
+            dma((2,)), dma((2,)), dma((2,)), dma((4, 3)), dma((4, 3)), dma((C,)), dma((C,)),
+            dma((KH, C)), dma((KH, C)), dma((C,)), dma((C,)),
+            dma((2, F)), dma((2, F + 1)), dma((F,)), dma((F,)), dma((S,)), dma((S,)),
+        ],
+        compiler_params=params(identity, 62),
+    )(*args)
+
+
 def split_low(values):
     high = lax.reduce_precision(values, 8, 7)
     return high.astype(BF), (values - high).astype(BF)
@@ -1049,123 +1461,158 @@
     grad_resid_norm, ffn_gain_terms = norm_back(residual, ffn_factor, ffn_gain, grad_ffn)
     grad_residual = grad_out + grad_resid_norm
     grad_own = grad_residual.astype(bf_type)
-    grad_other = lax.ppermute(grad_own, "tp", swap)
-    grad_attn = jnp.where(
-        t == 0,
-        jnp.concatenate([grad_own, grad_other], axis=0),
-        jnp.concatenate([grad_other, grad_own], axis=0),
-    )
-    grad_heads = jnp.transpose(
-        outer_cols(grad_attn, full_o)
-        .astype(bf_type)
-        .reshape(row_count, kv_heads, group_size, head_size),
-        (1, 2, 0, 3),
-    )
-
-    def delta_step(running, offset):
-        probabilities, key_rows, value_rows = probs_of(offset)
-        grad_weights = jnp.einsum(
-            "kgqd,kjd->kgqj", grad_heads, value_rows, preferred_element_type=fl_type
-        )
-        return (running + jnp.sum(probabilities * grad_weights, axis=-1), None)
-
-    delta, _ = lax.scan(delta_step, jnp.zeros(stat_shape, fl_type), offsets)
-
-    def grad_step(running, offset):
-        probabilities, key_rows, value_rows = probs_of(offset)
-        grad_weights = jnp.einsum(
-            "kgqd,kjd->kgqj", grad_heads, value_rows, preferred_element_type=fl_type
-        )
-        grad_scores = (probabilities * (grad_weights - delta[..., None])).astype(bf_type)
-        running = (
-            running
-            + jnp.einsum("kgqj,kjd->kgqd", grad_scores, key_rows, preferred_element_type=fl_type)
-            * inv_root
-        )
-        key_part = (
-            jnp.einsum("kgqj,kgqd->kjd", grad_scores, queries, preferred_element_type=fl_type)
-            * inv_root
-        )
-        value_part = jnp.einsum(
-            "kgqj,kgqd->kjd",
-            probabilities.astype(bf_type),
-            grad_heads,
-            preferred_element_type=fl_type,
-        )
-        return (running, (key_part, value_part))
-
-    grad_qrot, (key_blocks, value_blocks) = lax.scan(
-        grad_step, jnp.zeros((kv_heads, group_size, row_count, head_size), fl_type), offsets
-    )
-    both_grads = jnp.concatenate([key_blocks, value_blocks], axis=1).astype(bf_type)
-    both_grads = jnp.transpose(both_grads, (0, 2, 1, 3)).reshape(C, row_count, 2 * kv_cols)
-    both_sum = ctx_sum(6, C, both_grads)
-    grad_krot = both_sum[:, :kv_cols].reshape(row_count, kv_heads, head_size)
-    grad_values_low = both_sum[:, kv_cols:].astype(bf_type)
-    grad_qrot = jnp.transpose(grad_qrot, (2, 0, 1, 3)).reshape(row_count, q_heads, head_size)
-    grad_qraw, query_gain_terms = norm_back(
-        q_raw, q_factor, query_gain, rotate(grad_qrot, cosine, -sine_tab)
-    )
-    grad_kraw, key_gain_terms = norm_back(
-        k_raw, k_factor, key_gain, rotate(grad_krot, cosine, -sine_tab)
-    )
-    grad_raw = jnp.concatenate(
-        [
-            grad_qraw.astype(bf_type).reshape(row_count, -1),
-            grad_kraw.astype(bf_type).reshape(row_count, -1),
-            grad_values_low,
-        ],
-        axis=1,
-    )
-    raw_other = lax.dynamic_slice_in_dim(grad_raw, other_start, half_rows, 0)
-    raw_own = lax.dynamic_slice_in_dim(grad_raw, row_start, half_rows, 0)
-    norm_theirs = outer_cols(raw_other, full_qkv).astype(bf_type)
-    norm_ours = lax.ppermute(norm_theirs, "tp", swap)
-    grad_normed = outer_cols(raw_own, full_qkv) + norm_ours.astype(fl_type)
-    grad_input_norm, attn_gain_terms = norm_back(own_inputs, own_factor, attn_gain, grad_normed)
-    grad_input = grad_residual + grad_input_norm
-
-    total_a, total_o = weight_grads(
-        7, C, F, normed_low.T, grad_raw, heads_low.T, grad_attn
-    )
-    total_a = total_a.reshape(-1, proj_cols).astype(fl_type)
-    grad_query = total_a[:, :q_cols]
-    grad_key = total_a[:, q_cols : q_cols + kv_cols]
-    grad_value = total_a[:, q_cols + kv_cols :]
-    grad_output_w = total_o.reshape(w_output.shape).astype(fl_type)
-
-    vector = jnp.concatenate(
-        [
-            jnp.sum(attn_gain_terms, axis=0),
-            jnp.sum(ffn_gain_terms, axis=0),
-            jnp.sum(query_gain_terms, axis=(0, 1)),
-            jnp.sum(key_gain_terms, axis=(0, 1)),
-            loss_part[None],
-        ]
-    )
-    vector = jnp.pad(vector, (0, -vector.shape[0] % 1024)).reshape(-1, 128)
-    router_rows = router_part.reshape(F, -1, 128)
-    small = jnp.concatenate(
-        [router_rows, jnp.broadcast_to(vector[None], (F,) + vector.shape)], axis=1
-    )
-    summed = small_sum(8, C, F, T, small)
-    router_len = router_rows.shape[1]
-    grad_router = summed[:router_len].reshape(w_router.shape)
-    flat = summed[router_len:].reshape(-1)
-    head_at = 2 * width
-    loss_value = flat[head_at + 2 * head_size] / (count * width)
+    if C == 4 and T == 2:
+        cos_full = jnp.concatenate([cosine, cosine], axis=1)
+        sin_signed = jnp.concatenate([-sine_tab, sine_tab], axis=1)
+        key_pos = jnp.arange(total_len, dtype=jnp.int32)[:, None]
+        bias = jnp.where((key_pos <= positions[None, :]) & (key_pos < length), 0.0, MASKED)
+        vec_in = jnp.zeros((8, width), fl_type)
+        vec_in = vec_in.at[1].set(jnp.sum(ffn_gain_terms, axis=0))
+        vec_in = vec_in.at[2, 2 * head_size].set(loss_part)
+        router_rows = router_part.reshape(F, -1, width)
+        grad_input, total_a, total_o, summed = tail(
+            9, C, F, T, kv_heads,
+            (
+                grad_own, heads_low, normed_low, q_rot.reshape(row_count, q_cols), all_both,
+                jnp.swapaxes(all_keys, 1, 2), raw, log_total.reshape(q_heads, row_count), bias,
+                cos_full, sin_signed, query_gain[None], key_gain[None], attn_gain[None],
+                own_inputs, grad_residual, router_rows, vec_in, full_o, full_all,
+            ),
+            width, q_cols // C,
+        )
+        total_a = jnp.swapaxes(total_a, 0, 1).reshape(-1, proj_cols).astype(fl_type)
+        grad_query = total_a[:, :q_cols]
+        grad_key = total_a[:, q_cols : q_cols + kv_cols]
+        grad_value = total_a[:, q_cols + kv_cols :]
+        grad_output_w = total_o.reshape(w_output.shape).astype(fl_type)
+        router_len = router_rows.shape[1]
+        grad_router = summed[:router_len].reshape(w_router.shape)
+        sum_attn, sum_ffn = summed[router_len], summed[router_len + 1]
+        sum_query = summed[router_len + 2, :head_size]
+        sum_key = summed[router_len + 2, head_size : 2 * head_size]
+        loss_total = summed[router_len + 2, 2 * head_size]
+    else:
+        grad_other = lax.ppermute(grad_own, "tp", swap)
+        grad_attn = jnp.where(
+            t == 0,
+            jnp.concatenate([grad_own, grad_other], axis=0),
+            jnp.concatenate([grad_other, grad_own], axis=0),
+        )
+        grad_heads = jnp.transpose(
+            outer_cols(grad_attn, full_o)
+            .astype(bf_type)
+            .reshape(row_count, kv_heads, group_size, head_size),
+            (1, 2, 0, 3),
+        )
+
+        def delta_step(running, offset):
+            probabilities, key_rows, value_rows = probs_of(offset)
+            grad_weights = jnp.einsum(
+                "kgqd,kjd->kgqj", grad_heads, value_rows, preferred_element_type=fl_type
+            )
+            return (running + jnp.sum(probabilities * grad_weights, axis=-1), None)
+
+        delta, _ = lax.scan(delta_step, jnp.zeros(stat_shape, fl_type), offsets)
+
+        def grad_step(running, offset):
+            probabilities, key_rows, value_rows = probs_of(offset)
+            grad_weights = jnp.einsum(
+                "kgqd,kjd->kgqj", grad_heads, value_rows, preferred_element_type=fl_type
+            )
+            grad_scores = (probabilities * (grad_weights - delta[..., None])).astype(bf_type)
+            running = (
+                running
+                + jnp.einsum("kgqj,kjd->kgqd", grad_scores, key_rows, preferred_element_type=fl_type)
+                * inv_root
+            )
+            key_part = (
+                jnp.einsum("kgqj,kgqd->kjd", grad_scores, queries, preferred_element_type=fl_type)
+                * inv_root
+            )
+            value_part = jnp.einsum(
+                "kgqj,kgqd->kjd",
+                probabilities.astype(bf_type),
+                grad_heads,
+                preferred_element_type=fl_type,
+            )
+            return (running, (key_part, value_part))
+
+        grad_qrot, (key_blocks, value_blocks) = lax.scan(
+            grad_step, jnp.zeros((kv_heads, group_size, row_count, head_size), fl_type), offsets
+        )
+        both_grads = jnp.concatenate([key_blocks, value_blocks], axis=1).astype(bf_type)
+        both_grads = jnp.transpose(both_grads, (0, 2, 1, 3)).reshape(C, row_count, 2 * kv_cols)
+        both_sum = ctx_sum(6, C, both_grads)
+        grad_krot = both_sum[:, :kv_cols].reshape(row_count, kv_heads, head_size)
+        grad_values_low = both_sum[:, kv_cols:].astype(bf_type)
+        grad_qrot = jnp.transpose(grad_qrot, (2, 0, 1, 3)).reshape(row_count, q_heads, head_size)
+        grad_qraw, query_gain_terms = norm_back(
+            q_raw, q_factor, query_gain, rotate(grad_qrot, cosine, -sine_tab)
+        )
+        grad_kraw, key_gain_terms = norm_back(
+            k_raw, k_factor, key_gain, rotate(grad_krot, cosine, -sine_tab)
+        )
+        grad_raw = jnp.concatenate(
+            [
+                grad_qraw.astype(bf_type).reshape(row_count, -1),
+                grad_kraw.astype(bf_type).reshape(row_count, -1),
+                grad_values_low,
+            ],
+            axis=1,
+        )
+        raw_other = lax.dynamic_slice_in_dim(grad_raw, other_start, half_rows, 0)
+        raw_own = lax.dynamic_slice_in_dim(grad_raw, row_start, half_rows, 0)
+        norm_theirs = outer_cols(raw_other, full_qkv).astype(bf_type)
+        norm_ours = lax.ppermute(norm_theirs, "tp", swap)
+        grad_normed = outer_cols(raw_own, full_qkv) + norm_ours.astype(fl_type)
+        grad_input_norm, attn_gain_terms = norm_back(own_inputs, own_factor, attn_gain, grad_normed)
+        grad_input = grad_residual + grad_input_norm
+
+        total_a, total_o = weight_grads(
+            7, C, F, normed_low.T, grad_raw, heads_low.T, grad_attn
+        )
+        total_a = total_a.reshape(-1, proj_cols).astype(fl_type)
+        grad_query = total_a[:, :q_cols]
+        grad_key = total_a[:, q_cols : q_cols + kv_cols]
+        grad_value = total_a[:, q_cols + kv_cols :]
+        grad_output_w = total_o.reshape(w_output.shape).astype(fl_type)
+
+        vector = jnp.concatenate(
+            [
+                jnp.sum(attn_gain_terms, axis=0),
+                jnp.sum(ffn_gain_terms, axis=0),
+                jnp.sum(query_gain_terms, axis=(0, 1)),
+                jnp.sum(key_gain_terms, axis=(0, 1)),
+                loss_part[None],
+            ]
+        )
+        vector = jnp.pad(vector, (0, -vector.shape[0] % 1024)).reshape(-1, 128)
+        router_rows = router_part.reshape(F, -1, 128)
+        small = jnp.concatenate(
+            [router_rows, jnp.broadcast_to(vector[None], (F,) + vector.shape)], axis=1
+        )
+        summed = small_sum(8, C, F, T, small)
+        router_len = router_rows.shape[1]
+        grad_router = summed[:router_len].reshape(w_router.shape)
+        flat = summed[router_len:].reshape(-1)
+        head_at = 2 * width
+        sum_attn, sum_ffn = flat[:width], flat[width:head_at]
+        sum_query = flat[head_at : head_at + head_size]
+        sum_key = flat[head_at + head_size : head_at + 2 * head_size]
+        loss_total = flat[head_at + 2 * head_size]
+    loss_value = loss_total / (count * width)
     return (
         output_f.astype(bf_type)[None],
         loss_value,
         grad_input[None],
-        flat[:width],
+        sum_attn,
         grad_query,
         grad_key,
         grad_value,
         grad_output_w,
-        flat[head_at : head_at + head_size],
-        flat[head_at + head_size : head_at + 2 * head_size],
-        flat[width:head_at],
+        sum_query,
+        sum_key,
+        sum_ffn,
         grad_router,
         grad_expert_in[None],
         grad_expert_out[None],

time: 961 us -> 889 us (0.925)
  matrix products: 150 us -> 104 us
  other arithmetic: 74.6 us -> 47.5 us
  Pallas kernels: 623 us -> 637 us
  waiting for transfers between devices: 14.5 us -> 3.92 us
    dot_general x4 -> x0, matrix products: 32.4 us -> none  [the longest x1 12.5 us: grad_step(): jnp.einsum('kgqd,kjd->kgqj', grad_heads, value_rows, preferred_element_ty...]
    pallas_call x3 -> x1, Pallas kernels: 187 us -> 202 us  [tail(): pl.pallas_call(functools.partial(tail_body, C, F, T, KH), out_shape=(jax....]
    ppermute x2 -> x0, waiting for transfers between devices: 12.7 us -> none  [the longest x1 10.5 us: local(): norm_ours = lax.ppermute(norm_theirs, 'tp', swap)]
    dot_general x6 -> x3, matrix products: 43.9 us -> 32.9 us  [outer_cols(): lax.dot_general(left, right, (((1,), (1,)), ((), ())), preferred_element_...]
    unnamed x201 -> x99, local copies, waits for them, and re-layouts: 32.9 us -> 33.3 us
  transfers between devices with their start and end apart: 4 -> 2, of which waited for: 3 -> 1; matrix products, arithmetic and copies ran while one was open for 6% -> 3% of each run, Pallas kernels for 0% -> 0%
where the time goes in v2:
time: 889 us; the launch traced here: 883 us
  Pallas kernels  637 us (72%)
  matrix products  104 us (12%)
  local copies, waits for them, and re-layouts  70.4 us (8%)
  other arithmetic  47.5 us (5%)
  between operations  18.3 us (2%)
    pallas_call x1, Pallas kernels, tail(): pl.pallas_call(functools.partial(tail_body, C, F, T, KH), out_shape=(jax....  202 us
    pallas_call x2, Pallas kernels, dispatch(): pl.pallas_call(functools.partial(dispatch_body, C, F, T, tabbed), out_sha...  179 us
    pallas_call x2, Pallas kernels, combine(): pl.pallas_call(functools.partial(combine_body, C, F, T, tabbed), out_shap...  152 us
    pallas_call x1, Pallas kernels, gather_weights(): pl.pallas_call(functools.partial(gather_body, C, F), out_shape=(jax.Shape...  104 us
    unnamed x99, local copies, waits for them, and re-layouts  33.3 us
    dot_general x3, matrix products, outer_cols(): lax.dot_general(left, right, (((1,), (1,)), ((), ())), preferred_element_...  32.9 us
    dot_general x3, matrix products, inner_rows(): lax.dot_general(left, right, (((0,), (0,)), ((), ())), preferred_element_...  23.7 us
  transfers between devices with their start and end apart: 2, of which 1 were waited for; matrix products, arithmetic and copies ran while one was open for 3% of the time, Pallas kernels for 0%

profile of v2, /device:TPU:25, one launch (start us, length us, event | category | flops | bytes accessed | tf_op | source)
XLA Modules:
  0.0 882.6 jit_solution(14443532117922075702)
XLA Ops:
  15.4 104.3 %shard_map.254 = (bf16[2048,2688]{1,0:T(8,128)(2,1)S(1)}, bf16[2048,2048]{1,0:T(8,128)(2,1)S(1)}, f32[4,128,128]{2,1,0:T(8,128)S(1)}) custom-call(bf16[512,2688]{1,0:T(8,128)(2,1)S(1)} %fusion.13.wa, bf16[2048,512]{1,0:T(8,128)(2,1)S(1)} %copy-done.3, f32[128,128]{1,0:T(8,128)S(1)} %convolution_select_fusion.tab), custom_call_target="tpu_custom_call" | custom-call | tf_op jit(solution)/shard_map/pallas_call | solution.py:241
  119.8 3.3 copy-done
  123.1 2.9 fusion.1.raw
  158.2 4.6 fusion
  162.8 5.1 select_reduce_fusion
  168.0 5.9 fusion.18
  175.4 5.8 convolution_convert_fusion.2
  190.9 3.9 collective-permute-done
  194.8 5.2 multiply_reduce_fusion.5
  203.6 93.2 %shard_map.255 = (bf16[8,4,48,2048]{3,2,1,0:T(8,128)(2,1)S(1)}, bf16[4,128,2048]{2,1,0:T(8,128)(2,1)}, f32[4,128,128]{2,1,0:T(8,128)S(1)}) custom-call(bf16[128,2048]{1,0:T(8,128)(2,1)S(1)} %multiply_convert_fusion.3.rows, bf16[4,8,48,128]{3,2,1,0:T(8,128)(2,1)S(1)} %fusion.28.select, f32[128,128]{1,0:T(8,128)S(1)} %pad.20.refs_0_), custom_call_target="tpu_custom_call" | custom-call | tf_op jit(solution)/shard_map/pallas_call | solution.py:371
  301.3 14.7 %fusion.6 = f32[1536,1536]{0,1:T(8,128)S(1)} fusion(bf16[1536,2048]{1,0:T(8,128)(2,1)} %bitcast.155, bf16[1,2048,1536]{2,1,0:T(8,128)(2,1)} %param.32), kind=kOutput, calls=%fused_computation.13 | convolution fusion | flops 9663676416 | bytes 22020096 | tf_op jit(solution)/shard_map/dot_general | solution.py:1407
  320.7 5.4 convolution_convert_fusion
  326.1 73.4 %shard_map.256 = (bf16[4,8,48,2048]{3,2,1,0:T(8,128)(2,1)S(1)}, bf16[4,128,2048]{2,1,0:T(8,128)(2,1)S(1)}) custom-call(bf16[8,4,48,2048]{3,2,1,0:T(8,128)(2,1)S(1)} %bitcast.150, bf16[4,2,128,384]{3,2,1,0:T(8,128)(2,1)S(1)} %pad_maximum_fusion.4.weigh), custom_call_target="tpu_custom_call" | custom-call | tf_op jit(solution)/shard_map/pallas_call | solution.py:490
  401.9 85.7 %shard_map.257 = (bf16[8,4,48,2048]{3,2,1,0:T(8,128)(2,1)S(1)}, bf16[4,128,2048]{2,1,0:T(8,128)(2,1)S(1)}) custom-call(bf16[128,2048]{1,0:T(8,128)(2,1)S(1)} %multiply_convert_fusion.4.rows, bf16[4,8,48,256]{3,2,1,0:T(8,128)(2,1)S(1)} %pad_maximum_fusion.5.select), custom_call_target="tpu_custom_call" | custom-call | tf_op jit(solution)/shard_map/pallas_call | solution.py:371
  490.2 14.4 %multiply_convert_fusion.1 = (bf16[1536,768]{0,1:T(8,128)(2,1)}, bf16[1536,768]{0,1:T(8,128)(2,1)}) fusion(f32[1536,1536]{0,1:T(8,128)} %copy-done.9, bf16[1536,2048]{1,0:T(8,128)(2,1)} %bitcast.159, bf16[1,768,2048]{2,1,0:T(8,128)(2,1)} %param.33), kind=kOutput, calls=%fused_computation.20 | convolution fusion | flops 4847173632 | bytes 23592960 | tf_op jit(solution)/shard_map/dot_general | solution.py:65
  504.6 6.9 convolution_bitcast_fusion.1
  511.5 15.5 %convolution_bitcast_fusion = f32[1,2048,1536]{2,1,0:T(8,128)} fusion(bf16[1536,2048]{1,0:T(8,128)(2,1)S(1)} %bitcast.158, bf16[1536,768]{0,1:T(8,128)(2,1)} %get-tuple-element.217, bf16[1536,768]{0,1:T(8,128)(2,1)} %get-tuple-element.216), kind=kOutput, calls=%fused_computation.7 | convolution fusion | flops 9673113600 | bytes 23592960 | tf_op jit(solution)/shard_map/dot_general | solution.py:59
  527.0 15.7 %convolution_convert_fusion.1 = bf16[1536,2048]{1,0:T(8,128)(2,1)} fusion(bf16[1,2048,1536]{2,1,0:T(8,128)(2,1)} %param.32, bf16[1536,768]{0,1:T(8,128)(2,1)} %get-tuple-element.217, bf16[1536,768]{0,1:T(8,128)(2,1)} %get-tuple-element.216), kind=kOutput, calls=%fused_computation.11 | convolution fusion | flops 9676259328 | bytes 17301504 | tf_op jit(solution)/shard_map/dot_general | solution.py:65
  547.9 78.6 %shard_map.258 = (bf16[4,8,48,2048]{3,2,1,0:T(8,128)(2,1)}, bf16[4,128,2048]{2,1,0:T(8,128)(2,1)S(1)}, f32[4,128,128]{2,1,0:T(8,128)S(1)}) custom-call(bf16[8,4,48,2048]{3,2,1,0:T(8,128)(2,1)S(1)} %bitcast.151, bf16[4,1,128,384]{3,2,1,0:T(8,128)(2,1)S(1)} %get-tuple-element.214.weigh, f32[4,128,128]{2,1,0:T(8,128)S(1)} %pad.21.refs_0_), custom_call_target="tpu_custom_call" | custom-call | tf_op jit(solution)/shard_map/pallas_call | solution.py:490
  639.0 201.7 %shard_map.259 = (f32[128,2048]{1,0:T(8,128)}, bf16[4,512,640]{2,1,0:T(8,128)(2,1)}, bf16[4,512,512]{2,1,0:T(8,128)(2,1)}, f32[16,2048]{1,0:T(8,128)}) custom-call(bf16[128,2048]{1,0:T(8,128)(2,1)} %get-tuple-element.212.grad_own, bf16[256,2048]{1,0:T(8,128)(2,1)} %copy-done.8, bf16[256,2048]{1,0:T(8,128)(2,1)} %copy-done.13, bf16[256,2048]{1,0:T(8,128)(2,1)} %bitcast.164, ...), custom_call_target="tpu_custom_call" | custom-call | tf_op jit(solution)/shard_map/pallas_call | solution.py:1217
  845.4 4.4 convert_bitcast_fusion
  849.8 6.0 copy.180
  857.1 4.7 slice.155
  865.4 5.4 copy.181
  (198 shorter events, 97.8 us)
Async XLA Ops:
  7.2 8.3 copy-start.3
  7.2 151.0 %all-gather.2.cloned.1.call-start = ((), (), s32[]{:S(2)}) async-start(), calls=%async_computation | async-start | bytes 1310720 | tf_op jit(solution)/shard_map/all_gather | solution.py:1328
  13.2 110.0 %copy-start.13 = (bf16[256,2048]{1,0:T(8,128)(2,1)}, bf16[256,2048]{1,0:T(8,128)(2,1)S(1)}, u32[]{:S(2)}) copy-start(bf16[256,2048]{1,0:T(8,128)(2,1)S(1)} %fusion.17.normed) | copy-start | bytes 3145732
  123.1 9.5 %copy-start.36 = (f32[128]{0:T(128)S(1)}, f32[128]{0:T(128)}, u32[]{:S(2)}) copy-start(f32[128]{0:T(128)} %param.29) | copy-start | bytes 1540
  127.3 12.9 %copy-start.7 = (f32[256,2560]{1,0:T(8,128)}, f32[256,2560]{1,0:T(8,128)S(1)}, u32[]{:S(2)}) copy-start(f32[256,2560]{1,0:T(8,128)S(1)} %fusion.1.raw) | copy-start | bytes 7864324
  129.3 17.5 %copy-start.19 = (f32[256,64]{1,0:T(8,128)}, f32[256,64]{1,0:T(8,128)S(1)}, u32[]{:S(2)}) copy-start(f32[256,64]{1,0:T(8,128)S(1)} %get-tuple-element.235) | copy-start | bytes 196612
  132.6 7.6 copy-start.41
  175.3 19.5 %copy-start.8 = (bf16[256,2048]{1,0:T(8,128)(2,1)}, bf16[256,2048]{1,0:T(8,128)(2,1)S(1)}, u32[]{:S(2)}) copy-start(bf16[256,2048]{1,0:T(8,128)(2,1)S(1)} %copy.192.heads) | copy-start | bytes 3145732
  175.3 7.7 copy-start.42
  175.4 9.0 %copy-start.11 = (bf16[256,16,128]{2,1,0:T(8,128)(2,1)S(1)}, bf16[256,16,128]{2,1,0:T(8,128)(2,1)}, u32[]{:S(2)}) copy-start(bf16[256,16,128]{2,1,0:T(8,128)(2,1)} %pad_maximum_fusion.3) | copy-start | bytes 3145732
  181.2 13.6 %collective-permute-start = (bf16[128,2048]{1,0:T(8,128)(2,1)}, bf16[128,2048]{1,0:T(8,128)(2,1)S(1)}, u32[]{:S(2)}, u32[]{:S(2)}) collective-permute-start(bf16[128,2048]{1,0:T(8,128)(2,1)} %convolution_convert_fusion.2), channel_id=1, source_target_pairs={{0,1},{1,0},{2,3},{3,2},{4,5},{5,4},{6,7},{7,6},{8,9},{9,8},{10,11... | collective-permute-start | bytes 1572872 | tf_op jit(solution)/shard_map/ppermute | solution.py:1389
  190.9 10.1 %copy-start.30 = (f32[2048]{0:T(1024)S(1)}, f32[2048]{0:T(1024)}, u32[]{:S(2)}) copy-start(f32[2048]{0:T(1024)} %param.30) | copy-start | bytes 24580
  190.9 10.3 %copy-start.28 = (pred[128,128]{1,0:T(8,128)(4,1)S(1)}, pred[128,128]{1,0:T(8,128)(4,1)}, u32[]{:S(2)}) copy-start(pred[128,128]{1,0:T(8,128)(4,1)} %copy-done.27) | copy-start | bytes 49156
  326.1 73.9 %copy-start.24 = (bf16[1,128,2048]{2,1,0:T(8,128)(2,1)S(1)}, bf16[1,128,2048]{2,1,0:T(8,128)(2,1)}, u32[]{:S(2)}) copy-start(bf16[1,128,2048]{2,1,0:T(8,128)(2,1)} %param.20) | copy-start | bytes 1572868
  326.1 73.9 %copy-start.38 = (pred[128]{0:T(512)(128)(4,1)S(1)}, pred[128]{0:T(512)(128)(4,1)}, u32[]{:S(2)}) copy-start(pred[128]{0:T(512)(128)(4,1)} %dynamic-slice_compare_fusion) | copy-start | bytes 388
  401.8 109.7 %slice-start = ((s8[6291456]{0:T(1024)(128)(4,1)}), s8[4194304]{0:T(1024)(128)(4,1)S(1)}, s32[]{:S(2)}) async-start(s8[6291456]{0:T(1024)(128)(4,1)} %bitcast.156), calls=%async_computation.1 | async-start | bytes 8388608
  490.2 14.4 %copy-start.6 = (bf16[8,4,48,2048]{3,2,1,0:T(8,128)(2,1)S(1)}, bf16[8,4,48,2048]{3,2,1,0:T(8,128)(2,1)}, u32[]{:S(2)}) copy-start(bf16[8,4,48,2048]{3,2,1,0:T(8,128)(2,1)} %copy-done.5) | copy-start | bytes 18874372
  490.2 14.4 %copy-start.17 = (bf16[1536,768]{0,1:T(8,128)(2,1)S(1)}, bf16[1536,768]{0,1:T(8,128)(2,1)}, u32[]{:S(2)}) copy-start(bf16[1536,768]{0,1:T(8,128)(2,1)} %copy-done.16) | copy-start | bytes 7077892
  490.2 21.3 %slice-start.1 = ((s8[6291456]{0:T(1024)(128)(4,1)}), s8[2097152]{0:T(1024)(128)(4,1)S(1)}, s32[]{:S(2)}) async-start(s8[6291456]{0:T(1024)(128)(4,1)} %bitcast.156), calls=%async_computation.2 | async-start | bytes 4194304
  547.9 80.2 %copy-start.21 = (f32[128,32]{1,0:T(8,128)S(1)}, f32[128,32]{1,0:T(8,128)}, u32[]{:S(2)}) copy-start(f32[128,32]{1,0:T(8,128)} %copy-done.20) | copy-start | bytes 49156
  547.9 81.7 %copy-start.31 = (f32[2048]{0:T(1024)S(1)}, f32[2048]{0:T(1024)}, u32[]{:S(2)}) copy-start(f32[2048]{0:T(1024)} %param.30) | copy-start | bytes 24580
  547.9 81.7 %copy-start.35 = (f32[128]{0:T(128)S(1)}, f32[128]{0:T(128)}, u32[]{:S(2)}) copy-start(f32[128]{0:T(128)} %copy-done.34) | copy-start | bytes 1540
  626.5 8.4 copy-start.39
  865.4 8.1 copy-start.22
  (23 other events, 85.8 us)
Sparse Core Ops, SparseCore 0:
  135.4 18.1 all-gather.1

commit v3 on v2

--- a/solution.py
+++ b/solution.py
@@ -851,7 +851,7 @@
     KC = KH * HS
     pa = rq.shape[2]
     po = hq.shape[2]
-    rows_a, cols_o = outa.shape[1], outo.shape[2]
+    rows_a, cols_o = outa.shape[0], outo.shape[1]
     root = HS ** (-0.5)
     core = lax.rem(c, 2)
     sib = c + 1 - 2 * core
@@ -879,30 +879,30 @@
     swap_d_in = remote(grad_own, dall.at[c, at_u], xs.at[0], xr.at[0], beside)
     swap_n = remote(nsend, ngot, xs.at[1], xr.at[1], beside)
 
-    def spread(buf, n, i):
-        here = buf.at[mate] if i == 2 else buf.at[c]
+    def spread(view, n, i):
+        here = view(mate) if i == 2 else view(c)
         there = (mate if i == 0 else sib, f, t)
         return remote(here, here, as_.at[n, i], ar.at[n, i], there)
 
-    def spread_in(buf, n, i):
-        here = buf.at[(mate, sib, mate_sib)[i]]
+    def spread_in(view, n, i):
+        here = view((mate, sib, mate_sib)[i])
         return remote(here, here, as_.at[n, i], ar.at[n, i], (sib, f, t))
 
-    def spread_start(buf, n):
-        spread(buf, n, 0).start()
-        spread(buf, n, 1).start()
-
-    def spread_pass(buf, n):
-        spread_in(buf, n, 0).wait_recv()
-        spread(buf, n, 2).start()
-
-    def spread_end(buf, n):
-        spread_in(buf, n, 1).wait_recv()
-        spread_in(buf, n, 2).wait_recv()
-
-    def spread_sent(buf, n):
+    def spread_start(view, n):
+        spread(view, n, 0).start()
+        spread(view, n, 1).start()
+
+    def spread_pass(view, n):
+        spread_in(view, n, 0).wait_recv()
+        spread(view, n, 2).start()
+
+    def spread_end(view, n):
+        spread_in(view, n, 1).wait_recv()
+        spread_in(view, n, 2).wait_recv()
+
+    def spread_sent(view, n):
         for i in range(3):
-            spread(buf, n, i).wait_send()
+            spread(view, n, i).wait_send()
 
     def chunk_copies(source, target, ss, sr):
         out, come = [], []
@@ -922,19 +922,28 @@
         chunk_copies(lambda p, g=g: ksend.at[g, p], lambda o, g=g: kgot.at[g, o], ds_.at[g], dr.at[g])
         for g in range(KH)
     ]
-    raw_out, raw_come = chunk_copies(
-        lambda p: draw.at[:, lane(p, pa)], lambda o: rq.at[o], rs, rr
-    )
+    def nall_of(p):
+        return nall.at[p]
+
+    def outo_of(p):
+        return outo.at[lane(p, po)]
+
+    def outa_of(p):
+        return outa.at[:, lane(p, pa)]
+
+    dall_of = [
+        lambda p, q=q: dall.at[p, :, lane(blocks[q], cols_o)] for q in range(F)
+    ]
 
     swap_d.start()
     for copy in heads_out:
         copy.start()
     dall[c, at_t] = grad_own[...]
     nall[c] = normed[...]
-    spread_start(nall, 0)
     hq[c] = heads[:, lane(c, po)]
     swap_d_in.wait_recv()
-    spread_start(dall, 1)
+    for q in range(F):
+        spread_start(dall_of[q], 3 + q)
 
     load_o.wait()
     step = min(512, QC)
@@ -957,51 +966,6 @@
         return out, jnp.sum(terms, axis=0, keepdims=True)
 
     gains[...] = jnp.zeros_like(gains)
-    key_step = min(L, 512)
-    for g in range(KH):
-        dk[...] = jnp.zeros_like(dk)
-        dv[...] = jnp.zeros_like(dv)
-
-        def one_head(i, carry):
-            h = g * G + i
-            at = lane(h, HS)
-            q_head, o_grad = qrot[:, at], dheads[:, at]
-            product = o_grad.astype(FL) * heads[:, at].astype(FL)
-            delta = jnp.sum(product.T, axis=0, keepdims=True)
-            row = lse[pl.ds(h, 1), :]
-            q_grad = jnp.zeros((HS, R), FL)
-            for j in range(L // key_step):
-                ks = pl.ds(j * key_step, key_step)
-                scores = outer_cols(kv[g, ks, :], q_head) * root
-                probs = jnp.exp(scores + bias[ks, :] - row)
-                d_probs = outer_cols(kv[KH + g, ks, :], o_grad)
-                d_scores = (probs * (d_probs - delta)).astype(BF)
-                dv[ks, :] += jnp.dot(probs.astype(BF), o_grad, preferred_element_type=FL)
-                dk[ks, :] += jnp.dot(d_scores, q_head, preferred_element_type=FL)
-                q_grad += jnp.dot(keys_t[g, :, ks], d_scores, preferred_element_type=FL)
-            q_back, terms = norm_grads(raw[:, at], qgain[...], unturn(q_grad.T * root))
-            draw[:, at] = q_back.astype(BF)
-            gains[0:1, :] += terms
-            return carry
-
-        lax.fori_loop(0, G, one_head, 0)
-        for p in range(C):
-            at = pl.ds(p * R, R)
-            ksend[g, p, :, 0:HS] = (dk[at, :] * root).astype(BF)
-            ksend[g, p, :, HS : 2 * HS] = dv[at, :].astype(BF)
-        for copy in kv_moves[g][0]:
-            copy.start()
-        kgot[g, c] = ksend[g, c]
-        if g == 0:
-            spread_pass(nall, 0)
-            spread_pass(dall, 1)
-    if KH == 0:
-        spread_pass(nall, 0)
-
-    for copy in heads_come:
-        copy.wait_recv()
-    spread_end(dall, 1)
-
     def piece_o(b):
         return inner_rows(
             hq[...].reshape(C * R, po), dall[:, :, lane(b, cols_o)].reshape(C * R, cols_o)
@@ -1012,7 +976,7 @@
             nall[:, :, lane(b, rows_a)].reshape(C * R, rows_a), rq[...].reshape(C * R, pa)
         )
 
-    pieces = ((piece_o, szo, rzo, outo), (piece_a, sza, rza, outa))
+    pieces = ((piece_o, szo, rzo, outo_of), (piece_a, sza, rza, outa_of))
     end = (f == 0) | (f == F - 1)
 
     def z_out(n, q):
@@ -1041,14 +1005,18 @@
         def _():
             z_down(n, q).start()
 
-    def z_first(n):
+    def z_first(n, q):
         fn, send, _, _ = pieces[n]
 
         @pl.when(end)
         def _():
-            for q in range(F - 1):
-                send[blocks[q]] = fn(blocks[q]).astype(BF)
-                z_send(n, q)
+            send[blocks[q]] = fn(blocks[q]).astype(BF)
+            z_send(n, q)
+
+    def o_first(q):
+        spread_end(dall_of[q], 3 + q)
+        if q < F - 1:
+            z_first(0, q)
 
     def z_relay(n, q):
         fn, send, got, _ = pieces[n]
@@ -1072,13 +1040,98 @@
         @pl.when(f < F - 1)
         def _():
             z_wait(n, F)
-            out[c] = (send[f].astype(FL) + got[F].astype(FL)).astype(BF)
+            out(c)[...] = (send[f].astype(FL) + got[F].astype(FL)).astype(BF)
 
         @pl.when(f == F - 1)
         def _():
-            out[c] = send[f]
-
-    z_first(0)
+            out(c)[...] = send[f]
+
+
+    key_step = min(L, 512)
+
+    def one_head(g, h):
+        at = lane(h, HS)
+        q_head, o_grad = qrot[:, at], dheads[:, at]
+        product = o_grad.astype(FL) * heads[:, at].astype(FL)
+        delta = jnp.sum(product.T, axis=0, keepdims=True)
+        row = lse[pl.ds(h, 1), :]
+        q_grad = jnp.zeros((HS, R), FL)
+        for j in range(L // key_step):
+            ks = pl.ds(j * key_step, key_step)
+            scores = outer_cols(kv[g, ks, :], q_head) * root
+            probs = jnp.exp(scores + bias[ks, :] - row)
+            d_probs = outer_cols(kv[KH + g, ks, :], o_grad)
+            d_scores = (probs * (d_probs - delta)).astype(BF)
+            dv[ks, :] += jnp.dot(probs.astype(BF), o_grad, preferred_element_type=FL)
+            dk[ks, :] += jnp.dot(d_scores, q_head, preferred_element_type=FL)
+            q_grad += jnp.dot(keys_t[g, :, ks], d_scores, preferred_element_type=FL)
+        q_back, terms = norm_grads(raw[:, at], qgain[...], unturn(q_grad.T * root))
+        draw[:, at] = q_back.astype(BF)
+        gains[0:1, :] += terms
+
+    def some_heads(g, first, count):
+        def step_(i, carry):
+            one_head(g, first + i)
+            return carry
+
+        lax.fori_loop(0, count, step_, 0)
+
+    raw_due = [-(-min((p + 1) * pa, QC) // HS) for p in range(C)]
+    raw_gone = []
+
+    def raw_sends(done):
+        for p in range(C):
+            if p not in raw_gone and raw_due[p] <= done and (p + 1) * pa <= QC:
+                raw_gone.append(p)
+                raw_send(p)
+
+    def raw_copy(p):
+        return remote(draw.at[:, p * pa : (p + 1) * pa], rq.at[c], rs.at[p], rr.at[c], (p, f, t))
+
+    def raw_come(o):
+        return remote(draw.at[:, 0:pa], rq.at[o], rs.at[0], rr.at[o], (o, f, t))
+
+    def raw_send(p):
+        @pl.when(c != p)
+        def _():
+            raw_copy(p).start()
+
+        @pl.when(c == p)
+        def _():
+            rq[c] = draw[:, p * pa : (p + 1) * pa]
+
+    halves = 2
+    part_heads = G // halves
+    beat = 0
+    for g in range(KH):
+        dk[...] = jnp.zeros_like(dk)
+        dv[...] = jnp.zeros_like(dv)
+        for half in range(halves):
+            some_heads(g, g * G + half * part_heads, part_heads)
+            raw_sends(g * G + (half + 1) * part_heads)
+            if half == halves - 1:
+                for p in range(C):
+                    at = pl.ds(p * R, R)
+                    ksend[g, p, :, 0:HS] = (dk[at, :] * root).astype(BF)
+                    ksend[g, p, :, HS : 2 * HS] = dv[at, :].astype(BF)
+                for copy in kv_moves[g][0]:
+                    copy.start()
+                kgot[g, c] = ksend[g, c]
+            if beat < F:
+                spread_pass(dall_of[beat], 3 + beat)
+            if beat == 0:
+                for copy in heads_come:
+                    copy.wait_recv()
+            elif beat < F:
+                o_first(beat - 1)
+            beat += 1
+    for q in range(beat, F):
+        spread_pass(dall_of[q], 3 + q)
+        o_first(q - 1)
+    spread_start(nall_of, 0)
+
+    o_first(F - 1)
+    z_relay(0, 0)
 
     for g in range(KH):
         for copy in kv_moves[g][1]:
@@ -1091,9 +1144,10 @@
         draw[:, k_cols] = k_back.astype(BF)
         draw[:, QC + KC + g * HS : QC + KC + (g + 1) * HS] = total[:, HS:].astype(BF)
         gains[1:2, :] += terms
-    for copy in raw_out:
-        copy.start()
-    rq[c] = draw[:, lane(c, pa)]
+    for p in range(C):
+        if p not in raw_gone:
+            raw_send(p)
+    z_relay(0, 1)
     load_w.wait()
     width_step = min(512, W)
 
@@ -1112,12 +1166,17 @@
 
     lax.fori_loop(0, W // width_step, norm_ours, 0)
 
-    spread_end(nall, 0)
-    for copy in raw_come:
-        copy.wait_recv()
-    z_first(1)
-    z_relay(0, 0)
+    spread_pass(nall_of, 0)
+    for q in range(2, F - 1):
+        z_relay(0, q)
+    spread_end(nall_of, 0)
+    for k in range(1, C):
+        raw_come(lax.rem(c + k, C)).wait_recv()
+    for q in range(F - 1):
+        z_first(1, q)
     z_relay(1, 0)
+    z_last(0)
+    spread_start(outo_of, 1)
 
     swap_n.wait_recv()
     upstream = nown[...] + ngot[...].astype(FL)
@@ -1144,8 +1203,8 @@
         t_copy(k).start()
     zgot[f] = smx[f]
     for q in range(1, F - 1):
-        z_relay(0, q)
         z_relay(1, q)
+    spread_pass(outo_of, 1)
     for k in range(1, F):
         t_arrival(k).wait_recv()
     total = zgot[0]
@@ -1165,27 +1224,32 @@
 
     for j in range(1, S):
         u_copy(j).start()
-    z_last(0)
-    spread_start(outo, 2)
     z_last(1)
-    spread_start(outa, 3)
+    spread_start(outa_of, 2)
     for j in range(1, S):
         u_arrival(j).wait_recv()
     total = sgot[0]
     for e in range(1, S):
         total += sgot[e]
     small[...] = total
-    spread_pass(outo, 2)
-    spread_pass(outa, 3)
-    spread_end(outo, 2)
-    spread_end(outa, 3)
-
-    for buf, n in ((nall, 0), (dall, 1), (outo, 2), (outa, 3)):
-        spread_sent(buf, n)
+    spread_end(outo_of, 1)
+    spread_pass(outa_of, 2)
+    spread_end(outa_of, 2)
+
+    for view, n in ((nall_of, 0), (outo_of, 1), (outa_of, 2)):
+        spread_sent(view, n)
+    for q in range(F):
+        spread_sent(dall_of[q], 3 + q)
     swap_d.wait_send()
     swap_n.wait_send()
-    for copy in heads_out + raw_out:
+    for copy in heads_out:
         copy.wait_send()
+    for p in range(C):
+
+        @pl.when(c != p)
+        def _():
+            raw_copy(p).wait_send()
+
     for g in range(KH):
         for copy in kv_moves[g][0]:
             copy.wait_send()
@@ -1218,8 +1282,8 @@
         functools.partial(tail_body, C, F, T, KH),
         out_shape=(
             jax.ShapeDtypeStruct((Rh, W), FL),
-            jax.ShapeDtypeStruct((C, rows_a, pa), BF),
-            jax.ShapeDtypeStruct((C, po, cols_o), BF),
+            jax.ShapeDtypeStruct((rows_a, C * pa), BF),
+            jax.ShapeDtypeStruct((C * po, cols_o), BF),
             jax.ShapeDtypeStruct(small_shape, FL),
         ),
         in_specs=[VMEM] * 18 + [ANY] * 2,
@@ -1233,11 +1297,331 @@
             V((F + 1, rows_a, pa), BF), V((F + 1, po, cols_o), BF),
             V((F,) + small_shape, FL), V((F,) + small_shape, FL), V(small_shape, FL),
             V((S,) + small_shape, FL),
-            dma((2,)), dma((2,)), dma((2,)), dma((4, 3)), dma((4, 3)), dma((C,)), dma((C,)),
+            dma((2,)), dma((2,)), dma((2,)), dma((3 + F, 3)), dma((3 + F, 3)), dma((C,)), dma((C,)),
             dma((KH, C)), dma((KH, C)), dma((C,)), dma((C,)),
             dma((2, F)), dma((2, F + 1)), dma((F,)), dma((F,)), dma((S,)), dma((S,)),
         ],
         compiler_params=params(identity, 62),
+    )(*args)
+
+
+def head_body(
+    C, F, T, KH,
+    hidden, tab, again, qgain, kgain, fgain, cosf, sins, bias, wa, wo,
+    fall, full, ftab, raw, qrot, kv, keys_t, lse, heads, normed, resid, low, gates,
+    fa, fo, vals_t, nsend, ngot, nown,
+    loc, zs, zr, ys, yr, ks, kr, ts, tr, cs, cr, xs, xr,
+):
+    c, f, t, me = slab_place(C, T)
+    S = C * T
+    R, W = hidden.shape
+    Rh = tab.shape[0]
+    HS = qgain.shape[1]
+    PC = raw.shape[1]
+    QC = heads.shape[1]
+    KC = KH * HS
+    L = kv.shape[1]
+    G = QC // HS // KH
+    root = HS ** (-0.5)
+    core = lax.rem(c, 2)
+    sib = c + 1 - 2 * core
+    mate = lax.rem(c + 2, C)
+    mate_sib = lax.rem(sib + 2, C)
+    ra, (ro, co) = wa.shape[0], wo.shape
+    pa, po = ra // C, ro // C
+    ha, ho = pa // 2, po // 2
+    columns = [(c, lax.rem(f + k, F), t) for k in range(1, F)]
+    greet(columns + [slab_device(lax.rem(me + j, S), f, T) for j in range(1, S)])
+
+    def spot(arr, b, p):
+        half = arr % 2
+        if arr < 2:
+            return fa.at[pl.ds(pl.multiple_of(b * ra + p * pa + half * ha, ha), ha)]
+        rows = pl.ds(pl.multiple_of(p * po + half * ho, ho), ho)
+        return fo.at[rows, pl.ds(pl.multiple_of(b * co, co), co)]
+
+    def own(arr):
+        half = arr % 2
+        if arr < 2:
+            return wa.at[pl.ds(pl.multiple_of(c * pa + half * ha, ha), ha)]
+        return wo.at[pl.ds(pl.multiple_of(c * po + half * ho, ho), ho)]
+
+    def z_copy(arr, s, d):
+        b = f - (s - 1) if d == 0 else f + (s - 1)
+        source = own(arr) if s == 1 else spot(arr, b, c)
+        there = (c, f + 1 if d == 0 else f - 1, t)
+        return remote(source, spot(arr, b, c), zs.at[d, s, arr], zr.at[d, s, arr], there)
+
+    def z_sends(s, d):
+        b = f - (s - 1) if d == 0 else f + (s - 1)
+        return (f + 1 < F) & (b >= 0) if d == 0 else (f > 0) & (b < F)
+
+    def z_gets(s, d):
+        return f - s >= 0 if d == 0 else f + s < F
+
+    def came(s, d):
+        return f - s if d == 0 else f + s
+
+    def move(arr, s, d, p, sent, got, i, device):
+        here = spot(arr, came(s, d), p)
+        return remote(here, here, sent.at[d, s, arr, i], got.at[d, s, arr, i], device)
+
+    def z_begin(arr):
+        for d in range(2):
+
+            @pl.when(z_sends(1, d))
+            def _():
+                z_copy(arr, 1, d).start()
+
+    def z_in(arr, s):
+        for d in range(2):
+
+            @pl.when(z_gets(s, d))
+            def _():
+                here = spot(arr, came(s, d), c)
+                remote(here, here, zs.at[d, s, arr], zr.at[d, s, arr], (sib, f, t)).wait_recv()
+                if s + 1 < F:
+
+                    @pl.when(z_sends(s + 1, d))
+                    def _():
+                        z_copy(arr, s + 1, d).start()
+
+                move(arr, s, d, c, ys, yr, 0, (mate, f, t)).start()
+                move(arr, s, d, c, ks, kr, 0, (sib, f, t)).start()
+
+    def y_in(arr, s):
+        for d in range(2):
+
+            @pl.when(z_gets(s, d))
+            def _():
+                move(arr, s, d, mate, ys, yr, 0, (mate, f, t)).wait_recv()
+                move(arr, s, d, mate, ks, kr, 1, (sib, f, t)).start()
+
+    def k_in(arr, s, d):
+        move(arr, s, d, sib, ks, kr, 0, (sib, f, t)).wait_recv()
+        move(arr, s, d, mate_sib, ks, kr, 1, (sib, f, t)).wait_recv()
+
+    z_begin(0)
+    z_begin(1)
+    tabs = [
+        remote(tab, ftab.at[f], ts.at[k], tr.at[k], columns[k - 1]) for k in range(1, F)
+    ]
+    for copy in tabs:
+        copy.start()
+    own_a = pltpu.make_async_copy(wa, fa.at[pl.ds(pl.multiple_of(f * ra, ra), ra)], loc.at[0])
+    own_o = pltpu.make_async_copy(
+        wo, fo.at[:, pl.ds(pl.multiple_of(f * co, co), co)], loc.at[1]
+    )
+    own_a.start()
+    own_o.start()
+    ftab[f] = tab[...]
+
+    inputs = hidden[...].astype(FL)
+    normed[...] = norm_rows(inputs, again[...])[0].astype(BF)
+    wide = min(512, PC)
+
+    def project(b, first):
+        at = pl.ds(pl.multiple_of(b * ra, ra), ra)
+        left = normed[:, at]
+
+        def piece(i, carry):
+            cols = pl.ds(pl.multiple_of(i * wide, wide), wide)
+            part = jnp.dot(left, fa[at, cols], preferred_element_type=FL)
+            if first:
+                raw[:, cols] = part
+            else:
+                raw[:, cols] += part
+            return carry
+
+        lax.fori_loop(0, PC // wide, piece, 0)
+
+    def project_in(s):
+        for d in range(2):
+
+            @pl.when(z_gets(s, d))
+            def _():
+                k_in(0, s, d)
+                k_in(1, s, d)
+                project(came(s, d), False)
+
+    own_a.wait()
+    project(f, True)
+    z_in(0, 1)
+    z_in(1, 1)
+    for s in range(2, F):
+        z_in(0, s)
+        y_in(0, s - 1)
+        z_in(1, s)
+        y_in(1, s - 1)
+        if s == F - 2:
+            z_begin(2)
+            z_begin(3)
+        project_in(s - 1)
+    y_in(0, F - 1)
+    y_in(1, F - 1)
+    project_in(F - 1)
+
+    def turn(values):
+        return values * cosf[...] + pltpu.roll(values, HS // 2, 1) * sins[...]
+
+    at_c = pl.ds(pl.multiple_of(c * R, R), R)
+    for g in range(KH):
+        k_raw = raw[:, QC + g * HS : QC + (g + 1) * HS]
+        kv[g, at_c, :] = turn(norm_rows(k_raw, kgain[...])[0]).astype(BF)
+        kv[KH + g, at_c, :] = raw[:, QC + KC + g * HS : QC + KC + (g + 1) * HS].astype(BF)
+
+    def kv_move(p, i, device):
+        here = kv.at[:, pl.ds(pl.multiple_of(p * R, R), R), :]
+        return remote(here, here, cs.at[i], cr.at[i], device)
+
+    kv_move(c, 0, (mate, f, t)).start()
+    kv_move(c, 1, (sib, f, t)).start()
+
+    def query(i, carry):
+        at = pl.ds(pl.multiple_of(i * HS, HS), HS)
+        qrot[:, at] = turn(norm_rows(raw[:, at], qgain[...])[0]).astype(BF)
+        return carry
+
+    lax.fori_loop(0, QC // HS, query, 0)
+    save_a = pltpu.make_async_copy(fa, fall, loc.at[2])
+    save_a.start()
+    z_in(2, 1)
+    z_in(3, 1)
+    kv_move(mate, 0, (mate, f, t)).wait_recv()
+    kv_move(mate, 2, (sib, f, t)).start()
+    kv_move(sib, 1, (sib, f, t)).wait_recv()
+    kv_move(mate_sib, 2, (sib, f, t)).wait_recv()
+    for g in range(KH):
+        keys_t[g] = kv[g].astype(FL).T.astype(BF)
+        vals_t[g] = kv[KH + g].astype(FL).T.astype(BF)
+
+    def some_heads(g, first, count):
+        def one_head(i, carry):
+            h = first + i
+            at = pl.ds(pl.multiple_of(h * HS, HS), HS)
+            scores = outer_cols(kv[g], qrot[:, at]) * root + bias[...]
+            peak = jnp.max(scores, axis=0, keepdims=True)
+            weight = jnp.exp(scores - peak)
+            total = jnp.sum(weight, axis=0, keepdims=True)
+            lse[pl.ds(h, 1), :] = peak + jnp.log(total)
+            probs = (weight / total).astype(BF)
+            heads[:, at] = jnp.dot(vals_t[g], probs, preferred_element_type=FL).T.astype(BF)
+            return carry
+
+        lax.fori_loop(0, count, one_head, 0)
+
+    o_events = []
+    for s in range(2, F):
+        o_events.append((z_in, 2, s, y_in, 2, s - 1))
+        o_events.append((z_in, 3, s, y_in, 3, s - 1))
+    half = G // 2
+    for i in range(2 * KH):
+        some_heads(i // 2, i * half, half)
+        if i < len(o_events):
+            za, arr_a, sa, ya, arr_b, sb = o_events[i]
+            za(arr_a, sa)
+            ya(arr_b, sb)
+    for za, arr_a, sa, ya, arr_b, sb in o_events[2 * KH :]:
+        za(arr_a, sa)
+        ya(arr_b, sb)
+    y_in(2, F - 1)
+    y_in(3, F - 1)
+    for s in range(1, F):
+        for d in range(2):
+
+            @pl.when(z_gets(s, d))
+            def _():
+                k_in(2, s, d)
+                k_in(3, s, d)
+
+    own_o.wait()
+    save_o = pltpu.make_async_copy(fo, full, loc.at[3])
+    save_o.start()
+    at_t = pl.ds(pl.multiple_of(t * Rh, Rh), Rh)
+    at_u = pl.ds(pl.multiple_of((1 - t) * Rh, Rh), Rh)
+    step = min(512, W)
+
+    def theirs(i, carry):
+        cols = pl.ds(pl.multiple_of(i * step, step), step)
+        nsend[:, cols] = jnp.dot(
+            heads[at_u, :], fo[:, cols], preferred_element_type=FL
+        ).astype(BF)
+        return carry
+
+    def ours(i, carry):
+        cols = pl.ds(pl.multiple_of(i * step, step), step)
+        nown[:, cols] = jnp.dot(heads[at_t, :], fo[:, cols], preferred_element_type=FL)
+        return carry
+
+    lax.fori_loop(0, W // step, theirs, 0)
+    swap = remote(nsend, ngot, xs.at[0], xr.at[0], (c, f, 1 - t))
+    swap.start()
+    lax.fori_loop(0, W // step, ours, 0)
+    swap.wait_recv()
+    total = hidden[at_t, :].astype(FL) + (nown[...] + ngot[...].astype(FL))
+    resid[...] = total
+    ffn_low = norm_rows(total, fgain[...])[0].astype(BF)
+    low[...] = ffn_low
+    logits = jnp.dot(ffn_low, fa[:, PC:], preferred_element_type=FL)
+    named = tab[...] >= 0.0
+    masked = jnp.where(named, logits, MASKED)
+    shifted = jnp.where(
+        named, jnp.exp(masked - jnp.max(masked, axis=-1, keepdims=True)), 0.0
+    )
+    gates[...] = shifted / jnp.sum(shifted, axis=-1, keepdims=True)
+
+    save_a.wait()
+    save_o.wait()
+    swap.wait_send()
+    for copy in tabs:
+        copy.wait()
+    kv_move(c, 0, (mate, f, t)).wait_send()
+    kv_move(c, 1, (sib, f, t)).wait_send()
+    kv_move(mate, 2, (sib, f, t)).wait_send()
+    for s in range(1, F):
+        for d in range(2):
+
+            @pl.when(z_sends(s, d))
+            def _():
+                for arr in range(4):
+                    z_copy(arr, s, d).wait_send()
+
+            @pl.when(z_gets(s, d))
+            def _():
+                for arr in range(4):
+                    move(arr, s, d, c, ys, yr, 0, (mate, f, t)).wait_send()
+                    move(arr, s, d, c, ks, kr, 0, (sib, f, t)).wait_send()
+                    move(arr, s, d, mate, ks, kr, 1, (sib, f, t)).wait_send()
+
+
+def head(identity, C, F, T, KH, PC, L, args):
+    hidden, tab, qgain, wa, wo = args[0], args[1], args[3], args[9], args[10]
+    R, W = hidden.shape
+    Rh, lanes = tab.shape
+    HS = qgain.shape[1]
+    ra, ca = wa.shape
+    QC, co = wo.shape
+    dma = pltpu.SemaphoreType.DMA
+    V = pltpu.VMEM
+    shape = jax.ShapeDtypeStruct
+    return pl.pallas_call(
+        functools.partial(head_body, C, F, T, KH),
+        out_shape=(
+            shape((F * ra, ca), BF), shape((QC, F * co), BF), shape((F, Rh, lanes), FL),
+            shape((R, PC), FL), shape((R, QC), BF), shape((2 * KH, L, HS), BF),
+            shape((KH, HS, L), BF), shape((QC // HS, R), FL), shape((R, QC), BF),
+            shape((R, W), BF), shape((Rh, W), FL), shape((Rh, W), BF), shape((Rh, lanes), FL),
+        ),
+        in_specs=[VMEM] * 9 + [ANY] * 2,
+        out_specs=[ANY] * 2 + [VMEM] * 11,
+        scratch_shapes=[
+            V((F * ra, ca), BF), V((QC, F * co), BF), V((KH, HS, L), BF),
+            V((Rh, W), BF), V((Rh, W), BF), V((Rh, W), FL),
+            dma((4,)), dma((2, F, 4)), dma((2, F, 4)), dma((2, F, 4, 1)), dma((2, F, 4, 1)),
+            dma((2, F, 4, 2)), dma((2, F, 4, 2)), dma((F,)), dma((F,)), dma((3,)), dma((3,)),
+            dma((1,)), dma((1,)),
+        ],
+        compiler_params=params(identity, 58),
     )(*args)
 
 
@@ -1291,10 +1675,123 @@
     w_all = jnp.concatenate(
         [w_query, w_key, w_value, jnp.pad(w_router, ((0, 0), (0, lanes - expert_count)))], axis=1
     )
-    full_all, full_o, rank_z = gather_weights(C, F, w_all, w_output, rank_tab)
     proj_cols = q_cols + 2 * kv_cols
-    full_qkv = full_all[:, :proj_cols]
-    full_router = full_all[:, proj_cols : proj_cols + expert_count]
+    q_heads = q_cols // head_size
+    kv_heads = kv_cols // head_size
+    group_size = q_heads // kv_heads
+    inputs = hidden_in[0].astype(fl_type)
+    positions = c * row_count + jnp.arange(row_count, dtype=jnp.int32)
+    cosine, sine_tab = rope_tables(positions, head_size)
+    length = jnp.take(lengths, f)
+    total_len = row_count * C
+    row_start = t * half_rows
+    other_start = (1 - t) * half_rows
+    own_inputs = lax.dynamic_slice_in_dim(inputs, row_start, half_rows, 0)
+    own_positions = lax.dynamic_slice_in_dim(positions, row_start, half_rows, 0)
+    fused = C == 4 and T == 2
+    swap = [(i, 1 - i) for i in range(T)]
+    if fused:
+        cos_full = jnp.concatenate([cosine, cosine], axis=1)
+        sin_signed = jnp.concatenate([-sine_tab, sine_tab], axis=1)
+        key_pos = jnp.arange(total_len, dtype=jnp.int32)[:, None]
+        bias = jnp.where((key_pos <= positions[None, :]) & (key_pos < length), 0.0, MASKED)
+        (
+            full_all, full_o, rank_z, raw, q_rot, all_both, keys_t, log_total, heads_low,
+            normed_low, residual, ffn_low, gate_tab,
+        ) = head(
+            1, C, F, T, kv_heads, proj_cols, total_len,
+            (
+                hidden_in[0], rank_tab, attn_gain[None], query_gain[None], key_gain[None],
+                ffn_gain[None], cos_full, sin_signed, bias, w_all, w_output,
+            ),
+        )
+        full_router = full_all[:, proj_cols : proj_cols + expert_count]
+        gates = gate_tab[:, :expert_count]
+        ffn_factor = lax.rsqrt(jnp.mean(residual * residual, axis=-1, keepdims=True) + EPS)
+    else:
+        full_all, full_o, rank_z = gather_weights(C, F, w_all, w_output, rank_tab)
+        full_qkv = full_all[:, :proj_cols]
+        full_router = full_all[:, proj_cols : proj_cols + expert_count]
+        normed, norm_factor = norm_rows(inputs, attn_gain)
+        normed_low = normed.astype(bf_type)
+        raw = jnp.dot(normed_low, full_qkv, preferred_element_type=fl_type)
+        q_raw = raw[:, :q_cols].reshape(row_count, q_heads, head_size)
+        k_raw = raw[:, q_cols : q_cols + kv_cols].reshape(row_count, kv_heads, head_size)
+        values_low = raw[:, q_cols + kv_cols :].astype(bf_type).reshape(row_count, kv_heads, head_size)
+        q_normed, q_factor = norm_rows(q_raw, query_gain)
+        k_normed, k_factor = norm_rows(k_raw, key_gain)
+        q_rot = rotate(q_normed, cosine, sine_tab).astype(bf_type)
+        k_rot = rotate(k_normed, cosine, sine_tab).astype(bf_type)
+        queries = jnp.transpose(q_rot.reshape(row_count, kv_heads, group_size, head_size), (1, 2, 0, 3))
+        both = jnp.transpose(jnp.concatenate([k_rot, values_low], axis=1), (1, 0, 2))
+        all_both = lax.all_gather(both, "ctx", axis=1, tiled=True)
+        all_keys, all_values = all_both[:kv_heads], all_both[kv_heads:]
+        block_len = min(1024, total_len)
+        offsets = jnp.arange(total_len // block_len, dtype=jnp.int32) * block_len
+        stat_shape = (kv_heads, group_size, row_count)
+
+        def lse_step(carry, offset):
+            running_max, running_sum = carry
+            key_rows = lax.dynamic_slice_in_dim(all_keys, offset, block_len, 1)
+            scores, allowed = block_scores(queries, key_rows, offset, positions, length, inv_root)
+            new_max = jnp.maximum(running_max, jnp.max(scores, axis=-1))
+            exponent = jnp.where(allowed, jnp.exp(scores - new_max[..., None]), 0.0)
+            return (
+                (new_max, running_sum * jnp.exp(running_max - new_max) + jnp.sum(exponent, axis=-1)),
+                None,
+            )
+
+        (row_max, row_sum), _ = lax.scan(
+            lse_step, (jnp.full(stat_shape, MASKED, fl_type), jnp.zeros(stat_shape, fl_type)), offsets
+        )
+        log_total = row_max + jnp.log(row_sum)
+
+        def probs_of(offset):
+            key_rows = lax.dynamic_slice_in_dim(all_keys, offset, block_len, 1)
+            value_rows = lax.dynamic_slice_in_dim(all_values, offset, block_len, 1)
+            scores, allowed = block_scores(queries, key_rows, offset, positions, length, inv_root)
+            return (
+                jnp.where(allowed, jnp.exp(scores - log_total[..., None]), 0.0),
+                key_rows,
+                value_rows,
+            )
+
+        def out_step(running, offset):
+            probabilities, key_rows, value_rows = probs_of(offset)
+            return (
+                running
+                + jnp.einsum(
+                    "kgqj,kjd->kgqd",
+                    probabilities.astype(bf_type),
+                    value_rows,
+                    preferred_element_type=fl_type,
+                ),
+                None,
+            )
+
+        attn_acc, _ = lax.scan(
+            out_step, jnp.zeros((kv_heads, group_size, row_count, head_size), fl_type), offsets
+        )
+        heads_low = (
+            jnp.transpose(attn_acc, (2, 0, 1, 3))
+            .reshape(row_count, q_heads * head_size)
+            .astype(bf_type)
+        )
+        heads_other = lax.dynamic_slice_in_dim(heads_low, other_start, half_rows, 0)
+        heads_own = lax.dynamic_slice_in_dim(heads_low, row_start, half_rows, 0)
+        theirs = jnp.dot(heads_other, full_o, preferred_element_type=fl_type).astype(bf_type)
+        ours = lax.ppermute(theirs, "tp", swap)
+        attn_rows = jnp.dot(heads_own, full_o, preferred_element_type=fl_type) + ours.astype(fl_type)
+        own_factor = lax.dynamic_slice_in_dim(norm_factor, row_start, half_rows, 0)
+        residual = own_inputs + attn_rows
+        ffn_in, ffn_factor = norm_rows(residual, ffn_gain)
+        ffn_low = ffn_in.astype(bf_type)
+        logits = jnp.dot(ffn_low, full_router, preferred_element_type=fl_type)
+        is_named = named[:, :expert_count]
+        masked = jnp.where(is_named, logits, MASKED)
+        shifted = jnp.where(is_named, jnp.exp(masked - jnp.max(masked, axis=-1, keepdims=True)), 0.0)
+        gates = shifted / jnp.sum(shifted, axis=-1, keepdims=True)
+        gate_tab = jnp.pad(gates, ((0, 0), (0, lanes - expert_count)))
 
     def of_slab(table):
         picked = table[:, :, :expert_count].reshape(F, half_rows, C, F, T)
@@ -1306,100 +1803,6 @@
     chosen_slots = (
         jnp.transpose(rank_slab, (0, 2, 1))[:, :, None, :] == slot_ids[:, None]
     )
-
-    q_heads = q_cols // head_size
-    kv_heads = kv_cols // head_size
-    group_size = q_heads // kv_heads
-    inputs = hidden_in[0].astype(fl_type)
-    normed, norm_factor = norm_rows(inputs, attn_gain)
-    normed_low = normed.astype(bf_type)
-    raw = jnp.dot(normed_low, full_qkv, preferred_element_type=fl_type)
-    q_raw = raw[:, :q_cols].reshape(row_count, q_heads, head_size)
-    k_raw = raw[:, q_cols : q_cols + kv_cols].reshape(row_count, kv_heads, head_size)
-    values_low = raw[:, q_cols + kv_cols :].astype(bf_type).reshape(row_count, kv_heads, head_size)
-    q_normed, q_factor = norm_rows(q_raw, query_gain)
-    k_normed, k_factor = norm_rows(k_raw, key_gain)
-    positions = c * row_count + jnp.arange(row_count, dtype=jnp.int32)
-    cosine, sine_tab = rope_tables(positions, head_size)
-    q_rot = rotate(q_normed, cosine, sine_tab).astype(bf_type)
-    k_rot = rotate(k_normed, cosine, sine_tab).astype(bf_type)
-    queries = jnp.transpose(q_rot.reshape(row_count, kv_heads, group_size, head_size), (1, 2, 0, 3))
-    both = jnp.transpose(jnp.concatenate([k_rot, values_low], axis=1), (1, 0, 2))
-    all_both = lax.all_gather(both, "ctx", axis=1, tiled=True)
-    all_keys, all_values = all_both[:kv_heads], all_both[kv_heads:]
-    total_len = all_keys.shape[1]
-    block_len = min(1024, total_len)
-    offsets = jnp.arange(total_len // block_len, dtype=jnp.int32) * block_len
-    length = jnp.take(lengths, f)
-    stat_shape = (kv_heads, group_size, row_count)
-
-    def lse_step(carry, offset):
-        running_max, running_sum = carry
-        key_rows = lax.dynamic_slice_in_dim(all_keys, offset, block_len, 1)
-        scores, allowed = block_scores(queries, key_rows, offset, positions, length, inv_root)
-        new_max = jnp.maximum(running_max, jnp.max(scores, axis=-1))
-        exponent = jnp.where(allowed, jnp.exp(scores - new_max[..., None]), 0.0)
-        return (
-            (new_max, running_sum * jnp.exp(running_max - new_max) + jnp.sum(exponent, axis=-1)),
-            None,
-        )
-
-    (row_max, row_sum), _ = lax.scan(
-        lse_step, (jnp.full(stat_shape, MASKED, fl_type), jnp.zeros(stat_shape, fl_type)), offsets
-    )
-    log_total = row_max + jnp.log(row_sum)
-
-    def probs_of(offset):
-        key_rows = lax.dynamic_slice_in_dim(all_keys, offset, block_len, 1)
-        value_rows = lax.dynamic_slice_in_dim(all_values, offset, block_len, 1)
-        scores, allowed = block_scores(queries, key_rows, offset, positions, length, inv_root)
-        return (
-            jnp.where(allowed, jnp.exp(scores - log_total[..., None]), 0.0),
-            key_rows,
-            value_rows,
-        )
-
-    def out_step(running, offset):
-        probabilities, key_rows, value_rows = probs_of(offset)
-        return (
-            running
-            + jnp.einsum(
-                "kgqj,kjd->kgqd",
-                probabilities.astype(bf_type),
-                value_rows,
-                preferred_element_type=fl_type,
-            ),
-            None,
-        )
-
-    attn_acc, _ = lax.scan(
-        out_step, jnp.zeros((kv_heads, group_size, row_count, head_size), fl_type), offsets
-    )
-    heads_low = (
-        jnp.transpose(attn_acc, (2, 0, 1, 3))
-        .reshape(row_count, q_heads * head_size)
-        .astype(bf_type)
-    )
-    swap = [(i, 1 - i) for i in range(T)]
-    row_start = t * half_rows
-    other_start = (1 - t) * half_rows
-    heads_other = lax.dynamic_slice_in_dim(heads_low, other_start, half_rows, 0)
-    heads_own = lax.dynamic_slice_in_dim(heads_low, row_start, half_rows, 0)
-    theirs = jnp.dot(heads_other, full_o, preferred_element_type=fl_type).astype(bf_type)
-    ours = lax.ppermute(theirs, "tp", swap)
-    attn_rows = jnp.dot(heads_own, full_o, preferred_element_type=fl_type) + ours.astype(fl_type)
-    own_inputs = lax.dynamic_slice_in_dim(inputs, row_start, half_rows, 0)
-    own_factor = lax.dynamic_slice_in_dim(norm_factor, row_start, half_rows, 0)
-    own_positions = lax.dynamic_slice_in_dim(positions, row_start, half_rows, 0)
-    residual = own_inputs + attn_rows
-    ffn_in, ffn_factor = norm_rows(residual, ffn_gain)
-    ffn_low = ffn_in.astype(bf_type)
-    logits = jnp.dot(ffn_low, full_router, preferred_element_type=fl_type)
-    is_named = named[:, :expert_count]
-    masked = jnp.where(is_named, logits, MASKED)
-    shifted = jnp.where(is_named, jnp.exp(masked - jnp.max(masked, axis=-1, keepdims=True)), 0.0)
-    gates = shifted / jnp.sum(shifted, axis=-1, keepdims=True)
-    gate_tab = jnp.pad(gates, ((0, 0), (0, lanes - expert_count)))
 
     select = chosen_slots.astype(bf_type)
     received, _, gate_z = dispatch(2, C, F, T, ffn_low, select, gate_tab)
@@ -1461,11 +1864,7 @@
     grad_resid_norm, ffn_gain_terms = norm_back(residual, ffn_factor, ffn_gain, grad_ffn)
     grad_residual = grad_out + grad_resid_norm
     grad_own = grad_residual.astype(bf_type)
-    if C == 4 and T == 2:
-        cos_full = jnp.concatenate([cosine, cosine], axis=1)
-        sin_signed = jnp.concatenate([-sine_tab, sine_tab], axis=1)
-        key_pos = jnp.arange(total_len, dtype=jnp.int32)[:, None]
-        bias = jnp.where((key_pos <= positions[None, :]) & (key_pos < length), 0.0, MASKED)
+    if fused:
         vec_in = jnp.zeros((8, width), fl_type)
         vec_in = vec_in.at[1].set(jnp.sum(ffn_gain_terms, axis=0))
         vec_in = vec_in.at[2, 2 * head_size].set(loss_part)
@@ -1473,18 +1872,16 @@
         grad_input, total_a, total_o, summed = tail(
             9, C, F, T, kv_heads,
             (
-                grad_own, heads_low, normed_low, q_rot.reshape(row_count, q_cols), all_both,
-                jnp.swapaxes(all_keys, 1, 2), raw, log_total.reshape(q_heads, row_count), bias,
+                grad_own, heads_low, normed_low, q_rot, all_both, keys_t, raw, log_total, bias,
                 cos_full, sin_signed, query_gain[None], key_gain[None], attn_gain[None],
                 own_inputs, grad_residual, router_rows, vec_in, full_o, full_all,
             ),
             width, q_cols // C,
         )
-        total_a = jnp.swapaxes(total_a, 0, 1).reshape(-1, proj_cols).astype(fl_type)
-        grad_query = total_a[:, :q_cols]
-        grad_key = total_a[:, q_cols : q_cols + kv_cols]
-        grad_value = total_a[:, q_cols + kv_cols :]
-        grad_output_w = total_o.reshape(w_output.shape).astype(fl_type)
+        grad_query = total_a[:, :q_cols].astype(fl_type)
+        grad_key = total_a[:, q_cols : q_cols + kv_cols].astype(fl_type)
+        grad_value = total_a[:, q_cols + kv_cols :].astype(fl_type)
+        grad_output_w = total_o.astype(fl_type)
         router_len = router_rows.shape[1]
         grad_router = summed[:router_len].reshape(w_router.shape)
         sum_attn, sum_ffn = summed[router_len], summed[router_len + 1]

time: 889 us -> 763 us (0.86)
  local copies, waits for them, and re-layouts: 70.4 us -> 17.8 us
  matrix products: 104 us -> 71.7 us
  other arithmetic: 47.5 us -> 27.2 us
  between operations: 18.3 us -> 4.44 us
    unnamed x99 -> x35, local copies, waits for them, and re-layouts: 33.3 us -> 6.48 us
    dot_general x6 -> x0, matrix products: 25.7 us -> none  [the longest x1 5.87 us: out_step(): jnp.einsum('kgqj,kjd->kgqd', probabilities.astype(bf_type), value_rows, p...]
    pallas_call x1, Pallas kernels: 202 us -> 177 us  [tail(): pl.pallas_call(functools.partial(tail_body, C, F, T, KH), out_shape=(jax....]
    pallas_call x1, Pallas kernels: 104 us -> 128 us  [head(): pl.pallas_call(functools.partial(head_body, C, F, T, KH), out_shape=(shap...]
  transfers between devices with their start and end apart: 2 -> 0, of which waited for: 1 -> 0; matrix products, arithmetic and copies ran while one was open for 3% -> 0% of each run, Pallas kernels for 0% -> 0%
where the time goes in v3:
time: 763 us; the launch traced here: 754 us
  Pallas kernels  633 us (83%)
  matrix products  71.7 us (9%)
  other arithmetic  27.2 us (4%)
  local copies, waits for them, and re-layouts  17.8 us (2%)
    pallas_call x1, Pallas kernels, tail(): pl.pallas_call(functools.partial(tail_body, C, F, T, KH), out_shape=(jax....  177 us
    pallas_call x2, Pallas kernels, dispatch(): pl.pallas_call(functools.partial(dispatch_body, C, F, T, tabbed), out_sha...  174 us
    pallas_call x2, Pallas kernels, combine(): pl.pallas_call(functools.partial(combine_body, C, F, T, tabbed), out_shap...  154 us
    pallas_call x1, Pallas kernels, head(): pl.pallas_call(functools.partial(head_body, C, F, T, KH), out_shape=(shap...  128 us
    dot_general x3, matrix products, inner_rows(): lax.dot_general(left, right, (((0,), (0,)), ((), ())), preferred_element_...  24.3 us
    dot_general x3, matrix products, outer_cols(): lax.dot_general(left, right, (((1,), (1,)), ((), ())), preferred_element_...  24.1 us

profile of v3, /device:TPU:25, one launch (start us, length us, event | category | flops | bytes accessed | tf_op | source)
XLA Modules:
  0.0 754.0 jit_solution(2502771467103922154)
XLA Ops:
  10.9 2.1 dynamic-slice_convert_fusion.own_in
  13.0 3.2 fusion.8.wa
  16.2 128.3 %shard_map.254 = (bf16[2048,2688]{1,0:T(8,128)(2,1)}, bf16[2048,2048]{1,0:T(8,128)(2,1)}, f32[4,128,128]{2,1,0:T(8,128)}, f32[256,2560]{1,0:T(8,128)}, bf16[256,...) custom-call(bf16[256,2048]{1,0:T(8,128)(2,1)} %bitcast.87, ...), custom_call_target="tpu_custom_call" | custom-call | tf_op jit(solution)/shard_map/pallas_call | solution.py:1607
  147.1 89.9 %shard_map.255 = (bf16[8,4,48,2048]{3,2,1,0:T(8,128)(2,1)S(1)}, bf16[4,128,2048]{2,1,0:T(8,128)(2,1)}, f32[4,128,128]{2,1,0:T(8,128)S(1)}) custom-call(bf16[128,2048]{1,0:T(8,128)(2,1)S(1)} %copy-done, bf16[4,8,48,128]{3,2,1,0:T(8,128)(2,1)S(1)} %fusion.15.select, f32[128,128]{1,0:T(8,128)S(1)} %copy-done.1), custom_call_target="tpu_custom_call" | custom-call | tf_op jit(solution)/shard_map/pallas_call | solution.py:371
  237.0 2.6 copy-done.3
  240.7 15.2 %fusion.1 = f32[1536,1536]{0,1:T(8,128)S(1)} fusion(bf16[1536,2048]{1,0:T(8,128)(2,1)} %bitcast.80, bf16[1,2048,1536]{2,1,0:T(8,128)(2,1)} %param.32), kind=kOutput, calls=%fused_computation.5 | convolution fusion | flops 9663676416 | bytes 22020096 | tf_op jit(solution)/shard_map/dot_general | solution.py:1810
  255.9 1.5 multiply_convert_fusion.2
  257.8 5.4 convolution_convert_fusion
  263.2 76.2 %shard_map.256 = (bf16[4,8,48,2048]{3,2,1,0:T(8,128)(2,1)S(1)}, bf16[4,128,2048]{2,1,0:T(8,128)(2,1)S(1)}) custom-call(bf16[8,4,48,2048]{3,2,1,0:T(8,128)(2,1)S(1)} %bitcast.76, bf16[4,2,128,384]{3,2,1,0:T(8,128)(2,1)S(1)} %pad_maximum_fusion.3.weigh), custom_call_target="tpu_custom_call" | custom-call | tf_op jit(solution)/shard_map/pallas_call | solution.py:490
  339.8 1.8 multiply_reduce_fusion.1
  341.7 83.9 %shard_map.257 = (bf16[8,4,48,2048]{3,2,1,0:T(8,128)(2,1)S(1)}, bf16[4,128,2048]{2,1,0:T(8,128)(2,1)S(1)}) custom-call(bf16[128,2048]{1,0:T(8,128)(2,1)S(1)} %multiply_convert_fusion.3.rows, bf16[4,8,48,256]{3,2,1,0:T(8,128)(2,1)S(1)} %pad_maximum_fusion.4.select), custom_call_target="tpu_custom_call" | custom-call | tf_op jit(solution)/shard_map/pallas_call | solution.py:371
  425.6 1.9 multiply_reduce_fusion
  427.8 10.0 %multiply_convert_fusion.1 = (bf16[1536,768]{0,1:T(8,128)(2,1)}, bf16[1536,768]{0,1:T(8,128)(2,1)}) fusion(f32[1536,1536]{0,1:T(8,128)S(1)} %fusion.1, bf16[1536,2048]{1,0:T(8,128)(2,1)S(1)} %bitcast.82, bf16[1,768,2048]{2,1,0:T(8,128)(2,1)} %param.33), kind=kOutput, calls=%fused_computation.11 | convolution fusion | flops 4847173632 | bytes 23592960 | tf_op jit(solution)/shard_map/dot_general | solution.py:65
  437.8 6.9 convolution_bitcast_fusion.1
  444.9 17.1 %convolution_bitcast_fusion = f32[1,2048,1536]{2,1,0:T(8,128)} fusion(bf16[1536,2048]{1,0:T(8,128)(2,1)} %bitcast.81, bf16[1536,768]{0,1:T(8,128)(2,1)} %get-tuple-element.164, bf16[1536,768]{0,1:T(8,128)(2,1)} %get-tuple-element.163), kind=kOutput, calls=%fused_computation.1 | convolution fusion | flops 9673113600 | bytes 23592960 | tf_op jit(solution)/shard_map/dot_general | solution.py:59
  462.0 12.2 %convolution_convert_fusion.1 = bf16[1536,2048]{1,0:T(8,128)(2,1)S(1)} fusion(bf16[1,2048,1536]{2,1,0:T(8,128)(2,1)} %param.32, bf16[1536,768]{0,1:T(8,128)(2,1)S(1)} %copy-done.15, bf16[1536,768]{0,1:T(8,128)(2,1)S(1)} %copy-done.14), kind=kOutput, calls=%fused_computation.3 | convolution fusion | flops 9676259328 | bytes 17301504 | tf_op jit(solution)/shard_map/dot_general | solution.py:65
  474.2 78.0 %shard_map.258 = (bf16[4,8,48,2048]{3,2,1,0:T(8,128)(2,1)}, bf16[4,128,2048]{2,1,0:T(8,128)(2,1)S(1)}, f32[4,128,128]{2,1,0:T(8,128)S(1)}) custom-call(bf16[8,4,48,2048]{3,2,1,0:T(8,128)(2,1)S(1)} %bitcast.77, bf16[4,1,128,384]{3,2,1,0:T(8,128)(2,1)S(1)} %get-tuple-element.161.weigh, f32[4,128,128]{2,1,0:T(8,128)S(1)} %pad.16.refs_0_), custom_call_target="tpu_custom_call" | custom-call | tf_op jit(solution)/shard_map/pallas_call | solution.py:490
  554.1 1.9 multiply_reduce_fusion.2
  556.0 1.6 fusion.24
  559.9 176.6 %shard_map.259 = (f32[128,2048]{1,0:T(8,128)}, bf16[512,2560]{1,0:T(8,128)(2,1)}, bf16[2048,512]{1,0:T(8,128)(2,1)}, f32[16,2048]{1,0:T(8,128)}) custom-call(bf16[128,2048]{1,0:T(8,128)(2,1)} %get-tuple-element.159.grad_own, bf16[256,2048]{1,0:T(8,128)(2,1)} %get-tuple-element.76.heads, bf16[256,2048]{1,0:T(8,128)(2,1)} %get-tuple-element.77.normed, ...), custom_call_target="tpu_custom_call" | custom-call | tf_op jit(solution)/shard_map/pallas_call | solution.py:1281
  739.6 1.5 fusion.26
  742.9 2.1 slice_convert_fusion.1
  744.9 4.1 slice_convert_fusion
  749.1 2.6 convert_element_type.133
  (84 shorter events, 22.8 us)
Async XLA Ops:
  0.6 12.3 %copy-start.8 = (bf16[512,2048]{1,0:T(8,128)(2,1)S(1)}, bf16[512,2048]{1,0:T(8,128)(2,1)}, u32[]{:S(2)}) copy-start(bf16[512,2048]{1,0:T(8,128)(2,1)} %param.24) | copy-start | bytes 6291460
  144.5 1.7 copy-start
  146.2 0.8 copy-start.1
  237.0 2.6 copy-start.3
  255.9 1.9 copy-start.13
  257.8 5.4 copy-start.5
  263.1 76.6 %copy-start.4 = (f32[128,2048]{1,0:T(8,128)S(1)}, f32[128,2048]{1,0:T(8,128)}, u32[]{:S(2)}) copy-start(f32[128,2048]{1,0:T(8,128)} %get-tuple-element.63) | copy-start | bytes 3145732
  263.1 76.6 %copy-start.10 = (bf16[1,128,2048]{2,1,0:T(8,128)(2,1)S(1)}, bf16[1,128,2048]{2,1,0:T(8,128)(2,1)}, u32[]{:S(2)}) copy-start(bf16[1,128,2048]{2,1,0:T(8,128)(2,1)} %param.20) | copy-start | bytes 1572868
  427.8 10.0 %copy-start.6 = (bf16[1536,768]{0,1:T(8,128)(2,1)S(1)}, bf16[1536,768]{0,1:T(8,128)(2,1)}, u32[]{:S(2)}) copy-start(bf16[1536,768]{0,1:T(8,128)(2,1)} %copy-done.5) | copy-start | bytes 7077892
  444.9 17.1 %copy-start.14 = (bf16[1536,768]{0,1:T(8,128)(2,1)S(1)}, bf16[1536,768]{0,1:T(8,128)(2,1)}, u32[]{:S(2)}) copy-start(bf16[1536,768]{0,1:T(8,128)(2,1)} %get-tuple-element.163) | copy-start | bytes 7077892
  444.9 17.1 %copy-start.15 = (bf16[1536,768]{0,1:T(8,128)(2,1)S(1)}, bf16[1536,768]{0,1:T(8,128)(2,1)}, u32[]{:S(2)}) copy-start(bf16[1536,768]{0,1:T(8,128)(2,1)} %get-tuple-element.164) | copy-start | bytes 7077892
  474.2 79.6 %copy-start.2 = (f32[128,128]{1,0:T(8,128)S(1)}, f32[128,128]{1,0:T(8,128)}, u32[]{:S(2)}) copy-start(f32[128,128]{1,0:T(8,128)} %get-tuple-element.66.refs_0_) | copy-start | bytes 196612
  474.2 79.8 %copy-start.12 = (f32[2048]{0:T(1024)S(1)}, f32[2048]{0:T(1024)}, u32[]{:S(2)}) copy-start(f32[2048]{0:T(1024)} %param.30) | copy-start | bytes 24580
  558.3 1.6 copy-start.11
  736.4 12.6 %copy-start.7 = (bf16[2048,512]{1,0:T(8,128)(2,1)S(1)}, bf16[2048,512]{1,0:T(8,128)(2,1)}, u32[]{:S(2)}) copy-start(bf16[2048,512]{1,0:T(8,128)(2,1)} %get-tuple-element.87) | copy-start | bytes 6291460
  749.1 2.6 copy-start.9

commit v4 on v3

--- a/solution.py
+++ b/solution.py
@@ -1625,6 +1625,446 @@
     )(*args)
 
 
+def moe_place(C, F, T):
+    c, f, t, me = slab_place(C, T)
+    S = C * T
+    columns = [(c, lax.rem(f + k, F), t) for k in range(1, F)]
+    slab = [slab_device(lax.rem(me + j, S), f, T) for j in range(S)]
+
+    def block(k):
+        return lax.rem(f + F - k, F)
+
+    def to(j):
+        return lax.rem(me + j, S)
+
+    def come(j):
+        return lax.rem(me + S - j, S)
+
+    return c, f, t, me, columns, slab, block, to, come
+
+
+def moe_forward_body(
+    C, F, T,
+    rows, gate_t, select, w_in, w_out,
+    xr, got, pre, mixed, part, fgate,
+    zbuf, stage, xs, gs, ysend, wi, wo, pstage, zpart,
+    loc, zs, zr, ss, sr, rs, rr, ps, pr, ts, tr, xl, gl, pl_,
+):
+    c, f, t, me, columns, slab, block, to, come = moe_place(C, F, T)
+    S = C * T
+    K, W = xr.shape[2], xr.shape[3]
+    FFW = w_out.shape[0]
+    greet(columns + slab[1:])
+    load_i = pltpu.make_async_copy(w_in, wi, loc.at[0])
+    load_o = pltpu.make_async_copy(w_out, wo, loc.at[1])
+    z_out = [remote(rows, zbuf.at[f], zs.at[k], zr.at[k], columns[k - 1]) for k in range(1, F)]
+    g_out = [remote(gate_t, fgate.at[f], ts.at[k], tr.at[k], columns[k - 1]) for k in range(1, F)]
+    for copy in z_out + g_out:
+        copy.start()
+    load_i.start()
+    load_o.start()
+    zbuf[f] = rows[...]
+    fgate[f] = gate_t[...]
+
+    def slab_copy(k, j):
+        b = block(k)
+        return remote(stage.at[to(j), b], xs.at[b, me], ss.at[k, j], sr.at[k, j], slab[j])
+
+    def slab_arrival(k, j):
+        b = block(k)
+        return remote(stage.at[to(j), b], xs.at[b, come(j)], ss.at[k, j], sr.at[k, j], slab[j])
+
+    def back_copy(k, j):
+        b = block(k)
+        return remote(ysend.at[b, to(j)], gs.at[b, me], rs.at[k, j], rr.at[k, j], slab[j])
+
+    def back_arrival(k, j):
+        b = block(k)
+        return remote(ysend.at[b, to(j)], gs.at[b, come(j)], rs.at[k, j], rr.at[k, j], slab[j])
+
+    def part_copy(k):
+        b = block(k)
+        return remote(pstage.at[b], zpart.at[f], ps.at[k], pr.at[k], (c, b, t))
+
+    def part_arrival(k):
+        b = lax.rem(f + k, F)
+        return remote(pstage.at[b], zpart.at[b], ps.at[k], pr.at[k], (c, b, t))
+
+    def keep_x(k):
+        return pltpu.make_async_copy(xs.at[block(k)], xr.at[block(k)], xl.at[k])
+
+    def keep_got(k):
+        return pltpu.make_async_copy(gs.at[block(k)], got.at[block(k)], gl.at[k])
+
+    def send(k):
+        b = block(k)
+        if k > 0:
+            remote(rows, zbuf.at[b], zs.at[k], zr.at[k], columns[k - 1]).wait_recv()
+        for j in [*range(1, S), 0]:
+            e = to(j)
+            picked = jnp.dot(select[b, e], zbuf[b], preferred_element_type=FL).astype(BF)
+            if j:
+                stage[e, b] = picked
+                slab_copy(k, j).start()
+            else:
+                xs[b, me] = picked
+
+    def expert(k):
+        b = block(k)
+        for j in range(1, S):
+            slab_arrival(k, j).wait_recv()
+        if k == 0:
+            load_i.wait()
+        keep_x(k).start()
+        x = xs[b].reshape(S * K, W)
+        tile = 256
+        for i in range(FFW // tile):
+            at = slice(i * tile, (i + 1) * tile)
+            up_at = slice(FFW + i * tile, FFW + (i + 1) * tile)
+            gate_pre = jnp.dot(x, wi[:, at], preferred_element_type=FL)
+            up_pre = jnp.dot(x, wi[:, up_at], preferred_element_type=FL)
+            pre[b, :, at] = gate_pre
+            pre[b, :, up_at] = up_pre
+            mixed[b, :, at] = (gate_pre * jax.nn.sigmoid(gate_pre) * up_pre).astype(BF)
+        if k == 0:
+            load_o.wait()
+        hidden = mixed[b]
+        tile = min(512, W)
+        for i in range(W // tile):
+            at = slice(i * tile, (i + 1) * tile)
+            y = jnp.dot(hidden, wo[:, at], preferred_element_type=FL).astype(BF)
+            ysend[b, :, :, at] = y.reshape(S, K, tile)
+        for j in range(1, S):
+            back_copy(k, j).start()
+        gs[b, me] = ysend[b, me]
+
+    def gather(k):
+        b = block(k)
+        for j in range(1, S):
+            back_arrival(k, j).wait_recv()
+        keep_got(k).start()
+        scaled = []
+        for s in range(S):
+            e = (s // T) * F * T + f * T + s % T
+            scaled.append(select[b, s].astype(FL) * fgate[b, pl.ds(e, 1), :])
+        scaled = jnp.concatenate(scaled, axis=0)
+        high = scaled.astype(BF)
+        low = (scaled - high.astype(FL)).astype(BF)
+        tile = min(512, W)
+        for i in range(W // tile):
+            at = slice(i * tile, (i + 1) * tile)
+            y = gs[b, :, :, at].reshape(S * K, tile)
+            total = inner_rows(high, y) + inner_rows(low, y)
+            if k:
+                pstage[b, :, at] = total.astype(BF)
+            else:
+                part[:, at] = total
+        if k:
+            part_copy(k).start()
+
+    send(0)
+    send(1)
+    expert(0)
+    send(2)
+    expert(1)
+    for k in range(3, F):
+        send(k)
+    for k in range(1, F):
+        g_out[k - 1].wait_send()
+        remote(gate_t, fgate.at[block(k)], ts.at[k], tr.at[k], columns[k - 1]).wait_recv()
+    gather(0)
+    for k in range(2, F):
+        expert(k)
+        gather(k - 1)
+    gather(F - 1)
+    for k in range(1, F):
+        part_arrival(k).wait_recv()
+        part[...] += zpart[lax.rem(f + k, F)].astype(FL)
+    for copy in z_out:
+        copy.wait_send()
+    for k in range(F):
+        keep_x(k).wait()
+        keep_got(k).wait()
+        if k:
+            part_copy(k).wait_send()
+        for j in range(1, S):
+            slab_copy(k, j).wait_send()
+            back_copy(k, j).wait_send()
+
+
+def moe_forward(identity, C, F, T, rows, gate_t, select, w_in, w_out):
+    S = C * T
+    K = select.shape[2]
+    R, W = rows.shape
+    H2, FFW = w_in.shape[1], w_out.shape[0]
+    dma = pltpu.SemaphoreType.DMA
+    V = pltpu.VMEM
+    shape = jax.ShapeDtypeStruct
+    return pl.pallas_call(
+        functools.partial(moe_forward_body, C, F, T),
+        out_shape=(
+            shape((F, S, K, W), BF), shape((F, S, K, W), BF), shape((F, S * K, H2), FL),
+            shape((F, S * K, FFW), BF), shape((R, W), FL), shape((F,) + gate_t.shape, FL),
+        ),
+        in_specs=[VMEM] * 3 + [ANY] * 2,
+        out_specs=[ANY] * 2 + [VMEM] * 4,
+        scratch_shapes=[
+            V((F, R, W), BF), V((S, F, K, W), BF), V((F, S, K, W), BF), V((F, S, K, W), BF),
+            V((F, S, K, W), BF), V((W, H2), BF), V((FFW, W), BF), V((F, R, W), BF),
+            V((F, R, W), BF),
+            dma((2,)), dma((F,)), dma((F,)), dma((F, S)), dma((F, S)), dma((F, S)), dma((F, S)),
+            dma((F,)), dma((F,)), dma((F,)), dma((F,)), dma((F,)), dma((F,)), dma((F,)),
+        ],
+        compiler_params=params(identity, 60),
+    )(rows, gate_t, select, w_in, w_out)
+
+
+def moe_backward_body(
+    C, F, T,
+    rows, fgate, select, mixed, w_in, w_out, xr, got, pre,
+    part, grad_in, grad_out, dgate,
+    zbuf, stage, gs, ysx, back, wi, wo, pstage, zpart, dpre, prebuf, tiles, dgs, dgr,
+    loc, zs, zr, ss, sr, rs, rr, ps, pr, ds_, dr, pl_, tl,
+):
+    c, f, t, me, columns, slab, block, to, come = moe_place(C, F, T)
+    S = C * T
+    K, W = xr.shape[2], xr.shape[3]
+    FFW = w_out.shape[0]
+    R = rows.shape[0]
+    greet(columns + slab[1:])
+    load_i = pltpu.make_async_copy(w_in, wi, loc.at[0])
+    load_o = pltpu.make_async_copy(w_out, wo, loc.at[1])
+    load_y = pltpu.make_async_copy(got, ysx, loc.at[2])
+    load_x = pltpu.make_async_copy(xr, ysx, loc.at[3])
+    z_out = [remote(rows, zbuf.at[f], zs.at[k], zr.at[k], columns[k - 1]) for k in range(1, F)]
+    for copy in z_out:
+        copy.start()
+    load_y.start()
+    load_o.start()
+    load_i.start()
+    zbuf[f] = rows[...]
+
+    def pre_load(k):
+        return pltpu.make_async_copy(pre.at[block(k)], prebuf, pl_.at[k])
+
+    def slab_copy(k, j):
+        b = block(k)
+        return remote(stage.at[to(j), b], gs.at[b, me], ss.at[k, j], sr.at[k, j], slab[j])
+
+    def slab_arrival(k, j):
+        b = block(k)
+        return remote(stage.at[to(j), b], gs.at[b, come(j)], ss.at[k, j], sr.at[k, j], slab[j])
+
+    def back_copy(k, j):
+        b = block(k)
+        return remote(stage.at[to(j), b], back.at[b, me], rs.at[k, j], rr.at[k, j], slab[j])
+
+    def back_arrival(k, j):
+        b = block(k)
+        return remote(stage.at[to(j), b], back.at[b, come(j)], rs.at[k, j], rr.at[k, j], slab[j])
+
+    def part_copy(k):
+        b = block(k)
+        return remote(pstage.at[b], zpart.at[f], ps.at[k], pr.at[k], (c, b, t))
+
+    def part_arrival(k):
+        b = lax.rem(f + k, F)
+        return remote(pstage.at[b], zpart.at[b], ps.at[k], pr.at[k], (c, b, t))
+
+    def gate_copy(k):
+        b = block(k)
+        return remote(dgs.at[b], dgr.at[f], ds_.at[k], dr.at[k], (c, b, t))
+
+    def gate_arrival(k):
+        b = lax.rem(f + k, F)
+        return remote(dgs.at[b], dgr.at[b], ds_.at[k], dr.at[k], (c, b, t))
+
+    lanes = lax.broadcasted_iota(jnp.int32, (K, R), 1)
+
+    def send(k):
+        b = block(k)
+        if k > 0:
+            remote(rows, zbuf.at[b], zs.at[k], zr.at[k], columns[k - 1]).wait_recv()
+        for j in [*range(1, S), 0]:
+            s = to(j)
+            e = lax.div(s, T) * F * T + f * T + lax.rem(s, T)
+            chosen = select[b, s]
+            picked = jnp.dot(chosen, zbuf[b], preferred_element_type=FL)
+            gate = jnp.sum(
+                chosen.astype(FL) * fgate[b, pl.ds(e, 1), :], axis=1, keepdims=True
+            )
+            scaled = (picked * gate).astype(BF)
+            if j:
+                stage[s, b] = scaled
+                slab_copy(k, j).start()
+            else:
+                gs[b, me] = scaled
+
+    def gate_grads(k):
+        b = block(k)
+        total = jnp.zeros((R, R), FL)
+        for s in range(S):
+            chosen = select[b, s]
+            picked = jnp.dot(chosen, zbuf[b], preferred_element_type=FL)
+            dots = jnp.sum(picked * ysx[b, s].astype(FL), axis=1, keepdims=True)
+            spread = jnp.where(lanes == s, dots, 0.0)
+            high = spread.astype(BF)
+            low = (spread - high.astype(FL)).astype(BF)
+            total += inner_rows(high, chosen) + inner_rows(low, chosen)
+        dgs[b] = total[:S, :]
+        if k:
+            gate_copy(k).start()
+        else:
+            dgr[f] = total[:S, :]
+
+    def expert(k):
+        b = block(k)
+        for j in range(1, S):
+            slab_arrival(k, j).wait_recv()
+        if k == 0:
+            load_o.wait()
+        g = gs[b].reshape(S * K, W)
+        pre_load(k).wait()
+        tile = 256
+        for i in range(FFW // tile):
+            at = slice(i * tile, (i + 1) * tile)
+            up_at = slice(FFW + i * tile, FFW + (i + 1) * tile)
+            grad_mixed = outer_cols(g, wo[at, :])
+            gate_pre = prebuf[:, at]
+            up_pre = prebuf[:, up_at]
+            sigmoid = jax.nn.sigmoid(gate_pre)
+            dpre[b, :, at] = (
+                grad_mixed * up_pre * (sigmoid * (1.0 + gate_pre * (1.0 - sigmoid)))
+            ).astype(BF)
+            dpre[b, :, up_at] = (grad_mixed * (gate_pre * sigmoid)).astype(BF)
+        if k + 1 < F:
+            pre_load(k + 1).start()
+        if k == 0:
+            load_i.wait()
+        for j in range(1, S):
+            slab_copy(k, j).wait_send()
+        d = dpre[b]
+        tile = min(512, W)
+        for i in range(W // tile):
+            at = slice(i * tile, (i + 1) * tile)
+            x = outer_cols(d, wi[at, :]).astype(BF).reshape(S, K, tile)
+            for s in range(S):
+                stage[s, b, :, at] = x[s]
+        for j in range(1, S):
+            back_copy(k, j).start()
+        back[b, me] = stage[me, b]
+
+    def gather(k):
+        b = block(k)
+        for j in range(1, S):
+            back_arrival(k, j).wait_recv()
+        chosen = select[b].reshape(S * K, R)
+        tile = min(512, W)
+        for i in range(W // tile):
+            at = slice(i * tile, (i + 1) * tile)
+            total = inner_rows(chosen, back[b, :, :, at].reshape(S * K, tile))
+            if k:
+                pstage[b, :, at] = total.astype(BF)
+            else:
+                part[:, at] = total
+        if k:
+            part_copy(k).start()
+
+    made = []
+
+    def weight_tile(left, right, target, at):
+        n = len(made)
+        slot = n % 2
+        if n >= 2:
+            made[n - 2].wait()
+        width = right.shape[1]
+        tiles[slot, :, 0:width] = inner_rows(left, right)
+        copy = pltpu.make_async_copy(
+            tiles.at[slot, :, pl.ds(0, width)], target.at[pl.ds(at, 256)], tl.at[n]
+        )
+        copy.start()
+        made.append(copy)
+
+    def out_grads(first, last):
+        g = gs[...].reshape(F * S * K, W)
+        for i in range(first, last):
+            left = mixed[:, :, i * 256 : (i + 1) * 256].reshape(F * S * K, 256)
+            weight_tile(left, g, grad_out, i * 256)
+
+    def in_grads(first, last):
+        d = dpre[...].reshape(F * S * K, 2 * FFW)
+        for i in range(first, last):
+            left = ysx[:, :, :, i * 256 : (i + 1) * 256].reshape(F * S * K, 256)
+            weight_tile(left, d, grad_in, i * 256)
+
+    pre_load(0).start()
+    send(0)
+    load_y.wait()
+    gate_grads(0)
+    send(1)
+    gate_grads(1)
+    expert(0)
+    send(2)
+    gate_grads(2)
+    expert(1)
+    for k in range(3, F):
+        send(k)
+        gate_grads(k)
+    load_x.start()
+    gather(0)
+    for k in range(2, F):
+        expert(k)
+        gather(k - 1)
+    out_grads(0, FFW // 256)
+    load_x.wait()
+    in_grads(0, W // 512)
+    gather(F - 1)
+    in_grads(W // 512, W // 256)
+    for k in range(1, F):
+        part_arrival(k).wait_recv()
+        part[...] += zpart[lax.rem(f + k, F)].astype(FL)
+        gate_arrival(k).wait_recv()
+    dgate[...] = dgr[...]
+    for copy in made[-2:]:
+        copy.wait()
+    for copy in z_out:
+        copy.wait_send()
+    for k in range(F):
+        if k:
+            part_copy(k).wait_send()
+            gate_copy(k).wait_send()
+        for j in range(1, S):
+            back_copy(k, j).wait_send()
+
+
+def moe_backward(identity, C, F, T, rows, fgate, select, mixed, w_in, w_out, xr, got, pre):
+    S = C * T
+    K = select.shape[2]
+    R, W = rows.shape
+    H2, FFW = w_in.shape[1], w_out.shape[0]
+    dma = pltpu.SemaphoreType.DMA
+    V = pltpu.VMEM
+    shape = jax.ShapeDtypeStruct
+    return pl.pallas_call(
+        functools.partial(moe_backward_body, C, F, T),
+        out_shape=(
+            shape((R, W), FL), shape((W, H2), FL), shape((FFW, W), FL), shape((F, S, R), FL),
+        ),
+        in_specs=[VMEM] * 4 + [ANY] * 5,
+        out_specs=[VMEM, ANY, ANY, VMEM],
+        scratch_shapes=[
+            V((F, R, W), BF), V((S, F, K, W), BF), V((F, S, K, W), BF), V((F, S, K, W), BF),
+            V((F, S, K, W), BF), V((W, H2), BF), V((FFW, W), BF), V((F, R, W), BF),
+            V((F, R, W), BF), V((F, S * K, H2), BF), V((S * K, H2), FL),
+            V((2, 256, max(W, H2)), FL), V((F, S, R), FL), V((F, S, R), FL),
+            dma((4,)), dma((F,)), dma((F,)), dma((F, S)), dma((F, S)), dma((F, S)), dma((F, S)),
+            dma((F,)), dma((F,)), dma((F,)), dma((F,)), dma((F,)),
+            dma((FFW // 256 + W // 256,)),
+        ],
+        compiler_params=params(identity, 62),
+    )(rows, fgate, select, mixed, w_in, w_out, xr, got, pre)
+
+
 def split_low(values):
     high = lax.reduce_precision(values, 8, 7)
     return high.astype(BF), (values - high).astype(BF)
@@ -1805,25 +2245,32 @@
     )
 
     select = chosen_slots.astype(bf_type)
-    received, _, gate_z = dispatch(2, C, F, T, ffn_low, select, gate_tab)
-    expert_rows = received.reshape(-1, width)
-    both_pre = jnp.dot(expert_rows, w_expert_in[0], preferred_element_type=fl_type)
-    ff_width = w_expert_out.shape[1]
-    gate_pre = both_pre[:, :ff_width]
-    up_pre = both_pre[:, ff_width:]
-    sigmoid_gate = jax.nn.sigmoid(gate_pre)
-    silu_gate = gate_pre * sigmoid_gate
-    mixed_low = (silu_gate * up_pre).astype(bf_type)
-    expert_out = (
-        jnp.dot(mixed_low, w_expert_out[0], preferred_element_type=fl_type)
-        .astype(bf_type)
-        .reshape(S, F, cap, width)
-    )
-    gate_slab = of_slab(gate_z)
-    weigh = jnp.where(chosen_rows, gate_slab[..., None], 0.0).reshape(F, 1, half_rows, S * cap)
-    weigh = jnp.concatenate(split_low(weigh), axis=1)
-    returned, parts = combine(3, C, F, T, expert_out, weigh)
-    output_f = residual + jnp.sum(parts.astype(fl_type), axis=0)
+    if fused:
+        gate_t = jnp.swapaxes(gates, 0, 1)
+        expert_x, returned, both_pre, mixed_low, mixture, gate_z = moe_forward(
+            2, C, F, T, ffn_low, gate_t, select, w_expert_in[0], w_expert_out[0]
+        )
+    else:
+        received, _, gate_z = dispatch(2, C, F, T, ffn_low, select, gate_tab)
+        expert_rows = received.reshape(-1, width)
+        both_pre = jnp.dot(expert_rows, w_expert_in[0], preferred_element_type=fl_type)
+        ff_width = w_expert_out.shape[1]
+        gate_pre = both_pre[:, :ff_width]
+        up_pre = both_pre[:, ff_width:]
+        sigmoid_gate = jax.nn.sigmoid(gate_pre)
+        silu_gate = gate_pre * sigmoid_gate
+        mixed_low = (silu_gate * up_pre).astype(bf_type)
+        expert_out = (
+            jnp.dot(mixed_low, w_expert_out[0], preferred_element_type=fl_type)
+            .astype(bf_type)
+            .reshape(S, F, cap, width)
+        )
+        gate_slab = of_slab(gate_z)
+        weigh = jnp.where(chosen_rows, gate_slab[..., None], 0.0).reshape(F, 1, half_rows, S * cap)
+        weigh = jnp.concatenate(split_low(weigh), axis=1)
+        returned, parts = combine(3, C, F, T, expert_out, weigh)
+        mixture = jnp.sum(parts.astype(fl_type), axis=0)
+    output_f = residual + mixture
     count = jnp.sum(lengths).astype(fl_type)
     tokens_total = lengths.shape[0] * row_count * C
     valid = own_positions < length
@@ -1831,35 +2278,45 @@
     loss_part = jnp.sum(error * error)
     grad_out = error * (tokens_total / count)
 
-    select_gates = jnp.where(
-        chosen_slots, jnp.transpose(gate_slab, (0, 2, 1))[:, :, None, :], 0.0
-    )
-    select_gates = jnp.concatenate(split_low(select_gates), axis=-1)
-    grad_recv, grad_out_z = dispatch(4, C, F, T, grad_out.astype(bf_type), select_gates)
-    slot_grads = jnp.einsum("zskr,zrd->zskd", select, grad_out_z, preferred_element_type=fl_type)
-    slot_gate = jnp.sum(slot_grads * returned.astype(fl_type), axis=-1)
-    gate_grads = jnp.sum(jnp.where(chosen_rows, slot_gate[:, None, :, :], 0.0), axis=-1)
-    gate_grads = jnp.pad(gate_grads, ((0, 0), (0, 0), (0, -S % 128)))
-
-    grad_recv = grad_recv.reshape(-1, width)
-    grad_mixed = outer_cols(grad_recv, w_expert_out[0])
-    grad_expert_out = inner_rows(mixed_low, grad_recv)
-    grad_gate_pre = grad_mixed * up_pre * (sigmoid_gate * (1.0 + gate_pre * (1.0 - sigmoid_gate)))
-    grad_up_pre = grad_mixed * silu_gate
-    grad_pre = jnp.concatenate([grad_gate_pre, grad_up_pre], axis=1).astype(bf_type)
-    grad_expert_in = inner_rows(expert_rows, grad_pre)
-    grad_rows = (
-        outer_cols(grad_pre, w_expert_in[0]).astype(bf_type).reshape(S, F, cap, width)
-    )
-    weigh_one = chosen_rows.astype(bf_type).reshape(F, 1, half_rows, S * cap)
-    _, grad_parts, gate_back = combine(5, C, F, T, grad_rows, weigh_one, gate_grads)
-    grad_gate = jnp.transpose(
-        gate_back[:, :, :S].reshape(F, half_rows, C, T), (1, 2, 0, 3)
-    ).reshape(half_rows, expert_count)
+    if fused:
+        grad_mixture, grad_expert_in, grad_expert_out, gate_back = moe_backward(
+            3, C, F, T, grad_out.astype(bf_type), gate_z, select, mixed_low,
+            w_expert_in[0], w_expert_out[0], expert_x, returned, both_pre,
+        )
+        grad_gate = jnp.transpose(
+            gate_back.reshape(F, C, T, half_rows), (3, 1, 0, 2)
+        ).reshape(half_rows, expert_count)
+    else:
+        select_gates = jnp.where(
+            chosen_slots, jnp.transpose(gate_slab, (0, 2, 1))[:, :, None, :], 0.0
+        )
+        select_gates = jnp.concatenate(split_low(select_gates), axis=-1)
+        grad_recv, grad_out_z = dispatch(4, C, F, T, grad_out.astype(bf_type), select_gates)
+        slot_grads = jnp.einsum("zskr,zrd->zskd", select, grad_out_z, preferred_element_type=fl_type)
+        slot_gate = jnp.sum(slot_grads * returned.astype(fl_type), axis=-1)
+        gate_grads = jnp.sum(jnp.where(chosen_rows, slot_gate[:, None, :, :], 0.0), axis=-1)
+        gate_grads = jnp.pad(gate_grads, ((0, 0), (0, 0), (0, -S % 128)))
+
+        grad_recv = grad_recv.reshape(-1, width)
+        grad_mixed = outer_cols(grad_recv, w_expert_out[0])
+        grad_expert_out = inner_rows(mixed_low, grad_recv)
+        grad_gate_pre = grad_mixed * up_pre * (sigmoid_gate * (1.0 + gate_pre * (1.0 - sigmoid_gate)))
+        grad_up_pre = grad_mixed * silu_gate
+        grad_pre = jnp.concatenate([grad_gate_pre, grad_up_pre], axis=1).astype(bf_type)
+        grad_expert_in = inner_rows(expert_rows, grad_pre)
+        grad_rows = (
+            outer_cols(grad_pre, w_expert_in[0]).astype(bf_type).reshape(S, F, cap, width)
+        )
+        weigh_one = chosen_rows.astype(bf_type).reshape(F, 1, half_rows, S * cap)
+        _, grad_parts, gate_back = combine(5, C, F, T, grad_rows, weigh_one, gate_grads)
+        grad_gate = jnp.transpose(
+            gate_back[:, :, :S].reshape(F, half_rows, C, T), (1, 2, 0, 3)
+        ).reshape(half_rows, expert_count)
+        grad_mixture = jnp.sum(grad_parts.astype(fl_type), axis=0)
     grad_logits = (
         gates * (grad_gate - jnp.sum(gates * grad_gate, axis=-1, keepdims=True))
     ).astype(bf_type)
-    grad_ffn = jnp.sum(grad_parts.astype(fl_type), axis=0) + outer_cols(grad_logits, full_router)
+    grad_ffn = grad_mixture + outer_cols(grad_logits, full_router)
     router_part = inner_rows(ffn_low, grad_logits)
     grad_resid_norm, ffn_gain_terms = norm_back(residual, ffn_factor, ffn_gain, grad_ffn)
     grad_residual = grad_out + grad_resid_norm

time: 763 us -> 708 us (0.928)
  matrix products: 71.7 us -> 5.23 us
  local copies, waits for them, and re-layouts: 17.8 us -> 26.5 us
    dot_general x3 -> x1, matrix products: 24.3 us -> 1.3 us  [inner_rows(): lax.dot_general(left, right, (((0,), (0,)), ((), ())), preferred_element_...]
    dot_general x3 -> x0, matrix products: 22.5 us -> none  [the longest x1 15.2 us: local(): jnp.dot(expert_rows, w_expert_in[0], preferred_element_type=fl_type)]
    dot_general x3 -> x1, matrix products: 24.1 us -> 3.15 us  [outer_cols(): lax.dot_general(left, right, (((1,), (1,)), ((), ())), preferred_element_...]
    unnamed x35 -> x31, local copies, waits for them, and re-layouts: 6.48 us -> 16.6 us
    pallas_call x4 -> x2, Pallas kernels: 328 us -> 330 us  [the longest x1 168 us: moe_forward(): pl.pallas_call(functools.partial(moe_forward_body, C, F, T), out_shape=(s...]
where the time goes in v4:
time: 708 us; the launch traced here: 699 us
  Pallas kernels  638 us (90%)
  local copies, waits for them, and re-layouts  26.5 us (4%)
  other arithmetic  24.8 us (4%)
    pallas_call x1, Pallas kernels, tail(): pl.pallas_call(functools.partial(tail_body, C, F, T, KH), out_shape=(jax....  179 us
    pallas_call x1, Pallas kernels, moe_forward(): pl.pallas_call(functools.partial(moe_forward_body, C, F, T), out_shape=(s...  168 us
    pallas_call x1, Pallas kernels, moe_backward(): pl.pallas_call(functools.partial(moe_backward_body, C, F, T), out_shape=(...  162 us
    pallas_call x1, Pallas kernels, head(): pl.pallas_call(functools.partial(head_body, C, F, T, KH), out_shape=(shap...  128 us
    unnamed x31, local copies, waits for them, and re-layouts  16.6 us

profile of v4, /device:TPU:25, one launch (start us, length us, event | category | flops | bytes accessed | tf_op | source)
XLA Modules:
  0.0 698.6 jit_solution(2610431670624362686)
XLA Ops:
  0.7 1.2 dynamic-slice.16
  2.6 1.2 fusion.4.bias
  5.9 0.9 copy.44
  6.7 3.0 fusion.1.wa
  10.9 128.1 %shard_map.254 = (bf16[2048,2688]{1,0:T(8,128)(2,1)}, bf16[2048,2048]{1,0:T(8,128)(2,1)}, f32[4,128,128]{2,1,0:T(8,128)}, f32[256,2560]{1,0:T(8,128)}, bf16[256,...) custom-call(bf16[256,2048]{1,0:T(8,128)(2,1)} %bitcast.51, ...), custom_call_target="tpu_custom_call" | custom-call | tf_op jit(solution)/shard_map/pallas_call | solution.py:1607
  139.0 1.1 copy.46
  140.9 0.9 copy.45
  142.5 168.3 %shard_map.255 = (bf16[4,8,48,2048]{3,2,1,0:T(8,128)(2,1)}, bf16[4,8,48,2048]{3,2,1,0:T(8,128)(2,1)}, f32[4,384,1536]{2,1,0:T(8,128)}, bf16[4,384,768]{2,1,0:T(8...) custom-call(bf16[128,2048]{1,0:T(8,128)(2,1)} %get-tuple-element.66.rows, f32[32,128]{1,0:T(8,128)} %slice_bitcast_fusion.gate_t, ...), custom_call_target="tpu_custom_call" | custom-call | tf_op jit(solution)/shard_map/pallas_call | solution.py:1803
  310.9 3.0 multiply_reduce_fusion
  315.2 0.9 multiply_convert_fusion.rows
  316.1 162.1 %shard_map.256 = (f32[128,2048]{1,0:T(8,128)}, f32[2048,1536]{1,0:T(8,128)}, f32[768,2048]{1,0:T(8,128)}, f32[4,8,128]{2,1,0:T(8,128)}) custom-call(bf16[128,2048]{1,0:T(8,128)(2,1)} %multiply_convert_fusion.rows, f32[4,32,128]{2,1,0:T(8,128)} %get-tuple-element.70.fgate, bf16[4,8,48,128]{3,2,1,0:T(8,128)(2,1)} %fusion.5.select, ...), custom_call_target="tpu_custom_call" | custom-call | tf_op jit(solution)/shard_map/pallas_call | solution.py:2048
  479.1 3.1 multiply_reduce_fusion.1
  482.3 0.9 scatter.9.vec_in
  483.2 1.3 fusion.13
  484.5 2.4 reshape.156.router
  487.0 2.7 fusion.11
  489.7 2.1 dynamic-slice_convert_fusion.own_in
  491.8 179.1 %shard_map.257 = (f32[128,2048]{1,0:T(8,128)}, bf16[512,2560]{1,0:T(8,128)(2,1)}, bf16[2048,512]{1,0:T(8,128)(2,1)}, f32[16,2048]{1,0:T(8,128)}) custom-call(bf16[128,2048]{1,0:T(8,128)(2,1)} %get-tuple-element.149.grad_own, bf16[256,2048]{1,0:T(8,128)(2,1)} %get-tuple-element.78.heads, bf16[256,2048]{1,0:T(8,128)(2,1)} %get-tuple-element.79.normed, ...), custom_call_target="tpu_custom_call" | custom-call | tf_op jit(solution)/shard_map/pallas_call | solution.py:1281
  670.9 4.3 convert_element_type.63
  675.3 2.6 slice_convert_fusion
  677.8 1.0 slice_convert_fusion.1
  682.0 1.0 copy.55
  683.0 11.3 %copy.56 = f32[1,2048,1536]{2,1,0:T(8,128)} copy(f32[1,2048,1536]{2,1,0:T(8,128)} %bitcast.45) | data formatting | bytes 25165824
  694.3 2.7 copy.57
  (53 shorter events, 8.8 us)
Async XLA Ops:
  0.6 9.1 %copy-start.9 = (s32[1,128,8]{1,2,0:T(8,128)S(1)}, s32[1,128,8]{1,2,0:T(8,128)}, u32[]{:S(2)}) copy-start(s32[1,128,8]{1,2,0:T(8,128)} %param.22) | copy-start | bytes 12292
  142.4 168.4 %copy-start = (f32[128,2048]{1,0:T(8,128)S(1)}, f32[128,2048]{1,0:T(8,128)}, u32[]{:S(2)}) copy-start(f32[128,2048]{1,0:T(8,128)} %get-tuple-element.65) | copy-start | bytes 3145732
  142.5 168.4 %copy-start.5 = (bf16[1,128,2048]{2,1,0:T(8,128)(2,1)S(1)}, bf16[1,128,2048]{2,1,0:T(8,128)(2,1)}, u32[]{:S(2)}) copy-start(bf16[1,128,2048]{2,1,0:T(8,128)(2,1)} %param.20) | copy-start | bytes 1572868
  310.8 3.1 copy-start.10
  316.1 163.0 %copy-start.7 = (f32[2048]{0:T(1024)S(1)}, f32[2048]{0:T(1024)}, u32[]{:S(2)}) copy-start(f32[2048]{0:T(1024)} %param.30) | copy-start | bytes 24580
  478.2 5.0 copy-start.3
  478.2 8.8 %copy-start.1 = (f32[128,2048]{1,0:T(8,128)S(1)}, f32[128,2048]{1,0:T(8,128)}, u32[]{:S(2)}) copy-start(f32[128,2048]{1,0:T(8,128)} %get-tuple-element.65) | copy-start | bytes 3145732
  483.2 8.6 %copy-start.6 = (f32[8,2048]{1,0:T(8,128)}, f32[8,2048]{1,0:T(8,128)S(1)}, u32[]{:S(2)}) copy-start(f32[8,2048]{1,0:T(8,128)S(1)} %scatter.9.vec_in) | copy-start | bytes 196612
  670.9 4.4 copy-start.2
  675.3 3.6 copy-start.8
  675.3 6.8 copy-start.4
  682.0 12.2 %slice-start = ((s8[6291456]{0:T(1024)(128)(4,1)}), s8[4194304]{0:T(1024)(128)(4,1)S(1)}, s32[]{:S(2)}) async-start(s8[6291456]{0:T(1024)(128)(4,1)} %bitcast.48), calls=%async_computation | async-start | bytes 8388608
  683.0 11.3 %slice-start.1 = ((s8[6291456]{0:T(1024)(128)(4,1)}), s8[2097152]{0:T(1024)(128)(4,1)S(1)}, s32[]{:S(2)}) async-start(s8[6291456]{0:T(1024)(128)(4,1)} %bitcast.48), calls=%async_computation.1 | async-start | bytes 4194304

commit v5 on v3

--- a/solution.py
+++ b/solution.py
@@ -10,6 +10,7 @@
 EPS = 1e-06
 ROPE_BASE = 1000000.0
 MASKED = -1e30
+LOG2E = 1.4426950408889634
 AXES = ("ctx", "fsdp", "tp")
 MESH = pl.DeviceIdType.MESH
 ANY = pl.BlockSpec(memory_space=pl.ANY)
@@ -831,17 +832,17 @@
 
 def tail_body(
     C, F, T, KH,
-    grad_own, heads, normed, qrot, kv, keys_t, raw, lse, bias, cosf, sins, qgain, kgain, again,
-    own_in, resid_in, router, vec_in, fo, fall,
+    grad_own, heads, qrot, kv, keys_t, raw, lse, bias, cosf, sins, qgain, kgain, again,
+    own_in, resid_in, router, vec_in, normed, fo, fall,
     gin, outa, outo, small,
     wbuf, dall, nall, hq, rq, dheads, draw, dk, dv, ksend, kgot, gains, nsend, ngot, nown,
-    sza, szo, rza, rzo, smx, zgot, mid, sgot,
-    wsem, xs, xr, as_, ar, hs, hr, ds_, dr, rs, rr, z_s, z_r, ts, tr, us, ur,
+    sza, szo, rza, rzo, smx, zgot, sums, sgot,
+    wsem, xs, xr, as_, ar, hs, hr, ns, nr, gs_, gr, ds_, dr, rs, rr, z_s, z_r, ts, tr, us, ur,
 ):
     c, f, t, me = slab_place(C, T)
     S = C * T
     R, QC = heads.shape
-    W = normed.shape[1]
+    W = grad_own.shape[1]
     PC = raw.shape[1]
     L = kv.shape[1]
     HS = qgain.shape[1]
@@ -922,28 +923,52 @@
         chunk_copies(lambda p, g=g: ksend.at[g, p], lambda o, g=g: kgot.at[g, o], ds_.at[g], dr.at[g])
         for g in range(KH)
     ]
-    def nall_of(p):
-        return nall.at[p]
-
     def outo_of(p):
         return outo.at[lane(p, po)]
 
     def outa_of(p):
         return outa.at[:, lane(p, pa)]
 
-    dall_of = [
-        lambda p, q=q: dall.at[p, :, lane(blocks[q], cols_o)] for q in range(F)
+    def dall_of(q):
+        def view(p, half):
+            at = lane(blocks[q], cols_o)
+            if half is None:
+                return dall.at[p, :, at]
+            return dall.at[p, pl.ds(pl.multiple_of(half * Rh, Rh), Rh), at]
+
+        return view
+
+    d_moves = [
+        row_spread(C, dall_of(q), lambda i, q=q: gs_.at[q, i], lambda i, q=q: gr.at[q, i])
+        for q in range(F)
     ]
 
+    def nall_of(p, half):
+        if half is None:
+            return nall.at[p]
+        return nall.at[p, pl.ds(pl.multiple_of(half * Rh, Rh), Rh)]
+
+    def normed_of(half):
+        if half is None:
+            return normed
+        return normed.at[pl.ds(pl.multiple_of(half * Rh, Rh), Rh)]
+
+    n_start, n_wait, n_drain = row_spread(
+        C, nall_of, lambda i: ns.at[i], lambda i: nr.at[i], normed_of
+    )
+
     swap_d.start()
+    dall[c, at_t] = grad_own[...]
+    for q in range(F):
+        d_moves[q][0](0)
     for copy in heads_out:
         copy.start()
-    dall[c, at_t] = grad_own[...]
+    n_start(0, 1)
+    hq[c] = heads[:, lane(c, po)]
     nall[c] = normed[...]
-    hq[c] = heads[:, lane(c, po)]
     swap_d_in.wait_recv()
     for q in range(F):
-        spread_start(dall_of[q], 3 + q)
+        d_moves[q][0](1)
 
     load_o.wait()
     step = min(512, QC)
@@ -1014,7 +1039,7 @@
             z_send(n, q)
 
     def o_first(q):
-        spread_end(dall_of[q], 3 + q)
+        d_moves[q][1](1, 3, 4)
         if q < F - 1:
             z_first(0, q)
 
@@ -1058,8 +1083,8 @@
         q_grad = jnp.zeros((HS, R), FL)
         for j in range(L // key_step):
             ks = pl.ds(j * key_step, key_step)
-            scores = outer_cols(kv[g, ks, :], q_head) * root
-            probs = jnp.exp(scores + bias[ks, :] - row)
+            scores = outer_cols(kv[g, ks, :], q_head) * (root * LOG2E)
+            probs = jnp.exp2(scores + bias[ks, :] - row)
             d_probs = outer_cols(kv[KH + g, ks, :], o_grad)
             d_scores = (probs * (d_probs - delta)).astype(BF)
             dv[ks, :] += jnp.dot(probs.astype(BF), o_grad, preferred_element_type=FL)
@@ -1099,6 +1124,14 @@
         @pl.when(c == p)
         def _():
             rq[c] = draw[:, p * pa : (p + 1) * pa]
+
+    def d_pass(q):
+        if q == 0:
+            for p in range(F):
+                d_moves[p][1](0)
+                d_moves[p][0](2, 3)
+        d_moves[q][1](2)
+        d_moves[q][0](4)
 
     halves = 2
     part_heads = G // halves
@@ -1118,7 +1151,13 @@
                     copy.start()
                 kgot[g, c] = ksend[g, c]
             if beat < F:
-                spread_pass(dall_of[beat], 3 + beat)
+                d_pass(beat)
+            if beat == 1:
+                n_wait(0)
+                n_start(2, 3)
+            if beat == 2:
+                n_wait(2)
+                n_start(4)
             if beat == 0:
                 for copy in heads_come:
                     copy.wait_recv()
@@ -1126,9 +1165,8 @@
                 o_first(beat - 1)
             beat += 1
     for q in range(beat, F):
-        spread_pass(dall_of[q], 3 + q)
+        d_pass(q)
         o_first(q - 1)
-    spread_start(nall_of, 0)
 
     o_first(F - 1)
     z_relay(0, 0)
@@ -1166,17 +1204,16 @@
 
     lax.fori_loop(0, W // width_step, norm_ours, 0)
 
-    spread_pass(nall_of, 0)
     for q in range(2, F - 1):
         z_relay(0, q)
-    spread_end(nall_of, 0)
+    n_wait(1, 3, 4)
     for k in range(1, C):
         raw_come(lax.rem(c + k, C)).wait_recv()
     for q in range(F - 1):
         z_first(1, q)
     z_relay(1, 0)
     z_last(0)
-    spread_start(outo_of, 1)
+    spread_start(outo_of, 0)
 
     swap_n.wait_recv()
     upstream = nown[...] + ngot[...].astype(FL)
@@ -1204,46 +1241,42 @@
     zgot[f] = smx[f]
     for q in range(1, F - 1):
         z_relay(1, q)
-    spread_pass(outo_of, 1)
+    spread_pass(outo_of, 0)
     for k in range(1, F):
         t_arrival(k).wait_recv()
     total = zgot[0]
     for b in range(1, F):
         total += zgot[b]
-    mid[...] = total
-    sgot[me] = total
-
-    def u_copy(j):
-        return remote(
-            mid, sgot.at[me], us.at[j], ur.at[j], slab_device(lax.rem(me + j, S), f, T)
-        )
-
-    def u_arrival(j):
-        e = lax.rem(me + S - j, S)
-        return remote(mid, sgot.at[e], us.at[j], ur.at[j], slab_device(e, f, T))
-
-    for j in range(1, S):
-        u_copy(j).start()
+    sums[0] = total
+
+    def u_copy(i):
+        there = ((sib, f, t), beside, (mate, f, t))[i]
+        return remote(sums.at[i], sgot.at[i], us.at[i], ur.at[i], there)
+
+    u_copy(0).start()
     z_last(1)
-    spread_start(outa_of, 2)
-    for j in range(1, S):
-        u_arrival(j).wait_recv()
-    total = sgot[0]
-    for e in range(1, S):
-        total += sgot[e]
-    small[...] = total
-    spread_end(outo_of, 1)
-    spread_pass(outa_of, 2)
-    spread_end(outa_of, 2)
-
-    for view, n in ((nall_of, 0), (outo_of, 1), (outa_of, 2)):
+    spread_start(outa_of, 1)
+    for i in range(3):
+        u_copy(i).wait_recv()
+        total = sums[i] + sgot[i]
+        if i < 2:
+            sums[i + 1] = total
+            u_copy(i + 1).start()
+        else:
+            small[...] = total
+    spread_end(outo_of, 0)
+    spread_pass(outa_of, 1)
+    spread_end(outa_of, 1)
+
+    for view, n in ((outo_of, 0), (outa_of, 1)):
         spread_sent(view, n)
     for q in range(F):
-        spread_sent(dall_of[q], 3 + q)
+        d_moves[q][2]()
+    n_drain()
+    for copy in heads_out:
+        copy.wait_send()
     swap_d.wait_send()
     swap_n.wait_send()
-    for copy in heads_out:
-        copy.wait_send()
     for p in range(C):
 
         @pl.when(c != p)
@@ -1258,16 +1291,16 @@
             z_out(n, q).wait_send()
     for k in range(1, F):
         t_copy(k).wait_send()
-    for j in range(1, S):
-        u_copy(j).wait_send()
+    for i in range(3):
+        u_copy(i).wait_send()
 
 
 def tail(identity, C, F, T, KH, args, D, po):
-    grad_own, heads, normed, qrot, kv, keys_t, raw, lse, bias = args[:9]
-    qgain = args[11]
-    router, fall = args[16], args[19]
+    grad_own, heads, qrot, kv, keys_t, raw, lse, bias = args[:8]
+    qgain = args[10]
+    router = args[15]
     R, QC = heads.shape
-    W = normed.shape[1]
+    W = grad_own.shape[1]
     PC = raw.shape[1]
     L = kv.shape[1]
     HS = qgain.shape[1]
@@ -1295,25 +1328,58 @@
             V((Rh, W), BF), V((Rh, W), BF), V((Rh, W), FL),
             V((F, rows_a, pa), BF), V((F, po, cols_o), BF),
             V((F + 1, rows_a, pa), BF), V((F + 1, po, cols_o), BF),
-            V((F,) + small_shape, FL), V((F,) + small_shape, FL), V(small_shape, FL),
-            V((S,) + small_shape, FL),
-            dma((2,)), dma((2,)), dma((2,)), dma((3 + F, 3)), dma((3 + F, 3)), dma((C,)), dma((C,)),
+            V((F,) + small_shape, FL), V((F,) + small_shape, FL), V((3,) + small_shape, FL),
+            V((3,) + small_shape, FL),
+            dma((4,)), dma((2,)), dma((2,)), dma((2, 3)), dma((2, 3)), dma((C,)), dma((C,)), dma((5,)), dma((5,)),
+            dma((F, 5)), dma((F, 5)),
             dma((KH, C)), dma((KH, C)), dma((C,)), dma((C,)),
-            dma((2, F)), dma((2, F + 1)), dma((F,)), dma((F,)), dma((S,)), dma((S,)),
+            dma((2, F)), dma((2, F + 1)), dma((F,)), dma((F,)), dma((3,)), dma((3,)),
         ],
         compiler_params=params(identity, 62),
     )(*args)
 
 
+def row_spread(C, view, sent, got, own=None):
+    c, f, t = place()
+    sib = c + 1 - 2 * lax.rem(c, 2)
+    mate, mate_sib = lax.rem(c + 2, C), lax.rem(sib + 2, C)
+    to_mate, to_sib, to_side = (mate, f, t), (sib, f, t), (c, f, 1 - t)
+    here = (view(c, t), view(c, None))
+    if own is not None:
+        here = (own(t), own(None))
+    leave = (
+        (here[0], view(c, t), to_mate), (here[1], view(c, None), to_sib),
+        (view(mate, t), view(mate, t), to_side), (view(mate, t), view(mate, t), to_sib),
+        (view(mate, 1 - t), view(mate, 1 - t), to_sib),
+    )
+    arrive = (
+        view(mate, t), view(sib, None), view(mate, 1 - t), view(mate_sib, t),
+        view(mate_sib, 1 - t),
+    )
+
+    def start(*which):
+        for i in which:
+            remote(leave[i][0], leave[i][1], sent(i), got(i), leave[i][2]).start()
+
+    def wait(*which):
+        for i in which:
+            remote(arrive[i], arrive[i], sent(i), got(i), to_sib).wait_recv()
+
+    def drain():
+        for i in range(5):
+            remote(leave[i][0], leave[i][1], sent(i), got(i), leave[i][2]).wait_send()
+
+    return start, wait, drain
+
+
 def head_body(
     C, F, T, KH,
-    hidden, tab, again, qgain, kgain, fgain, cosf, sins, bias, wa, wo,
+    hidden, tab, tab_t, again, qgain, kgain, fgain, cosf, sins, bias, wa, wo,
     fall, full, ftab, raw, qrot, kv, keys_t, lse, heads, normed, resid, low, gates,
     fa, fo, vals_t, nsend, ngot, nown,
     loc, zs, zr, ys, yr, ks, kr, ts, tr, cs, cr, xs, xr,
 ):
-    c, f, t, me = slab_place(C, T)
-    S = C * T
+    c, f, t = place()
     R, W = hidden.shape
     Rh = tab.shape[0]
     HS = qgain.shape[1]
@@ -1330,8 +1396,8 @@
     ra, (ro, co) = wa.shape[0], wo.shape
     pa, po = ra // C, ro // C
     ha, ho = pa // 2, po // 2
-    columns = [(c, lax.rem(f + k, F), t) for k in range(1, F)]
-    greet(columns + [slab_device(lax.rem(me + j, S), f, T) for j in range(1, S)])
+    x = Exchange(C, F, T)
+    x.greet()
 
     def spot(arr, b, p):
         half = arr % 2
@@ -1403,9 +1469,7 @@
 
     z_begin(0)
     z_begin(1)
-    tabs = [
-        remote(tab, ftab.at[f], ts.at[k], tr.at[k], columns[k - 1]) for k in range(1, F)
-    ]
+    tabs, tabs_come = x.table_copies(tab_t, ftab, ts, tr)
     for copy in tabs:
         copy.start()
     own_a = pltpu.make_async_copy(wa, fa.at[pl.ds(pl.multiple_of(f * ra, ra), ra)], loc.at[0])
@@ -1414,7 +1478,7 @@
     )
     own_a.start()
     own_o.start()
-    ftab[f] = tab[...]
+    ftab[0, f] = tab_t[...]
 
     inputs = hidden[...].astype(FL)
     normed[...] = norm_rows(inputs, again[...])[0].astype(BF)
@@ -1459,6 +1523,8 @@
         project_in(s - 1)
     y_in(0, F - 1)
     y_in(1, F - 1)
+    z_in(2, 1)
+    z_in(3, 1)
     project_in(F - 1)
 
     def turn(values):
@@ -1485,8 +1551,9 @@
     lax.fori_loop(0, QC // HS, query, 0)
     save_a = pltpu.make_async_copy(fa, fall, loc.at[2])
     save_a.start()
-    z_in(2, 1)
-    z_in(3, 1)
+    y_in(2, 1)
+    y_in(3, 1)
+    z_in(2, 2)
     kv_move(mate, 0, (mate, f, t)).wait_recv()
     kv_move(mate, 2, (sib, f, t)).start()
     kv_move(sib, 1, (sib, f, t)).wait_recv()
@@ -1499,65 +1566,59 @@
         def one_head(i, carry):
             h = first + i
             at = pl.ds(pl.multiple_of(h * HS, HS), HS)
-            scores = outer_cols(kv[g], qrot[:, at]) * root + bias[...]
-            peak = jnp.max(scores, axis=0, keepdims=True)
-            weight = jnp.exp(scores - peak)
+            weight = jnp.exp2(outer_cols(kv[g], qrot[:, at]) * (root * LOG2E) + bias[...])
             total = jnp.sum(weight, axis=0, keepdims=True)
-            lse[pl.ds(h, 1), :] = peak + jnp.log(total)
-            probs = (weight / total).astype(BF)
+            lse[pl.ds(h, 1), :] = jnp.log2(total)
+            probs = (weight * (1.0 / total)).astype(BF)
             heads[:, at] = jnp.dot(vals_t[g], probs, preferred_element_type=FL).T.astype(BF)
             return carry
 
         lax.fori_loop(0, count, one_head, 0)
 
-    o_events = []
-    for s in range(2, F):
-        o_events.append((z_in, 2, s, y_in, 2, s - 1))
-        o_events.append((z_in, 3, s, y_in, 3, s - 1))
-    half = G // 2
-    for i in range(2 * KH):
-        some_heads(i // 2, i * half, half)
-        if i < len(o_events):
-            za, arr_a, sa, ya, arr_b, sb = o_events[i]
-            za(arr_a, sa)
-            ya(arr_b, sb)
-    for za, arr_a, sa, ya, arr_b, sb in o_events[2 * KH :]:
-        za(arr_a, sa)
-        ya(arr_b, sb)
-    y_in(2, F - 1)
-    y_in(3, F - 1)
-    for s in range(1, F):
+    at_t = pl.ds(pl.multiple_of(t * Rh, Rh), Rh)
+    at_u = pl.ds(pl.multiple_of((1 - t) * Rh, Rh), Rh)
+
+    def swap(b):
+        cols = pl.ds(pl.multiple_of(b * co, co), co)
+        return remote(nsend.at[:, cols], ngot.at[:, cols], xs.at[b], xr.at[b], (c, f, 1 - t))
+
+    def output(b):
+        cols = pl.ds(pl.multiple_of(b * co, co), co)
+        nsend[:, cols] = jnp.dot(
+            heads[at_u, :], fo[:, cols], preferred_element_type=FL
+        ).astype(BF)
+        swap(b).start()
+        nown[:, cols] = jnp.dot(heads[at_t, :], fo[:, cols], preferred_element_type=FL)
+
+    def output_in(s):
         for d in range(2):
 
             @pl.when(z_gets(s, d))
             def _():
                 k_in(2, s, d)
                 k_in(3, s, d)
-
+                output(came(s, d))
+
+    events = [[(z_in, 3, 2)], [(y_in, 2, 2)], [(y_in, 3, 2)]]
+    half = G // 2
+    for i in range(2 * KH):
+        some_heads(i // 2, i * half, half)
+        for event, arr, s in events[i] if i < len(events) else ():
+            event(arr, s)
     own_o.wait()
+    output(f)
+    output_in(1)
+    for s in range(3, F):
+        z_in(2, s)
+        z_in(3, s)
+        output_in(s - 1)
+        y_in(2, s)
+        y_in(3, s)
     save_o = pltpu.make_async_copy(fo, full, loc.at[3])
+    output_in(F - 1)
     save_o.start()
-    at_t = pl.ds(pl.multiple_of(t * Rh, Rh), Rh)
-    at_u = pl.ds(pl.multiple_of((1 - t) * Rh, Rh), Rh)
-    step = min(512, W)
-
-    def theirs(i, carry):
-        cols = pl.ds(pl.multiple_of(i * step, step), step)
-        nsend[:, cols] = jnp.dot(
-            heads[at_u, :], fo[:, cols], preferred_element_type=FL
-        ).astype(BF)
-        return carry
-
-    def ours(i, carry):
-        cols = pl.ds(pl.multiple_of(i * step, step), step)
-        nown[:, cols] = jnp.dot(heads[at_t, :], fo[:, cols], preferred_element_type=FL)
-        return carry
-
-    lax.fori_loop(0, W // step, theirs, 0)
-    swap = remote(nsend, ngot, xs.at[0], xr.at[0], (c, f, 1 - t))
-    swap.start()
-    lax.fori_loop(0, W // step, ours, 0)
-    swap.wait_recv()
+    for b in range(F):
+        swap(b).wait_recv()
     total = hidden[at_t, :].astype(FL) + (nown[...] + ngot[...].astype(FL))
     resid[...] = total
     ffn_low = norm_rows(total, fgain[...])[0].astype(BF)
@@ -1572,9 +1633,12 @@
 
     save_a.wait()
     save_o.wait()
-    swap.wait_send()
+    for b in range(F):
+        swap(b).wait_send()
     for copy in tabs:
-        copy.wait()
+        copy.wait_send()
+    for copy in tabs_come:
+        copy.wait_recv()
     kv_move(c, 0, (mate, f, t)).wait_send()
     kv_move(c, 1, (sib, f, t)).wait_send()
     kv_move(mate, 2, (sib, f, t)).wait_send()
@@ -1595,7 +1659,7 @@
 
 
 def head(identity, C, F, T, KH, PC, L, args):
-    hidden, tab, qgain, wa, wo = args[0], args[1], args[3], args[9], args[10]
+    hidden, tab, tab_t, qgain, wa, wo = args[0], args[1], args[2], args[4], args[10], args[11]
     R, W = hidden.shape
     Rh, lanes = tab.shape
     HS = qgain.shape[1]
@@ -1607,22 +1671,758 @@
     return pl.pallas_call(
         functools.partial(head_body, C, F, T, KH),
         out_shape=(
-            shape((F * ra, ca), BF), shape((QC, F * co), BF), shape((F, Rh, lanes), FL),
+            shape((F * ra, ca), BF), shape((QC, F * co), BF), shape((3, F) + tab_t.shape, FL),
             shape((R, PC), FL), shape((R, QC), BF), shape((2 * KH, L, HS), BF),
             shape((KH, HS, L), BF), shape((QC // HS, R), FL), shape((R, QC), BF),
-            shape((R, W), BF), shape((Rh, W), FL), shape((Rh, W), BF), shape((Rh, lanes), FL),
+            shape((R, W), BF), shape((Rh, W), FL), shape((Rh, W), BF),
+            shape((Rh, lanes), FL),
         ),
-        in_specs=[VMEM] * 9 + [ANY] * 2,
+        in_specs=[VMEM] * 10 + [ANY] * 2,
         out_specs=[ANY] * 2 + [VMEM] * 11,
         scratch_shapes=[
             V((F * ra, ca), BF), V((QC, F * co), BF), V((KH, HS, L), BF),
             V((Rh, W), BF), V((Rh, W), BF), V((Rh, W), FL),
             dma((4,)), dma((2, F, 4)), dma((2, F, 4)), dma((2, F, 4, 1)), dma((2, F, 4, 1)),
-            dma((2, F, 4, 2)), dma((2, F, 4, 2)), dma((F,)), dma((F,)), dma((3,)), dma((3,)),
-            dma((1,)), dma((1,)),
+            dma((2, F, 4, 2)), dma((2, F, 4, 2)), dma((3, F)), dma((3, F)), dma((3,)),
+            dma((3,)),
+            dma((F,)), dma((F,)),
         ],
-        compiler_params=params(identity, 58),
+        compiler_params=params(identity, 60),
     )(*args)
+
+
+def block_order(F):
+    if F == 4:
+        return [[0, 1, 3, 2], [1, 2, 3, 0], [2, 1, 0, 3], [3, 2, 0, 1]]
+    return [[(f + k) % F for k in range(F)] for f in range(F)]
+
+
+class Exchange:
+    def __init__(self, C, F, T):
+        c, f, t = place()
+        self.C, self.F, self.T, self.c, self.f, self.t = C, F, T, c, f, t
+        self.chip, self.core = lax.div(c, 2), lax.rem(c, 2)
+        self.mate = lax.rem(c + 2, C)
+        self.unit = self.core * T + t
+        table = block_order(F)
+        self.blocks = []
+        for k in range(F):
+            value = jnp.int32(table[0][k])
+            for g in range(1, F):
+                value = jnp.where(f == g, table[g][k], value)
+            self.blocks.append(value)
+        self.side = ((c, f, 1 - t), (self.mate, f, t))
+        self.own_at = (t, self.chip)
+        self.self_at = (c, self.unit)
+
+    def columns(self):
+        c, f, t, F = self.c, self.f, self.t, self.F
+        own = [(c, lax.rem(f + k, F), t) for k in range(1, F)]
+        beside = [(c, lax.rem(f + k, F), 1 - t) for k in range(F)]
+        across = [(self.mate, lax.rem(f + k, F), t) for k in range(F)]
+        return own, beside, across
+
+    def greet(self):
+        c, f, t, C = self.c, self.f, self.t, self.C
+        own, beside, across = self.columns()
+        rest = [(lax.rem(c + j, C), f, 1 - t) for j in range(1, C)]
+        rest += [(lax.rem(c + j, C), f, t) for j in (1, 3)]
+        greet(own + beside + across + rest)
+
+    def table_copies(self, source, tables, sent, got):
+        out, come = [], []
+        for i, column in enumerate(self.columns()):
+            for n, device in enumerate(column):
+                k = n + 1 if i == 0 else n
+                out.append(remote(source, tables.at[i, self.f], sent.at[i, k], got.at[i, k], device))
+                origin = lax.rem(self.f + self.F - k, self.F)
+                come.append(
+                    remote(source, tables.at[i, origin], sent.at[i, k], got.at[i, k], device)
+                )
+        return out, come
+
+    def target(self, group, j):
+        if group == 0:
+            p = lax.rem(self.c + j, 4)
+            return p, (p, self.f, self.t)
+        p = lax.rem(self.unit + j, 4)
+        return p, (self.chip * 2 + lax.div(p, self.T), self.f, lax.rem(p, self.T))
+
+    def expert_id(self, group, p):
+        if group == 0:
+            return (p * self.F + self.f) * self.T + self.t
+        chip_core = self.chip * 2 + lax.div(p, self.T)
+        return (chip_core * self.F + self.f) * self.T + lax.rem(p, self.T)
+
+    def origin_view(self, buf, group, b, p, H):
+        if group == 0:
+            first = pl.multiple_of(lax.rem(p, 2) * self.T, self.T)
+            return buf.at[b, lax.div(p, 2), pl.ds(first, self.T), :, pl.ds(0, H)]
+        return buf.at[b, :, p, :, pl.ds(H, H)]
+
+    def table_of(self, group, q):
+        own = q == self.own_at[group]
+        return jnp.where(own, 0, 1 + group)
+
+    def one_hot(self, ranks, group, b, q, p, K):
+        row = ranks[self.table_of(group, q), b, pl.ds(self.expert_id(group, p), 1), :]
+        slots = lax.broadcasted_iota(jnp.int32, (K, row.shape[1]), 0).astype(FL)
+        return slots == row
+
+    def gate_row(self, gates, group, b, q, p):
+        return gates[self.table_of(group, q), b, pl.ds(self.expert_id(group, p), 1), :]
+
+    def z_sends(self, s, d):
+        b = self.f - (s - 1) if d == 0 else self.f + (s - 1)
+        if d == 0:
+            return (self.f + 1 < self.F) & (b >= 0)
+        return (self.f > 0) & (b < self.F)
+
+    def z_gets(self, s, d):
+        return self.f - s >= 0 if d == 0 else self.f + s < self.F
+
+    def z_copy(self, zbuf, zs, zr, s, d):
+        b = self.f - (s - 1) if d == 0 else self.f + (s - 1)
+        there = (self.c, self.f + 1 if d == 0 else self.f - 1, self.t)
+        return remote(zbuf.at[b], zbuf.at[b], zs.at[d, s], zr.at[d, s], there)
+
+    def z_begin(self, zbuf, zs, zr):
+        for d in range(2):
+
+            @pl.when(self.z_sends(1, d))
+            def _():
+                self.z_copy(zbuf, zs, zr, 1, d).start()
+
+    def z_relay(self, zbuf, zs, zr, s):
+        for d in range(2):
+
+            @pl.when(self.z_gets(s, d))
+            def _():
+                b = self.f - s if d == 0 else self.f + s
+                remote(
+                    zbuf.at[b], zbuf.at[b], zs.at[d, s], zr.at[d, s], self.side[0]
+                ).wait_recv()
+                if s + 1 < self.F:
+
+                    @pl.when(self.z_sends(s + 1, d))
+                    def _():
+                        self.z_copy(zbuf, zs, zr, s + 1, d).start()
+
+    def z_drain(self, zbuf, zs, zr):
+        for s in range(1, self.F):
+            for d in range(2):
+
+                @pl.when(self.z_sends(s, d))
+                def _():
+                    self.z_copy(zbuf, zs, zr, s, d).wait_send()
+
+
+def moe_forward_body(
+    C, F, T,
+    rows, gate_t, ranks, w_in, w_out,
+    xr, got0, got1, pre, mixed, part, gates,
+    zbuf, dense, st0, st1, xs, gt0, gt1, wi, wo, prebuf, own_part, cross, pstage, zpart,
+    loc, zs, zr, es, er, ss, sr, rs, rr, cs, cr, ps, pr, ts, tr, xl, gl, pl_,
+):
+    x = Exchange(C, F, T)
+    c, f, t = x.c, x.f, x.t
+    K, W = xr.shape[3], xr.shape[4]
+    S, H = C * T, W // 2
+    FFW = w_out.shape[0]
+    stages, gots, keeps = (st0, st1), (gt0, gt1), (got0, got1)
+    x.greet()
+    zbuf[f] = rows[...]
+    x.z_begin(zbuf, zs, zr)
+
+    def dense_copy(k, g):
+        b = x.blocks[k]
+        return remote(
+            zbuf.at[b, :, pl.ds(g * H, H)], dense.at[g, b], es.at[g, k], er.at[g, k], x.side[g]
+        )
+
+    def send_dense(k):
+        for g in range(2):
+            dense_copy(k, g).start()
+
+    send_dense(0)
+    load_i = pltpu.make_async_copy(w_in, wi, loc.at[0])
+    load_o = pltpu.make_async_copy(w_out, wo, loc.at[1])
+    load_i.start()
+    load_o.start()
+    g_out, g_come = x.table_copies(gate_t, gates, ts, tr)
+    for copy in g_out:
+        copy.start()
+    gates[0, f] = gate_t[...]
+
+    def sparse(k, g, j, arriving):
+        b = x.blocks[k]
+        p, device = x.target(g, 4 - j if arriving else j)
+        index = p if arriving else x.self_at[g]
+        return remote(
+            stages[g].at[b, p], x.origin_view(xs, g, b, index, H),
+            ss.at[g, k, j], sr.at[g, k, j], device,
+        )
+
+    def back(k, g, j, arriving):
+        b = x.blocks[k]
+        p, device = x.target(g, 4 - j if arriving else j)
+        index = p if arriving else x.self_at[g]
+        return remote(
+            stages[g].at[b, p], gots[g].at[b, :, index], rs.at[g, k, j], rr.at[g, k, j], device
+        )
+
+    def source(k, g, q):
+        b = x.blocks[k]
+        own = zbuf[b, :, g * H : (g + 1) * H]
+        return jnp.where(q == x.own_at[g], own, dense[g, b])
+
+    def dispatch_rows(k):
+        b = x.blocks[k]
+        for g in range(2):
+            dense_copy(k, g).wait_recv()
+        for j in (2, 1, 3, 0):
+            for g in range(2):
+                p, _ = x.target(g, j)
+                for q in range(2):
+                    hot = x.one_hot(ranks, g, b, q, p, K).astype(BF)
+                    stages[g][b, p, q] = jnp.dot(
+                        hot, source(k, g, q), preferred_element_type=FL
+                    ).astype(BF)
+                if j:
+                    sparse(k, g, j, False).start()
+                else:
+                    x.origin_view(xs, g, b, p, H)[...] = stages[g][b, p]
+
+    def keep_x(k):
+        return pltpu.make_async_copy(xs.at[x.blocks[k]], xr.at[x.blocks[k]], xl.at[k])
+
+    def keep_got(k, g):
+        b = x.blocks[k]
+        return pltpu.make_async_copy(gots[g].at[b], keeps[g].at[b], gl.at[g, k])
+
+    def keep_pre(k):
+        return pltpu.make_async_copy(prebuf, pre.at[x.blocks[k]], pl_.at[k])
+
+    def expert(k):
+        b = x.blocks[k]
+        for j in range(1, 4):
+            for g in range(2):
+                sparse(k, g, j, True).wait_recv()
+        if k == 0:
+            load_i.wait()
+        else:
+            keep_pre(k - 1).wait()
+        keep_x(k).start()
+        left = xs[b].reshape(S * K, W)
+        tile = 256
+        for i in range(FFW // tile):
+            at = slice(i * tile, (i + 1) * tile)
+            up_at = slice(FFW + i * tile, FFW + (i + 1) * tile)
+            gate_pre = jnp.dot(left, wi[:, at], preferred_element_type=FL)
+            up_pre = jnp.dot(left, wi[:, up_at], preferred_element_type=FL)
+            prebuf[:, at] = gate_pre
+            prebuf[:, up_at] = up_pre
+            mixed[b, :, at] = (gate_pre * jax.nn.sigmoid(gate_pre) * up_pre).astype(BF)
+        keep_pre(k).start()
+        if k == 0:
+            load_o.wait()
+        for j in range(1, 4):
+            for g in range(2):
+                sparse(k, g, j, False).wait_send()
+        send_back(k, mixed[b], lambda at: wo[:, at], False)
+
+    def send_back(k, left, right, turned):
+        b = x.blocks[k]
+        tile = min(512, H)
+        for i in range(W // tile):
+            at = slice(i * tile, (i + 1) * tile)
+            y = jnp.dot(left, right(at), preferred_element_type=FL).astype(BF)
+            y = y.reshape(2, 4, K, tile)
+            for chip in range(2):
+                for unit in range(4):
+                    if i * tile < H:
+                        st0[b, chip * 2 + unit // T, unit % T, :, at] = y[chip, unit]
+                    else:
+                        cols = slice(i * tile - H, (i + 1) * tile - H)
+                        st1[b, unit, chip, :, cols] = y[chip, unit]
+            if (i + 1) * tile in (H, W):
+                g = 0 if (i + 1) * tile == H else 1
+                for j in (2, 1, 3):
+                    back(k, g, j, False).start()
+                me = x.self_at[g]
+                for q in range(2):
+                    gots[g][b, q, me] = stages[g][b, me, q]
+
+    def cross_copy(k, g):
+        b = x.blocks[k]
+        return remote(pstage.at[b, :, pl.ds(g * H, H)], cross.at[g, b], cs.at[g, k], cr.at[g, k], x.side[g])
+
+    def gather(k):
+        b = x.blocks[k]
+        for g in range(2):
+            for j in range(1, 4):
+                back(k, g, j, True).wait_recv()
+            keep_got(k, g).start()
+            for near in range(2):
+                q = x.own_at[g] if near else 1 - x.own_at[g]
+                scaled = []
+                for p in range(4):
+                    hot = x.one_hot(ranks, g, b, q, p, K)
+                    scaled.append(jnp.where(hot, x.gate_row(gates, g, b, q, p), 0.0))
+                scaled = jnp.concatenate(scaled, axis=0)
+                high = scaled.astype(BF)
+                low = (scaled - high.astype(FL)).astype(BF)
+                tile = min(512, H)
+                for i in range(H // tile):
+                    at = slice(i * tile, (i + 1) * tile)
+                    out_at = slice(g * H + i * tile, g * H + (i + 1) * tile)
+                    y = gots[g][b, q, :, :, at].reshape(4 * K, tile)
+                    total = inner_rows(high, y) + inner_rows(low, y)
+                    if near:
+                        own_part[k % 2, :, out_at] = total
+                    else:
+                        pstage[b, :, out_at] = total.astype(BF)
+                if not near:
+                    cross_copy(k, g).start()
+
+    def part_copy(k):
+        b = x.blocks[k]
+        return remote(pstage.at[b], zpart.at[f], ps.at[b], pr.at[f], (c, b, t))
+
+    def part_arrival(k):
+        b = x.blocks[k]
+        return remote(pstage.at[b], zpart.at[b], ps.at[b], pr.at[b], (c, b, t))
+
+    def finish(k):
+        b = x.blocks[k]
+        for g in range(2):
+            cross_copy(k, g).wait_recv()
+            cross_copy(k, g).wait_send()
+            at = slice(g * H, (g + 1) * H)
+            total = own_part[k % 2, :, at] + cross[g, b].astype(FL)
+            if k:
+                pstage[b, :, at] = total.astype(BF)
+            else:
+                part[:, at] = total
+        if k:
+            part_copy(k).start()
+
+    dispatch_rows(0)
+    x.z_relay(zbuf, zs, zr, 1)
+    send_dense(1)
+    expert(0)
+    dispatch_rows(1)
+    for s in range(2, F):
+        x.z_relay(zbuf, zs, zr, s)
+    for k in range(2, F):
+        send_dense(k)
+    for copy in g_out:
+        copy.wait_send()
+    for copy in g_come:
+        copy.wait_recv()
+    expert(1)
+    dispatch_rows(2)
+    gather(0)
+    dispatch_rows(3)
+    expert(2)
+    gather(1)
+    finish(0)
+    expert(3)
+    finish(1)
+    gather(2)
+    gather(3)
+    finish(2)
+    finish(3)
+    for k in range(1, F):
+        part_arrival(k).wait_recv()
+        part[...] += zpart[x.blocks[k]].astype(FL)
+    x.z_drain(zbuf, zs, zr)
+    keep_pre(F - 1).wait()
+    for k in range(F):
+        keep_x(k).wait()
+        if k:
+            part_copy(k).wait_send()
+        for g in range(2):
+            keep_got(k, g).wait()
+            dense_copy(k, g).wait_send()
+            for j in range(1, 4):
+                back(k, g, j, False).wait_send()
+
+
+def moe_forward(identity, C, F, T, K, rows, gate_t, ranks, w_in, w_out):
+    S = C * T
+    R, W = rows.shape
+    H = W // 2
+    H2, FFW = w_in.shape[1], w_out.shape[0]
+    dma = pltpu.SemaphoreType.DMA
+    V = pltpu.VMEM
+    shape = jax.ShapeDtypeStruct
+    return pl.pallas_call(
+        functools.partial(moe_forward_body, C, F, T),
+        out_shape=(
+            shape((F, 2, 4, K, W), BF), shape((F, 2, 4, K, H), BF), shape((F, 2, 4, K, H), BF),
+            shape((F, S * K, H2), FL), shape((F, S * K, FFW), BF), shape((R, W), FL),
+            shape((3, F) + gate_t.shape, FL),
+        ),
+        in_specs=[VMEM] * 3 + [ANY] * 2,
+        out_specs=[ANY] * 4 + [VMEM] * 3,
+        scratch_shapes=[
+            V((F, R, W), BF), V((2, F, R, H), BF), V((F, 4, 2, K, H), BF), V((F, 4, 2, K, H), BF),
+            V((F, 2, 4, K, W), BF), V((F, 2, 4, K, H), BF), V((F, 2, 4, K, H), BF),
+            V((W, H2), BF), V((FFW, W), BF), V((S * K, H2), FL), V((2, R, W), FL),
+            V((2, F, R, H), BF), V((F, R, W), BF), V((F, R, W), BF),
+            dma((2,)), dma((2, F)), dma((2, F)), dma((2, F)), dma((2, F)), dma((2, F, 4)),
+            dma((2, F, 4)), dma((2, F, 4)), dma((2, F, 4)), dma((2, F)), dma((2, F)), dma((F,)),
+            dma((F,)), dma((3, F)), dma((3, F)), dma((F,)), dma((2, F)), dma((F,)),
+        ],
+        compiler_params=params(identity, 61),
+    )(rows, gate_t, ranks, w_in, w_out)
+
+
+def moe_backward_body(
+    C, F, T,
+    gates, ranks, mixed, rows, w_in, w_out, xr, got0, got1, pre,
+    part, grad_in, grad_out, dgr0, dgr1,
+    zbuf, dense, st0, st1, xs, gt0, gt1, ysx, wi, wo, dpre, prebuf, tiles, own_part, cross,
+    pstage, zpart, dgs,
+    loc, zs, zr, es, er, ss, sr, rs, rr, cs, cr, ps, pr, ds_, dr, pl_, tl,
+):
+    x = Exchange(C, F, T)
+    c, f, t = x.c, x.f, x.t
+    K, W = xr.shape[3], xr.shape[4]
+    S, H = C * T, W // 2
+    FFW = w_out.shape[0]
+    R = rows.shape[0]
+    stages, gots, gate_in = (st0, st1), (gt0, gt1), (dgr0, dgr1)
+    load_r = pltpu.make_async_copy(rows, zbuf.at[f], loc.at[5])
+    load_r.start()
+    x.greet()
+    load_r.wait()
+    x.z_begin(zbuf, zs, zr)
+
+    def dense_copy(k, g):
+        b = x.blocks[k]
+        return remote(
+            zbuf.at[b, :, pl.ds(g * H, H)], dense.at[g, b], es.at[g, k], er.at[g, k], x.side[g]
+        )
+
+    def send_dense(k):
+        for g in range(2):
+            dense_copy(k, g).start()
+
+    send_dense(0)
+    load_y = [
+        pltpu.make_async_copy(got, ysx.at[:, :, :, :, pl.ds(g * H, H)], loc.at[g])
+        for g, got in enumerate((got0, got1))
+    ]
+    load_o = pltpu.make_async_copy(w_out, wo, loc.at[2])
+    load_i = pltpu.make_async_copy(w_in, wi, loc.at[3])
+    load_x = pltpu.make_async_copy(xr, ysx, loc.at[4])
+    for copy in load_y:
+        copy.start()
+    load_o.start()
+    load_i.start()
+
+    def pre_load(k):
+        return pltpu.make_async_copy(pre.at[x.blocks[k]], prebuf, pl_.at[k])
+
+    pre_load(0).start()
+
+    def sparse(k, g, j, arriving):
+        b = x.blocks[k]
+        p, device = x.target(g, 4 - j if arriving else j)
+        index = p if arriving else x.self_at[g]
+        return remote(
+            stages[g].at[b, p], x.origin_view(xs, g, b, index, H),
+            ss.at[g, k, j], sr.at[g, k, j], device,
+        )
+
+    def back(k, g, j, arriving):
+        b = x.blocks[k]
+        p, device = x.target(g, 4 - j if arriving else j)
+        index = p if arriving else x.self_at[g]
+        return remote(
+            stages[g].at[b, p], gots[g].at[b, :, index], rs.at[g, k, j], rr.at[g, k, j], device
+        )
+
+    def source(k, g, q):
+        b = x.blocks[k]
+        own = zbuf[b, :, g * H : (g + 1) * H]
+        return jnp.where(q == x.own_at[g], own, dense[g, b])
+
+    def dispatch_rows(k):
+        b = x.blocks[k]
+        for g in range(2):
+            dense_copy(k, g).wait_recv()
+        for j in (2, 1, 3, 0):
+            for g in range(2):
+                p, _ = x.target(g, j)
+                for q in range(2):
+                    hot = x.one_hot(ranks, g, b, q, p, K)
+                    gate = jnp.sum(
+                        jnp.where(hot, x.gate_row(gates, g, b, q, p), 0.0), axis=1, keepdims=True
+                    )
+                    picked = jnp.dot(
+                        hot.astype(BF), source(k, g, q), preferred_element_type=FL
+                    )
+                    stages[g][b, p, q] = (picked * gate).astype(BF)
+                if j:
+                    sparse(k, g, j, False).start()
+                else:
+                    x.origin_view(xs, g, b, p, H)[...] = stages[g][b, p]
+
+    lanes = lax.broadcasted_iota(jnp.int32, (K, R), 1)
+
+    def gate_copy(k, g, near):
+        b = x.blocks[k]
+        q = x.own_at[g] if near else 1 - x.own_at[g]
+        side = (c, b, 1 - t) if g == 0 else (x.mate, b, t)
+        device = (c, b, t) if near else side
+        return remote(
+            dgs.at[g, q, b], gate_in[g].at[x.own_at[g], f],
+            ds_.at[g, 1 - near, b], dr.at[g, 1 - near, f], device,
+        )
+
+    def gate_arrival(k, g, near):
+        b = x.blocks[k]
+        q = x.own_at[g] if near else 1 - x.own_at[g]
+        return remote(
+            dgs.at[g, q, b], gate_in[g].at[q, b],
+            ds_.at[g, 1 - near, b], dr.at[g, 1 - near, b], x.side[g],
+        )
+
+    def gate_grads(k):
+        b = x.blocks[k]
+        for g in range(2):
+            for near in range(2):
+                q = x.own_at[g] if near else 1 - x.own_at[g]
+                total = jnp.zeros((R, R), FL)
+                rows_q = zbuf[b, :, g * H : (g + 1) * H] if near else dense[g, b]
+                for p in range(4):
+                    hot = x.one_hot(ranks, g, b, q, p, K).astype(BF)
+                    picked = jnp.dot(hot, rows_q, preferred_element_type=FL)
+                    y = ysx[b, q, p, :, g * H : (g + 1) * H].astype(FL)
+                    dots = jnp.sum(picked * y, axis=1, keepdims=True)
+                    spread = jnp.where(lanes == p, dots, 0.0)
+                    high = spread.astype(BF)
+                    low = (spread - high.astype(FL)).astype(BF)
+                    total += inner_rows(high, hot) + inner_rows(low, hot)
+                if near and k == 0:
+                    gate_in[g][q, b] = total[:8, :]
+                else:
+                    dgs[g, q, b] = total[:8, :]
+                    gate_copy(k, g, near).start()
+
+    def expert(k):
+        b = x.blocks[k]
+        for j in range(1, 4):
+            for g in range(2):
+                sparse(k, g, j, True).wait_recv()
+        if k == 0:
+            load_o.wait()
+        left = xs[b].reshape(S * K, W)
+        pre_load(k).wait()
+        tile = 256
+        for i in range(FFW // tile):
+            at = slice(i * tile, (i + 1) * tile)
+            up_at = slice(FFW + i * tile, FFW + (i + 1) * tile)
+            grad_mixed = outer_cols(left, wo[at, :])
+            gate_pre = prebuf[:, at]
+            up_pre = prebuf[:, up_at]
+            sigmoid = jax.nn.sigmoid(gate_pre)
+            dpre[b, :, at] = (
+                grad_mixed * up_pre * (sigmoid * (1.0 + gate_pre * (1.0 - sigmoid)))
+            ).astype(BF)
+            dpre[b, :, up_at] = (grad_mixed * (gate_pre * sigmoid)).astype(BF)
+        if k + 1 < F:
+            pre_load(k + 1).start()
+        if k == 0:
+            load_i.wait()
+        for j in range(1, 4):
+            for g in range(2):
+                sparse(k, g, j, False).wait_send()
+        d = dpre[b]
+        tile = min(512, H)
+        for i in range(W // tile):
+            at = slice(i * tile, (i + 1) * tile)
+            y = outer_cols(d, wi[at, :]).astype(BF).reshape(2, 4, K, tile)
+            for chip in range(2):
+                for unit in range(4):
+                    if i * tile < H:
+                        st0[b, chip * 2 + unit // T, unit % T, :, at] = y[chip, unit]
+                    else:
+                        cols = slice(i * tile - H, (i + 1) * tile - H)
+                        st1[b, unit, chip, :, cols] = y[chip, unit]
+            if (i + 1) * tile in (H, W):
+                g = 0 if (i + 1) * tile == H else 1
+                for j in (2, 1, 3):
+                    back(k, g, j, False).start()
+                me = x.self_at[g]
+                for q in range(2):
+                    gots[g][b, q, me] = stages[g][b, me, q]
+
+    def cross_copy(k, g):
+        b = x.blocks[k]
+        return remote(pstage.at[b, :, pl.ds(g * H, H)], cross.at[g, b], cs.at[g, k], cr.at[g, k], x.side[g])
+
+    def gather(k):
+        b = x.blocks[k]
+        for g in range(2):
+            for j in range(1, 4):
+                back(k, g, j, True).wait_recv()
+            for near in range(2):
+                q = x.own_at[g] if near else 1 - x.own_at[g]
+                hot = jnp.concatenate(
+                    [x.one_hot(ranks, g, b, q, p, K).astype(FL) for p in range(4)], axis=0
+                ).astype(BF)
+                tile = min(512, H)
+                for i in range(H // tile):
+                    at = slice(i * tile, (i + 1) * tile)
+                    out_at = slice(g * H + i * tile, g * H + (i + 1) * tile)
+                    total = inner_rows(hot, gots[g][b, q, :, :, at].reshape(4 * K, tile))
+                    if near:
+                        own_part[:, out_at] = total
+                    else:
+                        pstage[b, :, out_at] = total.astype(BF)
+                if not near:
+                    cross_copy(k, g).start()
+
+    def part_copy(k):
+        b = x.blocks[k]
+        return remote(pstage.at[b], zpart.at[f], ps.at[b], pr.at[f], (c, b, t))
+
+    def part_arrival(k):
+        b = x.blocks[k]
+        return remote(pstage.at[b], zpart.at[b], ps.at[b], pr.at[b], (c, b, t))
+
+    def finish(k):
+        b = x.blocks[k]
+        for g in range(2):
+            cross_copy(k, g).wait_recv()
+            cross_copy(k, g).wait_send()
+            at = slice(g * H, (g + 1) * H)
+            total = own_part[:, at] + cross[g, b].astype(FL)
+            if k:
+                pstage[b, :, at] = total.astype(BF)
+            else:
+                part[:, at] = total
+        if k:
+            part_copy(k).start()
+
+    made = []
+
+    def weight_tile(left, right, target, at):
+        width = right.shape[1] // 2
+        for half in range(2):
+            n = len(made)
+            if n >= 2:
+                made[n - 2].wait()
+            cols = slice(half * width, (half + 1) * width)
+            tiles[n % 2, :, 0:width] = inner_rows(left, right[:, cols]).astype(BF)
+            copy = pltpu.make_async_copy(
+                tiles.at[n % 2, :, pl.ds(0, width)],
+                target.at[pl.ds(at, 256), pl.ds(half * width, width)],
+                tl.at[n],
+            )
+            copy.start()
+            made.append(copy)
+
+    def out_grads(first, last):
+        g = xs[...].reshape(F * S * K, W)
+        for i in range(first, last):
+            left = mixed[:, :, i * 256 : (i + 1) * 256].reshape(F * S * K, 256)
+            weight_tile(left, g, grad_out, i * 256)
+
+    def in_grads(first, last):
+        d = dpre[...].reshape(F * S * K, 2 * FFW)
+        for i in range(first, last):
+            left = ysx[:, :, :, :, i * 256 : (i + 1) * 256].reshape(F * S * K, 256)
+            weight_tile(left, d, grad_in, i * 256)
+
+    dispatch_rows(0)
+    x.z_relay(zbuf, zs, zr, 1)
+    send_dense(1)
+    for copy in load_y:
+        copy.wait()
+    gate_grads(0)
+    expert(0)
+    dispatch_rows(1)
+    for s in range(2, F):
+        x.z_relay(zbuf, zs, zr, s)
+    for k in range(2, F):
+        send_dense(k)
+    gate_grads(1)
+    expert(1)
+    dispatch_rows(2)
+    gather(0)
+    dispatch_rows(3)
+    gate_grads(2)
+    expert(2)
+    finish(0)
+    gather(1)
+    gate_grads(3)
+    load_x.start()
+    expert(3)
+    finish(1)
+    gather(2)
+    out_grads(0, FFW // 256)
+    finish(2)
+    gather(3)
+    load_x.wait()
+    in_grads(0, 1)
+    finish(3)
+    in_grads(1, W // 256)
+    for k in range(1, F):
+        part_arrival(k).wait_recv()
+        part[...] += zpart[x.blocks[k]].astype(FL)
+    for k in range(F):
+        for g in range(2):
+            for near in range(2):
+                if k or not near:
+                    gate_arrival(k, g, near).wait_recv()
+                    gate_copy(k, g, near).wait_send()
+    for copy in made[-2:]:
+        copy.wait()
+    x.z_drain(zbuf, zs, zr)
+    for k in range(F):
+        if k:
+            part_copy(k).wait_send()
+        for g in range(2):
+            dense_copy(k, g).wait_send()
+            for j in range(1, 4):
+                back(k, g, j, False).wait_send()
+
+
+def moe_backward(identity, C, F, T, rows, gates, ranks, mixed, w_in, w_out, xr, got0, got1, pre):
+    S = C * T
+    K = xr.shape[3]
+    R, W = rows.shape
+    H = W // 2
+    H2, FFW = w_in.shape[1], w_out.shape[0]
+    dma = pltpu.SemaphoreType.DMA
+    V = pltpu.VMEM
+    shape = jax.ShapeDtypeStruct
+    return pl.pallas_call(
+        functools.partial(moe_backward_body, C, F, T),
+        out_shape=(
+            shape((R, W), FL), shape((W, H2), BF), shape((FFW, W), BF),
+            shape((2, F, 8, R), FL), shape((2, F, 8, R), FL),
+        ),
+        in_specs=[VMEM] * 3 + [ANY] * 7,
+        out_specs=[VMEM, ANY, ANY, VMEM, VMEM],
+        scratch_shapes=[
+            V((F, R, W), BF), V((2, F, R, H), BF), V((F, 4, 2, K, H), BF), V((F, 4, 2, K, H), BF),
+            V((F, 2, 4, K, W), BF), V((F, 2, 4, K, H), BF), V((F, 2, 4, K, H), BF),
+            V((F, 2, 4, K, W), BF), V((W, H2), BF), V((FFW, W), BF), V((F, S * K, H2), BF),
+            V((S * K, H2), FL), V((2, 256, max(W, H2) // 2), BF), V((R, W), FL),
+            V((2, F, R, H), BF), V((F, R, W), BF), V((F, R, W), BF), V((2, 2, F, 8, R), FL),
+            dma((6,)), dma((2, F)), dma((2, F)), dma((2, F)), dma((2, F)), dma((2, F, 4)),
+            dma((2, F, 4)), dma((2, F, 4)), dma((2, F, 4)), dma((2, F)), dma((2, F)), dma((F,)),
+            dma((F,)), dma((2, 2, F)), dma((2, 2, F)), dma((F,)),
+            dma((2 * (FFW // 256 + W // 256),)),
+        ],
+        compiler_params=params(identity, 63.5),
+    )(gates, ranks, mixed, rows, w_in, w_out, xr, got0, got1, pre)
 
 
 def split_low(values):
@@ -1701,7 +2501,7 @@
         ) = head(
             1, C, F, T, kv_heads, proj_cols, total_len,
             (
-                hidden_in[0], rank_tab, attn_gain[None], query_gain[None], key_gain[None],
+                hidden_in[0], rank_tab, rank_tab[:, :expert_count].T, attn_gain[None], query_gain[None], key_gain[None],
                 ffn_gain[None], cos_full, sin_signed, bias, w_all, w_output,
             ),
         )
@@ -1793,37 +2593,44 @@
         gates = shifted / jnp.sum(shifted, axis=-1, keepdims=True)
         gate_tab = jnp.pad(gates, ((0, 0), (0, lanes - expert_count)))
 
-    def of_slab(table):
-        picked = table[:, :, :expert_count].reshape(F, half_rows, C, F, T)
-        return lax.dynamic_index_in_dim(picked, f, 3, keepdims=False).reshape(F, half_rows, S)
-
-    rank_slab = of_slab(rank_z)
-    slot_ids = jnp.arange(cap, dtype=fl_type)
-    chosen_rows = rank_slab[:, :, :, None] == slot_ids
-    chosen_slots = (
-        jnp.transpose(rank_slab, (0, 2, 1))[:, :, None, :] == slot_ids[:, None]
-    )
-
-    select = chosen_slots.astype(bf_type)
-    received, _, gate_z = dispatch(2, C, F, T, ffn_low, select, gate_tab)
-    expert_rows = received.reshape(-1, width)
-    both_pre = jnp.dot(expert_rows, w_expert_in[0], preferred_element_type=fl_type)
-    ff_width = w_expert_out.shape[1]
-    gate_pre = both_pre[:, :ff_width]
-    up_pre = both_pre[:, ff_width:]
-    sigmoid_gate = jax.nn.sigmoid(gate_pre)
-    silu_gate = gate_pre * sigmoid_gate
-    mixed_low = (silu_gate * up_pre).astype(bf_type)
-    expert_out = (
-        jnp.dot(mixed_low, w_expert_out[0], preferred_element_type=fl_type)
-        .astype(bf_type)
-        .reshape(S, F, cap, width)
-    )
-    gate_slab = of_slab(gate_z)
-    weigh = jnp.where(chosen_rows, gate_slab[..., None], 0.0).reshape(F, 1, half_rows, S * cap)
-    weigh = jnp.concatenate(split_low(weigh), axis=1)
-    returned, parts = combine(3, C, F, T, expert_out, weigh)
-    output_f = residual + jnp.sum(parts.astype(fl_type), axis=0)
+    if fused:
+        gate_t = jnp.swapaxes(gates, 0, 1)
+        expert_x, got_0, got_1, both_pre, mixed_low, mixture, gate_z = moe_forward(
+            2, C, F, T, cap, ffn_low, gate_t, rank_z, w_expert_in[0], w_expert_out[0]
+        )
+    else:
+        def of_slab(table):
+            picked = table[:, :, :expert_count].reshape(F, half_rows, C, F, T)
+            return lax.dynamic_index_in_dim(picked, f, 3, keepdims=False).reshape(F, half_rows, S)
+
+        rank_slab = of_slab(rank_z)
+        slot_ids = jnp.arange(cap, dtype=fl_type)
+        chosen_rows = rank_slab[:, :, :, None] == slot_ids
+        chosen_slots = (
+            jnp.transpose(rank_slab, (0, 2, 1))[:, :, None, :] == slot_ids[:, None]
+        )
+
+        select = chosen_slots.astype(bf_type)
+        received, _, gate_z = dispatch(2, C, F, T, ffn_low, select, gate_tab)
+        expert_rows = received.reshape(-1, width)
+        both_pre = jnp.dot(expert_rows, w_expert_in[0], preferred_element_type=fl_type)
+        ff_width = w_expert_out.shape[1]
+        gate_pre = both_pre[:, :ff_width]
+        up_pre = both_pre[:, ff_width:]
+        sigmoid_gate = jax.nn.sigmoid(gate_pre)
+        silu_gate = gate_pre * sigmoid_gate
+        mixed_low = (silu_gate * up_pre).astype(bf_type)
+        expert_out = (
+            jnp.dot(mixed_low, w_expert_out[0], preferred_element_type=fl_type)
+            .astype(bf_type)
+            .reshape(S, F, cap, width)
+        )
+        gate_slab = of_slab(gate_z)
+        weigh = jnp.where(chosen_rows, gate_slab[..., None], 0.0).reshape(F, 1, half_rows, S * cap)
+        weigh = jnp.concatenate(split_low(weigh), axis=1)
+        returned, parts = combine(3, C, F, T, expert_out, weigh)
+        mixture = jnp.sum(parts.astype(fl_type), axis=0)
+    output_f = residual + mixture
     count = jnp.sum(lengths).astype(fl_type)
     tokens_total = lengths.shape[0] * row_count * C
     valid = own_positions < length
@@ -1831,35 +2638,46 @@
     loss_part = jnp.sum(error * error)
     grad_out = error * (tokens_total / count)
 
-    select_gates = jnp.where(
-        chosen_slots, jnp.transpose(gate_slab, (0, 2, 1))[:, :, None, :], 0.0
-    )
-    select_gates = jnp.concatenate(split_low(select_gates), axis=-1)
-    grad_recv, grad_out_z = dispatch(4, C, F, T, grad_out.astype(bf_type), select_gates)
-    slot_grads = jnp.einsum("zskr,zrd->zskd", select, grad_out_z, preferred_element_type=fl_type)
-    slot_gate = jnp.sum(slot_grads * returned.astype(fl_type), axis=-1)
-    gate_grads = jnp.sum(jnp.where(chosen_rows, slot_gate[:, None, :, :], 0.0), axis=-1)
-    gate_grads = jnp.pad(gate_grads, ((0, 0), (0, 0), (0, -S % 128)))
-
-    grad_recv = grad_recv.reshape(-1, width)
-    grad_mixed = outer_cols(grad_recv, w_expert_out[0])
-    grad_expert_out = inner_rows(mixed_low, grad_recv)
-    grad_gate_pre = grad_mixed * up_pre * (sigmoid_gate * (1.0 + gate_pre * (1.0 - sigmoid_gate)))
-    grad_up_pre = grad_mixed * silu_gate
-    grad_pre = jnp.concatenate([grad_gate_pre, grad_up_pre], axis=1).astype(bf_type)
-    grad_expert_in = inner_rows(expert_rows, grad_pre)
-    grad_rows = (
-        outer_cols(grad_pre, w_expert_in[0]).astype(bf_type).reshape(S, F, cap, width)
-    )
-    weigh_one = chosen_rows.astype(bf_type).reshape(F, 1, half_rows, S * cap)
-    _, grad_parts, gate_back = combine(5, C, F, T, grad_rows, weigh_one, gate_grads)
-    grad_gate = jnp.transpose(
-        gate_back[:, :, :S].reshape(F, half_rows, C, T), (1, 2, 0, 3)
-    ).reshape(half_rows, expert_count)
+    if fused:
+        grad_mixture, grad_expert_in, grad_expert_out, back_0, back_1 = moe_backward(
+            3, C, F, T, grad_out.astype(bf_type), gate_z, rank_z, mixed_low,
+            w_expert_in[0], w_expert_out[0], expert_x, got_0, got_1, both_pre,
+        )
+        back_0 = jnp.transpose(back_0[:, :, :C], (3, 2, 1, 0))
+        back_1 = back_1[:, :, : 2 * T].reshape(2, F, 2, T, half_rows)
+        back_1 = jnp.transpose(back_1, (4, 0, 2, 1, 3)).reshape(half_rows, C, F, T)
+        grad_gate = (back_0 + back_1).reshape(half_rows, expert_count)
+    else:
+        select_gates = jnp.where(
+            chosen_slots, jnp.transpose(gate_slab, (0, 2, 1))[:, :, None, :], 0.0
+        )
+        select_gates = jnp.concatenate(split_low(select_gates), axis=-1)
+        grad_recv, grad_out_z = dispatch(4, C, F, T, grad_out.astype(bf_type), select_gates)
+        slot_grads = jnp.einsum("zskr,zrd->zskd", select, grad_out_z, preferred_element_type=fl_type)
+        slot_gate = jnp.sum(slot_grads * returned.astype(fl_type), axis=-1)
+        gate_grads = jnp.sum(jnp.where(chosen_rows, slot_gate[:, None, :, :], 0.0), axis=-1)
+        gate_grads = jnp.pad(gate_grads, ((0, 0), (0, 0), (0, -S % 128)))
+
+        grad_recv = grad_recv.reshape(-1, width)
+        grad_mixed = outer_cols(grad_recv, w_expert_out[0])
+        grad_expert_out = inner_rows(mixed_low, grad_recv)
+        grad_gate_pre = grad_mixed * up_pre * (sigmoid_gate * (1.0 + gate_pre * (1.0 - sigmoid_gate)))
+        grad_up_pre = grad_mixed * silu_gate
+        grad_pre = jnp.concatenate([grad_gate_pre, grad_up_pre], axis=1).astype(bf_type)
+        grad_expert_in = inner_rows(expert_rows, grad_pre)
+        grad_rows = (
+            outer_cols(grad_pre, w_expert_in[0]).astype(bf_type).reshape(S, F, cap, width)
+        )
+        weigh_one = chosen_rows.astype(bf_type).reshape(F, 1, half_rows, S * cap)
+        _, grad_parts, gate_back = combine(5, C, F, T, grad_rows, weigh_one, gate_grads)
+        grad_gate = jnp.transpose(
+            gate_back[:, :, :S].reshape(F, half_rows, C, T), (1, 2, 0, 3)
+        ).reshape(half_rows, expert_count)
+        grad_mixture = jnp.sum(grad_parts.astype(fl_type), axis=0)
     grad_logits = (
         gates * (grad_gate - jnp.sum(gates * grad_gate, axis=-1, keepdims=True))
     ).astype(bf_type)
-    grad_ffn = jnp.sum(grad_parts.astype(fl_type), axis=0) + outer_cols(grad_logits, full_router)
+    grad_ffn = grad_mixture + outer_cols(grad_logits, full_router)
     router_part = inner_rows(ffn_low, grad_logits)
     grad_resid_norm, ffn_gain_terms = norm_back(residual, ffn_factor, ffn_gain, grad_ffn)
     grad_residual = grad_out + grad_resid_norm
@@ -1872,9 +2690,9 @@
         grad_input, total_a, total_o, summed = tail(
             9, C, F, T, kv_heads,
             (
-                grad_own, heads_low, normed_low, q_rot, all_both, keys_t, raw, log_total, bias,
+                grad_own, heads_low, q_rot, all_both, keys_t, raw, log_total, bias,
                 cos_full, sin_signed, query_gain[None], key_gain[None], attn_gain[None],
-                own_inputs, grad_residual, router_rows, vec_in, full_o, full_all,
+                own_inputs, grad_residual, router_rows, vec_in, normed_low, full_o, full_all,
             ),
             width, q_cols // C,
         )
@@ -2011,8 +2829,8 @@
         sum_key,
         sum_ffn,
         grad_router,
-        grad_expert_in[None],
-        grad_expert_out[None],
+        grad_expert_in.astype(fl_type)[None],
+        grad_expert_out.astype(fl_type)[None],
     )
 
 

time: 763 us -> 669 us (0.88)
  matrix products: 71.7 us -> 4.76 us
  Pallas kernels: 633 us -> 597 us
  other arithmetic: 27.2 us -> 37.2 us
    dot_general x3 -> x1, matrix products: 24.3 us -> 1.39 us  [inner_rows(): lax.dot_general(left, right, (((0,), (0,)), ((), ())), preferred_element_...]
    dot_general x3 -> x0, matrix products: 22.5 us -> none  [the longest x1 15.2 us: local(): jnp.dot(expert_rows, w_expert_in[0], preferred_element_type=fl_type)]
    dot_general x3 -> x1, matrix products: 24.1 us -> 3.15 us  [outer_cols(): lax.dot_general(left, right, (((1,), (1,)), ((), ())), preferred_element_...]
    pallas_call x1, Pallas kernels: 177 us -> 159 us  [tail(): pl.pallas_call(functools.partial(tail_body, C, F, T, KH), out_shape=(jax....]
    pallas_call x4 -> x2, Pallas kernels: 328 us -> 313 us  [the longest x1 157 us: moe_backward(): pl.pallas_call(functools.partial(moe_backward_body, C, F, T), out_shape=(...]
    broadcast_in_dim x0 -> x2, other arithmetic: none -> 13 us  [the longest x1 9.49 us: local(): grad_expert_in.astype(fl_type)[None]]
where the time goes in v5:
time: 669 us; the launch traced here: 659 us
  Pallas kernels  597 us (89%)
  other arithmetic  37.2 us (6%)
  local copies, waits for them, and re-layouts  15.1 us (2%)
    pallas_call x1, Pallas kernels, tail(): pl.pallas_call(functools.partial(tail_body, C, F, T, KH), out_shape=(jax....  159 us
    pallas_call x1, Pallas kernels, moe_backward(): pl.pallas_call(functools.partial(moe_backward_body, C, F, T), out_shape=(...  157 us
    pallas_call x1, Pallas kernels, moe_forward(): pl.pallas_call(functools.partial(moe_forward_body, C, F, T), out_shape=(s...  156 us
    pallas_call x1, Pallas kernels, head(): pl.pallas_call(functools.partial(head_body, C, F, T, KH), out_shape=(shap...  125 us

profile of v5, /device:TPU:25, one launch (start us, length us, event | category | flops | bytes accessed | tf_op | source)
XLA Modules:
  0.0 658.6 jit_solution(10207968145871378232)
XLA Ops:
  0.7 1.4 dynamic-slice.16
  2.7 1.2 fusion.4.bias
  9.6 3.2 fusion.1.wa
  12.8 124.9 %shard_map.254 = (bf16[2048,2688]{1,0:T(8,128)(2,1)}, bf16[2048,2048]{1,0:T(8,128)(2,1)}, f32[3,4,32,128]{3,2,1,0:T(8,128)}, f32[256,2560]{1,0:T(8,128)}, bf16[2...) custom-call(bf16[256,2048]{1,0:T(8,128)(2,1)} %bitcast.51, ...), custom_call_target="tpu_custom_call" | custom-call | tf_op jit(solution)/shard_map/pallas_call | solution.py:1671
  137.7 0.9 copy.48
  139.3 156.0 %shard_map.255 = (bf16[4,2,4,48,2048]{4,3,2,1,0:T(8,128)(2,1)}, bf16[4,2,4,48,1024]{4,3,2,1,0:T(8,128)(2,1)}, bf16[4,2,4,48,1024]{4,3,2,1,0:T(8,128)(2,1)}, f32[...) custom-call(bf16[128,2048]{1,0:T(8,128)(2,1)} %get-tuple-element.68.rows, ...), custom_call_target="tpu_custom_call" | custom-call | tf_op jit(solution)/shard_map/pallas_call | solution.py:2060
  295.4 3.0 multiply_reduce_fusion
  300.8 157.2 %shard_map.256 = (f32[128,2048]{1,0:T(8,128)}, bf16[2048,1536]{1,0:T(8,128)(2,1)}, bf16[768,2048]{1,0:T(8,128)(2,1)}, f32[2,4,8,128]{3,2,1,0:T(8,128)}, f32[2,4,8,128]{3,2,1,0:T(8,128)}) custom-call(f32[3,4,32,128]{3,2,1,0:T(8,128)} %get-tuple-element.72.gates, f32[3,4,32,128]{3,2,1,0:T(8,128)} %get-tuple-element.70.ranks, ...), custom_call_target="tpu_custom_call" | custom-call | tf_op jit(solution)/shard_map/pallas_call | solution.py:2405
  459.8 3.2 multiply_reduce_fusion.1
  463.0 1.1 scatter.9.vec_in
  464.1 1.4 fusion.12
  465.5 1.2 reshape.150.router
  466.7 2.8 fusion.10
  469.6 1.1 dynamic-slice_convert_fusion.own_in
  470.6 159.2 %shard_map.257 = (f32[128,2048]{1,0:T(8,128)}, bf16[512,2560]{1,0:T(8,128)(2,1)}, bf16[2048,512]{1,0:T(8,128)(2,1)}, f32[16,2048]{1,0:T(8,128)}) custom-call(bf16[128,2048]{1,0:T(8,128)(2,1)} %get-tuple-element.153.grad_own, bf16[256,2048]{1,0:T(8,128)(2,1)} %get-tuple-element.82.heads, bf16[256,2048]{1,0:T(8,128)(2,1)} %get-tuple-element.83.qrot, ...), custom_call_target="tpu_custom_call" | custom-call | tf_op jit(solution)/shard_map/pallas_call | solution.py:1314
  629.9 4.3 convert_element_type.61
  634.2 2.6 slice_convert_fusion
  636.8 9.5 %bitcast_convert_fusion = f32[1,2048,1536]{2,1,0:T(8,128)} fusion(bf16[2048,1536]{1,0:T(8,128)(2,1)} %get-tuple-element.94), kind=kLoop, calls=%fused_computation | loop fusion | flops 3145728 | bytes 18874368 | tf_op jit(solution)/shard_map/broadcast_in_dim | solution.py:2832
  646.3 1.0 slice_convert_fusion.1
  648.2 1.5 fusion.11
  649.7 1.2 slice.80
  651.6 1.2 slice_bitcast_fusion.2
  652.8 3.5 bitcast_convert_fusion.1
  656.3 1.0 copy.57
  (57 shorter events, 10.7 us)
Async XLA Ops:
  0.6 9.0 %copy-start.7 = (bf16[512,2048]{1,0:T(8,128)(2,1)S(1)}, bf16[512,2048]{1,0:T(8,128)(2,1)}, u32[]{:S(2)}) copy-start(bf16[512,2048]{1,0:T(8,128)(2,1)} %param.24) | copy-start | bytes 6291460
  139.3 156.1 %copy-start.2 = (f32[128,2048]{1,0:T(8,128)S(1)}, f32[128,2048]{1,0:T(8,128)}, u32[]{:S(2)}) copy-start(f32[128,2048]{1,0:T(8,128)} %get-tuple-element.67) | copy-start | bytes 3145732
  139.3 156.1 %copy-start.9 = (bf16[1,128,2048]{2,1,0:T(8,128)(2,1)S(1)}, bf16[1,128,2048]{2,1,0:T(8,128)(2,1)}, u32[]{:S(2)}) copy-start(bf16[1,128,2048]{2,1,0:T(8,128)(2,1)} %param.20) | copy-start | bytes 1572868
  295.3 3.1 copy-start.13
  298.4 1.4 copy-start
  300.8 159.0 %copy-start.11 = (f32[2048]{0:T(1024)S(1)}, f32[2048]{0:T(1024)}, u32[]{:S(2)}) copy-start(f32[2048]{0:T(1024)} %param.30) | copy-start | bytes 24580
  458.0 8.7 %copy-start.1 = (f32[128,2048]{1,0:T(8,128)S(1)}, f32[128,2048]{1,0:T(8,128)}, u32[]{:S(2)}) copy-start(f32[128,2048]{1,0:T(8,128)} %copy-done) | copy-start | bytes 3145732
  458.0 8.7 %copy-start.3 = (f32[128,2048]{1,0:T(8,128)S(1)}, f32[128,2048]{1,0:T(8,128)}, u32[]{:S(2)}) copy-start(f32[128,2048]{1,0:T(8,128)} %get-tuple-element.67) | copy-start | bytes 3145732
  464.1 6.5 copy-start.10
  466.7 2.8 copy-start.6
  629.9 4.4 copy-start.5
  636.8 10.5 %copy-start.12 = (f32[16,2048]{1,0:T(8,128)S(1)}, f32[16,2048]{1,0:T(8,128)}, u32[]{:S(2)}) copy-start(f32[16,2048]{1,0:T(8,128)} %get-tuple-element.90) | copy-start | bytes 393220
  636.8 16.0 %copy-start.4 = (bf16[768,2048]{1,0:T(8,128)(2,1)S(1)}, bf16[768,2048]{1,0:T(8,128)(2,1)}, u32[]{:S(2)}) copy-start(bf16[768,2048]{1,0:T(8,128)(2,1)} %get-tuple-element.95) | copy-start | bytes 9437188
  652.8 3.6 copy-start.8

commit v6 on v5

--- a/solution.py
+++ b/solution.py
@@ -833,7 +833,7 @@
 def tail_body(
     C, F, T, KH,
     grad_own, heads, qrot, kv, keys_t, raw, lse, bias, cosf, sins, qgain, kgain, again,
-    own_in, resid_in, router, vec_in, normed, fo, fall,
+    hidden, resid_in, router, vec_in, normed, fo, fall,
     gin, outa, outo, small,
     wbuf, dall, nall, hq, rq, dheads, draw, dk, dv, ksend, kgot, gains, nsend, ngot, nown,
     sza, szo, rza, rzo, smx, zgot, sums, sgot,
@@ -926,9 +926,6 @@
     def outo_of(p):
         return outo.at[lane(p, po)]
 
-    def outa_of(p):
-        return outa.at[:, lane(p, pa)]
-
     def dall_of(q):
         def view(p, half):
             at = lane(blocks[q], cols_o)
@@ -996,28 +993,46 @@
             hq[...].reshape(C * R, po), dall[:, :, lane(b, cols_o)].reshape(C * R, cols_o)
         )
 
-    def piece_a(b):
+    cut = pa // 256 * 128
+    cuts = (slice(0, cut), slice(cut, pa))
+
+    def piece_a(b, cols):
         return inner_rows(
-            nall[:, :, lane(b, rows_a)].reshape(C * R, rows_a), rq[...].reshape(C * R, pa)
-        )
-
-    pieces = ((piece_o, szo, rzo, outo_of), (piece_a, sza, rza, outa_of))
+            nall[:, :, lane(b, rows_a)].reshape(C * R, rows_a),
+            rq[:, :, cols].reshape(C * R, cols.stop - cols.start),
+        )
+
+    def part_of(buf, cols):
+        return lambda b: buf.at[b, :, cols]
+
+    def outa_part(p, cols):
+        start = pl.multiple_of(p * pa + cols.start, 128)
+        return outa.at[:, pl.ds(start, cols.stop - cols.start)]
+
+    pieces = [(piece_o, lambda b: szo.at[b], lambda b: rzo.at[b], outo_of)]
+    for cols in cuts:
+        pieces.append(
+            (
+                functools.partial(piece_a, cols=cols), part_of(sza, cols), part_of(rza, cols),
+                functools.partial(outa_part, cols=cols),
+            )
+        )
     end = (f == 0) | (f == F - 1)
 
     def z_out(n, q):
         b = blocks[q]
         _, send, got, _ = pieces[n]
-        return remote(send.at[b], got.at[b], z_s.at[n, q], z_r.at[n, b], (c, f + 1, t))
+        return remote(send(b), got(b), z_s.at[n, q], z_r.at[n, b], (c, f + 1, t))
 
     def z_down(n, q):
         b = blocks[q]
         slot = jnp.where(b == f - 1, F, b)
         _, send, got, _ = pieces[n]
-        return remote(send.at[b], got.at[slot], z_s.at[n, q], z_r.at[n, slot], (c, f - 1, t))
+        return remote(send(b), got(slot), z_s.at[n, q], z_r.at[n, slot], (c, f - 1, t))
 
     def z_wait(n, slot):
         _, send, got, _ = pieces[n]
-        remote(send.at[0], got.at[slot], z_s.at[n, 0], z_r.at[n, slot], (c, f, t)).wait_recv()
+        remote(send(0), got(slot), z_s.at[n, 0], z_r.at[n, slot], (c, f, t)).wait_recv()
 
     def z_send(n, q):
         up = blocks[q] > f
@@ -1035,7 +1050,7 @@
 
         @pl.when(end)
         def _():
-            send[blocks[q]] = fn(blocks[q]).astype(BF)
+            send(blocks[q])[...] = fn(blocks[q]).astype(BF)
             z_send(n, q)
 
     def o_first(q):
@@ -1050,26 +1065,26 @@
         def _():
             b = blocks[q]
             z_wait(n, b)
-            send[b] = (fn(b) + got[b].astype(FL)).astype(BF)
+            send(b)[...] = (fn(b) + got(b)[...].astype(FL)).astype(BF)
             z_send(n, q)
 
     def z_last(n):
         fn, send, got, out = pieces[n]
-        send[f] = fn(f).astype(BF)
+        send(f)[...] = fn(f).astype(BF)
 
         @pl.when(f > 0)
         def _():
             z_wait(n, f)
-            send[f] = (send[f].astype(FL) + got[f].astype(FL)).astype(BF)
+            send(f)[...] = (send(f)[...].astype(FL) + got(f)[...].astype(FL)).astype(BF)
 
         @pl.when(f < F - 1)
         def _():
             z_wait(n, F)
-            out(c)[...] = (send[f].astype(FL) + got[F].astype(FL)).astype(BF)
+            out(c)[...] = (send(f)[...].astype(FL) + got(F)[...].astype(FL)).astype(BF)
 
         @pl.when(f == F - 1)
         def _():
-            out(c)[...] = send[f]
+            out(c)[...] = send(f)[...]
 
 
     key_step = min(L, 512)
@@ -1211,23 +1226,27 @@
         raw_come(lax.rem(c + k, C)).wait_recv()
     for q in range(F - 1):
         z_first(1, q)
+    for q in range(F - 1):
+        z_first(2, q)
     z_relay(1, 0)
     z_last(0)
     spread_start(outo_of, 0)
 
     swap_n.wait_recv()
     upstream = nown[...] + ngot[...].astype(FL)
-    values = own_in[...]
+    values = hidden[at_t, :].astype(FL)
     factor = lax.rsqrt(jnp.mean(values * values, axis=-1, keepdims=True) + EPS)
     back, terms = norm_back(values, factor, again[...], upstream)
     gin[...] = resid_in[...] + back
+    E, wide = router.shape[0], W // F
+    gain_sum = jnp.sum(terms, axis=0, keepdims=True)
     for b in range(F):
-        smx[b, 0 : router.shape[1]] = router[b]
-        at = router.shape[1]
-        smx[b, at : at + 8] = vec_in[...]
-        smx[b, at : at + 1] = jnp.sum(terms, axis=0, keepdims=True)
-        smx[b, at + 2 : at + 3, 0:HS] = gains[0:1, :]
-        smx[b, at + 2 : at + 3, HS : 2 * HS] = gains[1:2, :]
+        smx[b, 0:E] = router[:, b * wide : (b + 1) * wide]
+        smx[b, E : E + 16] = vec_in[...]
+        for i in range(F):
+            smx[b, E + i : E + i + 1] = gain_sum[:, i * wide : (i + 1) * wide]
+        smx[b, E + 8 : E + 9, 0:HS] = gains[0:1, :]
+        smx[b, E + 8 : E + 9, HS : 2 * HS] = gains[1:2, :]
 
     def t_copy(k):
         return remote(smx.at[lax.rem(f + k, F)], zgot.at[f], ts.at[k], tr.at[k], columns[k - 1])
@@ -1241,6 +1260,8 @@
     zgot[f] = smx[f]
     for q in range(1, F - 1):
         z_relay(1, q)
+    for q in range(F - 1):
+        z_relay(2, q)
     spread_pass(outo_of, 0)
     for k in range(1, F):
         t_arrival(k).wait_recv()
@@ -1255,7 +1276,7 @@
 
     u_copy(0).start()
     z_last(1)
-    spread_start(outa_of, 1)
+    spread_start(pieces[1][3], 1)
     for i in range(3):
         u_copy(i).wait_recv()
         total = sums[i] + sgot[i]
@@ -1265,11 +1286,15 @@
         else:
             small[...] = total
     spread_end(outo_of, 0)
-    spread_pass(outa_of, 1)
-    spread_end(outa_of, 1)
-
-    for view, n in ((outo_of, 0), (outa_of, 1)):
-        spread_sent(view, n)
+    z_last(2)
+    spread_start(pieces[2][3], 2)
+    for n in (1, 2):
+        spread_pass(pieces[n][3], n)
+    for n in (1, 2):
+        spread_end(pieces[n][3], n)
+
+    for n in range(3):
+        spread_sent(pieces[n][3], n)
     for q in range(F):
         d_moves[q][2]()
     n_drain()
@@ -1286,7 +1311,7 @@
     for g in range(KH):
         for copy in kv_moves[g][0]:
             copy.wait_send()
-    for n in range(2):
+    for n in range(3):
         for q in range(F - 1):
             z_out(n, q).wait_send()
     for k in range(1, F):
@@ -1308,7 +1333,7 @@
     S = C * T
     pa = PC // C
     rows_a, cols_o = W // F, W // F
-    small_shape = (router.shape[1] + 8, W)
+    small_shape = (router.shape[0] + 16, W // F)
     dma = pltpu.SemaphoreType.DMA
     V = pltpu.VMEM
     return pl.pallas_call(
@@ -1330,10 +1355,10 @@
             V((F + 1, rows_a, pa), BF), V((F + 1, po, cols_o), BF),
             V((F,) + small_shape, FL), V((F,) + small_shape, FL), V((3,) + small_shape, FL),
             V((3,) + small_shape, FL),
-            dma((4,)), dma((2,)), dma((2,)), dma((2, 3)), dma((2, 3)), dma((C,)), dma((C,)), dma((5,)), dma((5,)),
+            dma((4,)), dma((2,)), dma((2,)), dma((3, 3)), dma((3, 3)), dma((C,)), dma((C,)), dma((5,)), dma((5,)),
             dma((F, 5)), dma((F, 5)),
             dma((KH, C)), dma((KH, C)), dma((C,)), dma((C,)),
-            dma((2, F)), dma((2, F + 1)), dma((F,)), dma((F,)), dma((3,)), dma((3,)),
+            dma((3, F)), dma((3, F + 1)), dma((F,)), dma((F,)), dma((3,)), dma((3,)),
         ],
         compiler_params=params(identity, 62),
     )(*args)
@@ -1985,13 +2010,19 @@
                 if not near:
                     cross_copy(k, g).start()
 
-    def part_copy(k):
+    def part_copy(k, g):
         b = x.blocks[k]
-        return remote(pstage.at[b], zpart.at[f], ps.at[b], pr.at[f], (c, b, t))
-
-    def part_arrival(k):
+        at = pl.ds(g * H, H)
+        return remote(
+            pstage.at[b, :, at], zpart.at[f, :, at], ps.at[g, b], pr.at[g, f], (c, b, t)
+        )
+
+    def part_arrival(k, g):
         b = x.blocks[k]
-        return remote(pstage.at[b], zpart.at[b], ps.at[b], pr.at[b], (c, b, t))
+        at = pl.ds(g * H, H)
+        return remote(
+            pstage.at[b, :, at], zpart.at[b, :, at], ps.at[g, b], pr.at[g, b], (c, b, t)
+        )
 
     def finish(k):
         b = x.blocks[k]
@@ -2002,10 +2033,9 @@
             total = own_part[k % 2, :, at] + cross[g, b].astype(FL)
             if k:
                 pstage[b, :, at] = total.astype(BF)
+                part_copy(k, g).start()
             else:
                 part[:, at] = total
-        if k:
-            part_copy(k).start()
 
     dispatch_rows(0)
     x.z_relay(zbuf, zs, zr, 1)
@@ -2030,19 +2060,20 @@
     expert(3)
     finish(1)
     gather(2)
+    finish(2)
     gather(3)
-    finish(2)
     finish(3)
     for k in range(1, F):
-        part_arrival(k).wait_recv()
+        for g in range(2):
+            part_arrival(k, g).wait_recv()
         part[...] += zpart[x.blocks[k]].astype(FL)
     x.z_drain(zbuf, zs, zr)
     keep_pre(F - 1).wait()
     for k in range(F):
         keep_x(k).wait()
-        if k:
-            part_copy(k).wait_send()
         for g in range(2):
+            if k:
+                part_copy(k, g).wait_send()
             keep_got(k, g).wait()
             dense_copy(k, g).wait_send()
             for j in range(1, 4):
@@ -2072,8 +2103,8 @@
             V((W, H2), BF), V((FFW, W), BF), V((S * K, H2), FL), V((2, R, W), FL),
             V((2, F, R, H), BF), V((F, R, W), BF), V((F, R, W), BF),
             dma((2,)), dma((2, F)), dma((2, F)), dma((2, F)), dma((2, F)), dma((2, F, 4)),
-            dma((2, F, 4)), dma((2, F, 4)), dma((2, F, 4)), dma((2, F)), dma((2, F)), dma((F,)),
-            dma((F,)), dma((3, F)), dma((3, F)), dma((F,)), dma((2, F)), dma((F,)),
+            dma((2, F, 4)), dma((2, F, 4)), dma((2, F, 4)), dma((2, F)), dma((2, F)), dma((2, F)),
+            dma((2, F)), dma((3, F)), dma((3, F)), dma((F,)), dma((2, F)), dma((F,)),
         ],
         compiler_params=params(identity, 61),
     )(rows, gate_t, ranks, w_in, w_out)
@@ -2287,13 +2318,19 @@
                 if not near:
                     cross_copy(k, g).start()
 
-    def part_copy(k):
+    def part_copy(k, g):
         b = x.blocks[k]
-        return remote(pstage.at[b], zpart.at[f], ps.at[b], pr.at[f], (c, b, t))
-
-    def part_arrival(k):
+        at = pl.ds(g * H, H)
+        return remote(
+            pstage.at[b, :, at], zpart.at[f, :, at], ps.at[g, b], pr.at[g, f], (c, b, t)
+        )
+
+    def part_arrival(k, g):
         b = x.blocks[k]
-        return remote(pstage.at[b], zpart.at[b], ps.at[b], pr.at[b], (c, b, t))
+        at = pl.ds(g * H, H)
+        return remote(
+            pstage.at[b, :, at], zpart.at[b, :, at], ps.at[g, b], pr.at[g, b], (c, b, t)
+        )
 
     def finish(k):
         b = x.blocks[k]
@@ -2304,10 +2341,9 @@
             total = own_part[:, at] + cross[g, b].astype(FL)
             if k:
                 pstage[b, :, at] = total.astype(BF)
+                part_copy(k, g).start()
             else:
                 part[:, at] = total
-        if k:
-            part_copy(k).start()
 
     made = []
 
@@ -2365,15 +2401,17 @@
     expert(3)
     finish(1)
     gather(2)
-    out_grads(0, FFW // 256)
+    out_grads(0, 1)
     finish(2)
+    out_grads(1, FFW // 256)
     gather(3)
     load_x.wait()
     in_grads(0, 1)
     finish(3)
     in_grads(1, W // 256)
     for k in range(1, F):
-        part_arrival(k).wait_recv()
+        for g in range(2):
+            part_arrival(k, g).wait_recv()
         part[...] += zpart[x.blocks[k]].astype(FL)
     for k in range(F):
         for g in range(2):
@@ -2385,9 +2423,9 @@
         copy.wait()
     x.z_drain(zbuf, zs, zr)
     for k in range(F):
-        if k:
-            part_copy(k).wait_send()
         for g in range(2):
+            if k:
+                part_copy(k, g).wait_send()
             dense_copy(k, g).wait_send()
             for j in range(1, 4):
                 back(k, g, j, False).wait_send()
@@ -2417,8 +2455,8 @@
             V((S * K, H2), FL), V((2, 256, max(W, H2) // 2), BF), V((R, W), FL),
             V((2, F, R, H), BF), V((F, R, W), BF), V((F, R, W), BF), V((2, 2, F, 8, R), FL),
             dma((6,)), dma((2, F)), dma((2, F)), dma((2, F)), dma((2, F)), dma((2, F, 4)),
-            dma((2, F, 4)), dma((2, F, 4)), dma((2, F, 4)), dma((2, F)), dma((2, F)), dma((F,)),
-            dma((F,)), dma((2, 2, F)), dma((2, 2, F)), dma((F,)),
+            dma((2, F, 4)), dma((2, F, 4)), dma((2, F, 4)), dma((2, F)), dma((2, F)), dma((2, F)),
+            dma((2, F)), dma((2, 2, F)), dma((2, 2, F)), dma((F,)),
             dma((2 * (FFW // 256 + W // 256),)),
         ],
         compiler_params=params(identity, 63.5),
@@ -2683,16 +2721,17 @@
     grad_residual = grad_out + grad_resid_norm
     grad_own = grad_residual.astype(bf_type)
     if fused:
-        vec_in = jnp.zeros((8, width), fl_type)
-        vec_in = vec_in.at[1].set(jnp.sum(ffn_gain_terms, axis=0))
-        vec_in = vec_in.at[2, 2 * head_size].set(loss_part)
-        router_rows = router_part.reshape(F, -1, width)
+        wide = width // F
+        vec_in = jnp.zeros((16, wide), fl_type)
+        vec_in = vec_in.at[F : 2 * F].set(jnp.sum(ffn_gain_terms, axis=0).reshape(F, wide))
+        vec_in = vec_in.at[8, 2 * head_size].set(loss_part)
+        router_rows = inner_rows(grad_logits, ffn_low)
         grad_input, total_a, total_o, summed = tail(
             9, C, F, T, kv_heads,
             (
                 grad_own, heads_low, q_rot, all_both, keys_t, raw, log_total, bias,
                 cos_full, sin_signed, query_gain[None], key_gain[None], attn_gain[None],
-                own_inputs, grad_residual, router_rows, vec_in, normed_low, full_o, full_all,
+                hidden_in[0], grad_residual, router_rows, vec_in, normed_low, full_o, full_all,
             ),
             width, q_cols // C,
         )
@@ -2700,12 +2739,13 @@
         grad_key = total_a[:, q_cols : q_cols + kv_cols].astype(fl_type)
         grad_value = total_a[:, q_cols + kv_cols :].astype(fl_type)
         grad_output_w = total_o.astype(fl_type)
-        router_len = router_rows.shape[1]
-        grad_router = summed[:router_len].reshape(w_router.shape)
-        sum_attn, sum_ffn = summed[router_len], summed[router_len + 1]
-        sum_query = summed[router_len + 2, :head_size]
-        sum_key = summed[router_len + 2, head_size : 2 * head_size]
-        loss_total = summed[router_len + 2, 2 * head_size]
+        router_len = router_rows.shape[0]
+        grad_router = summed[:router_len].T
+        sum_attn = summed[router_len : router_len + F].reshape(width)
+        sum_ffn = summed[router_len + F : router_len + 2 * F].reshape(width)
+        sum_query = summed[router_len + 8, :head_size]
+        sum_key = summed[router_len + 8, head_size : 2 * head_size]
+        loss_total = summed[router_len + 8, 2 * head_size]
     else:
         grad_other = lax.ppermute(grad_own, "tp", swap)
         grad_attn = jnp.where(

time: 669 us -> 660 us (0.987)
  no operation moved by 1% of the time
where the time goes in v6:
time: 660 us; the launch traced here: 648 us
  Pallas kernels  593 us (90%)
  other arithmetic  34.8 us (5%)
  local copies, waits for them, and re-layouts  11.6 us (2%)
    pallas_call x1, Pallas kernels, moe_backward(): pl.pallas_call(functools.partial(moe_backward_body, C, F, T), out_shape=(...  157 us
    pallas_call x1, Pallas kernels, moe_forward(): pl.pallas_call(functools.partial(moe_forward_body, C, F, T), out_shape=(s...  156 us
    pallas_call x1, Pallas kernels, tail(): pl.pallas_call(functools.partial(tail_body, C, F, T, KH), out_shape=(jax....  155 us
    pallas_call x1, Pallas kernels, head(): pl.pallas_call(functools.partial(head_body, C, F, T, KH), out_shape=(shap...  125 us

profile of v6, /device:TPU:25, one launch (start us, length us, event | category | flops | bytes accessed | tf_op | source)
XLA Modules:
  0.0 648.4 jit_solution(1541947876334298352)
XLA Ops:
  0.7 1.4 dynamic-slice.15
  2.7 1.2 fusion.4.bias
  4.5 0.8 pad_maximum_fusion.1.sins
  6.0 0.8 copy.40
  8.7 0.9 copy.42
  9.6 3.2 fusion.1.wa
  12.8 124.9 %shard_map.254 = (bf16[2048,2688]{1,0:T(8,128)(2,1)}, bf16[2048,2048]{1,0:T(8,128)(2,1)}, f32[3,4,32,128]{3,2,1,0:T(8,128)}, f32[256,2560]{1,0:T(8,128)}, bf16[2...) custom-call(bf16[256,2048]{1,0:T(8,128)(2,1)} %bitcast.56, ...), custom_call_target="tpu_custom_call" | custom-call | tf_op jit(solution)/shard_map/pallas_call | solution.py:1696
  137.7 0.9 copy.44
  139.3 156.1 %shard_map.255 = (bf16[4,2,4,48,2048]{4,3,2,1,0:T(8,128)(2,1)}, bf16[4,2,4,48,1024]{4,3,2,1,0:T(8,128)(2,1)}, bf16[4,2,4,48,1024]{4,3,2,1,0:T(8,128)(2,1)}, f32[...) custom-call(bf16[128,2048]{1,0:T(8,128)(2,1)} %get-tuple-element.68.rows, ...), custom_call_target="tpu_custom_call" | custom-call | tf_op jit(solution)/shard_map/pallas_call | solution.py:2091
  295.5 3.0 multiply_reduce_fusion
  299.9 0.9 multiply_convert_fusion.rows
  300.8 157.3 %shard_map.256 = (f32[128,2048]{1,0:T(8,128)}, bf16[2048,1536]{1,0:T(8,128)(2,1)}, bf16[768,2048]{1,0:T(8,128)(2,1)}, f32[2,4,8,128]{3,2,1,0:T(8,128)}, f32[2,4,8,128]{3,2,1,0:T(8,128)}) custom-call(f32[3,4,32,128]{3,2,1,0:T(8,128)} %get-tuple-element.72.gates, f32[3,4,32,128]{3,2,1,0:T(8,128)} %get-tuple-element.70.ranks, ...), custom_call_target="tpu_custom_call" | custom-call | tf_op jit(solution)/shard_map/pallas_call | solution.py:2443
  458.1 0.9 slice.80
  459.0 0.8 bitcast_add_fusion
  459.9 2.3 multiply_reduce_fusion.1
  462.9 2.0 fusion.11.router
  464.9 1.5 fusion.10
  466.4 155.2 %shard_map.257 = (f32[128,2048]{1,0:T(8,128)}, bf16[512,2560]{1,0:T(8,128)(2,1)}, bf16[2048,512]{1,0:T(8,128)(2,1)}, f32[48,512]{1,0:T(8,128)}) custom-call(bf16[128,2048]{1,0:T(8,128)(2,1)} %get-tuple-element.111.grad_own, bf16[256,2048]{1,0:T(8,128)(2,1)} %get-tuple-element.82.heads, bf16[256,2048]{1,0:T(8,128)(2,1)} %get-tuple-element.83.qrot, ...), custom_call_target="tpu_custom_call" | custom-call | tf_op jit(solution)/shard_map/pallas_call | solution.py:1339
  621.6 4.3 convert_element_type.57
  626.0 2.6 slice_convert_fusion
  628.5 9.5 %bitcast_convert_fusion = f32[1,2048,1536]{2,1,0:T(8,128)} fusion(bf16[2048,1536]{1,0:T(8,128)(2,1)} %get-tuple-element.94), kind=kLoop, calls=%fused_computation | loop fusion | flops 3145728 | bytes 18874368 | tf_op jit(solution)/shard_map/broadcast_in_dim | solution.py:2872
  638.0 1.0 slice_convert_fusion.1
  642.6 3.5 bitcast_convert_fusion.1
  646.1 1.0 copy.52
  (54 shorter events, 8.4 us)
Async XLA Ops:
  0.6 9.0 %copy-start.6 = (bf16[512,2048]{1,0:T(8,128)(2,1)S(1)}, bf16[512,2048]{1,0:T(8,128)(2,1)}, u32[]{:S(2)}) copy-start(bf16[512,2048]{1,0:T(8,128)(2,1)} %param.24) | copy-start | bytes 6291460
  139.3 156.2 %copy-start.2 = (f32[128,2048]{1,0:T(8,128)S(1)}, f32[128,2048]{1,0:T(8,128)}, u32[]{:S(2)}) copy-start(f32[128,2048]{1,0:T(8,128)} %get-tuple-element.67) | copy-start | bytes 3145732
  139.3 156.2 %copy-start.8 = (bf16[1,128,2048]{2,1,0:T(8,128)(2,1)S(1)}, bf16[1,128,2048]{2,1,0:T(8,128)(2,1)}, u32[]{:S(2)}) copy-start(bf16[1,128,2048]{2,1,0:T(8,128)(2,1)} %param.20) | copy-start | bytes 1572868
  295.4 3.1 copy-start.12
  298.5 1.4 copy-start
  300.8 159.0 %copy-start.10 = (f32[2048]{0:T(1024)S(1)}, f32[2048]{0:T(1024)}, u32[]{:S(2)}) copy-start(f32[2048]{0:T(1024)} %param.30) | copy-start | bytes 24580
  458.1 6.8 %copy-start.1 = (f32[128,2048]{1,0:T(8,128)S(1)}, f32[128,2048]{1,0:T(8,128)}, u32[]{:S(2)}) copy-start(f32[128,2048]{1,0:T(8,128)} %copy-done) | copy-start | bytes 3145732
  458.1 6.8 %copy-start.3 = (f32[128,2048]{1,0:T(8,128)S(1)}, f32[128,2048]{1,0:T(8,128)}, u32[]{:S(2)}) copy-start(f32[128,2048]{1,0:T(8,128)} %get-tuple-element.67) | copy-start | bytes 3145732
  462.9 3.5 copy-start.9
  621.6 4.4 copy-start.5
  628.5 10.5 %copy-start.11 = (f32[48,512]{1,0:T(8,128)S(1)}, f32[48,512]{1,0:T(8,128)}, u32[]{:S(2)}) copy-start(f32[48,512]{1,0:T(8,128)} %get-tuple-element.90) | copy-start | bytes 294916
  628.5 14.1 %copy-start.4 = (bf16[768,2048]{1,0:T(8,128)(2,1)S(1)}, bf16[768,2048]{1,0:T(8,128)(2,1)}, u32[]{:S(2)}) copy-start(bf16[768,2048]{1,0:T(8,128)(2,1)} %get-tuple-element.95) | copy-start | bytes 9437188
  642.6 3.6 copy-start.7
